TPU v7x, 32 devices: a whole 2x2x4 slice. The times are simulated.
32 devices in a mesh: groups: 2 (over y), dp: 4 (over z), replica: 2 (over x), mp: 2 (over core).
Axes of the slice: x: 2, y: 2, z: 4, core: 2. Of those that a mesh axis runs over, the one named last changes fastest.
Arguments:
- hot_slab: bfloat16 [16, 64, 128], P(None, 'mp'), may hold values from -1.5 to 1.5
- linear_state: float32 [16, 64, 128], P('dp', 'mp'), may hold values from -6 to 6
- square_state: float32 [16, 64, 128], P('dp', 'mp'), may hold values from 0.05 to 5
- serve_table: bfloat16 [2, 16, 64, 128], P('replica', 'dp', 'mp'), may hold values from -1.5 to 1.5
- first_weight: bfloat16 [16, 64, 512], P(None, 'mp'), may hold values from -0.1875 to 0.1875
- second_weight: bfloat16 [512, 256], replicated, may hold values from -0.25 to 0.25
- out_weight: bfloat16 [256], replicated, may hold values from -1.5 to 1.5
- step_blocks: int32 [4, 4], P('groups'), parts along dimension 0, may hold values from 0 to 15, as said below
- feature_ids: int32 [2, 4096, 16, 4], P(None, ('groups', 'dp', 'replica')), parts along dimension 1, may hold values from 0 to 511
- click_labels: float32 [2, 4096], P(None, ('groups', 'dp', 'replica')), parts along dimension 1, may hold values from 0 to 1
- serve_layout: int32 [2, 4], P('replica'), may hold values from 0 to 3, each once within a row
- request_ids: int32 [2, 64, 16, 4], P('replica', ('groups', 'dp')), parts along dimension 1, may hold values from 0 to 2047
Outputs:
- new_linear: float32 [32, 64, 128], P(('groups', 'dp'), 'mp'), parts along dimension 0
- new_square: float32 [32, 64, 128], P(('groups', 'dp'), 'mp'), parts along dimension 0
- new_serve: bfloat16 [4, 16, 64, 128], P(('groups', 'replica'), 'dp', 'mp'), parts along dimension 0
- request_scores: float32 [2, 64], P('replica', ('groups', 'dp')), parts along dimension 1
There are 2 independent parts, one for each index of `groups`. A program takes and returns all parts, laid end to end along the dimension named above; an argument that names none is the same for every part. Nothing has to cross between parts.
Inputs may be any that keep to these rules, and one draw needn't show every extreme that they name: `step_blocks`: the blocks of one step are distinct; the last 2 blocks of step t are the first 2 of step t + 1. `serve_layout`: each row names every owner once.
All inputs are finite; a program needn't handle non-finite values.
Results may differ from a plain program's by a relative error of at most 0.011.
Values may be sent and summed in bfloat16 or wider, within the bound.
No kernel may reach another device: no remote copies, remote signals or barrier semaphores. Data moves between devices by JAX's collectives and lax.ppermute only.
A program may use at most 64 MiB of HBM per device.

v0:
```python
import jax
import jax.numpy as jnp
from jax import lax
from jax.sharding import PartitionSpec as P

step_alpha = 0.5
step_beta = 1.0
sparse_penalty = 0.1
ridge_penalty = 0.05
slot_group = 4


def silu_slope(inputs):
    logistic = jax.nn.sigmoid(inputs)
    return logistic * (1.0 + inputs * (1.0 - logistic))


def ftrl_update(linear, square, gradient, current):
    grown = square + gradient * gradient
    sigma_term = (jnp.sqrt(grown) - jnp.sqrt(square)) / step_alpha
    linear_next = linear + gradient - sigma_term * current
    shrunk = linear_next - jnp.clip(linear_next, -sparse_penalty, sparse_penalty)
    weights = -shrunk / ((step_beta + jnp.sqrt(grown)) / step_alpha + ridge_penalty)
    return (linear_next, grown, weights)


def slot_counts(group_ids, offset, active_count, block_rows):
    table_width = active_count * block_rows
    columns = jnp.arange(table_width, dtype=jnp.int32) + offset
    counts = jnp.zeros(group_ids.shape[:2] + (table_width,), jnp.bfloat16)
    for pick_index in range(group_ids.shape[2]):
        counts = counts + (group_ids[:, :, pick_index, None] == columns).astype(jnp.bfloat16)
    return counts.reshape(group_ids.shape[:2] + (active_count, block_rows))


def pool_slots(step_ids, active):
    pieces = []
    for group_start in range(0, step_ids.shape[1], slot_group):
        counts = slot_counts(
            step_ids[:, group_start : group_start + slot_group], 0, active.shape[0], active.shape[2]
        )
        pieces.append(
            jnp.einsum("bgar,acr->bgc", counts, active, preferred_element_type=jnp.float32)
        )
    return jnp.concatenate(pieces, axis=1)


def spread_slots(step_ids, grad_input, active_count, block_rows):
    summed = jnp.zeros((active_count, grad_input.shape[2], block_rows), jnp.float32)
    for group_start in range(0, step_ids.shape[1], slot_group):
        counts = slot_counts(
            step_ids[:, group_start : group_start + slot_group], 0, active_count, block_rows
        )
        summed = summed + jnp.einsum(
            "bgar,bgc->acr",
            counts,
            grad_input[:, group_start : group_start + slot_group],
            preferred_element_type=jnp.float32,
        )
    return summed


def layer_one(inputs, first_flat):
    partial_sum = jnp.dot(inputs, first_flat, preferred_element_type=jnp.float32)
    return lax.psum(partial_sum, "mp")


def layer_rest(hidden_pre, second_weight, out_weight):
    hidden_one = jax.nn.silu(hidden_pre).astype(jnp.bfloat16)
    second_pre = jnp.dot(hidden_one, second_weight, preferred_element_type=jnp.float32)
    hidden_two = jax.nn.silu(second_pre).astype(jnp.bfloat16)
    return (second_pre, jnp.dot(hidden_two, out_weight, preferred_element_type=jnp.float32))


def local(
    hot_slab,
    linear_state,
    square_state,
    serve_table,
    first_weight,
    second_weight,
    out_weight,
    step_blocks,
    feature_ids,
    click_labels,
    serve_layout,
    request_ids,
):
    owners = lax.axis_size("dp")
    owner_index = lax.axis_index("dp")
    owned_count, half_width, block_rows = linear_state.shape
    active_count = step_blocks.shape[1]
    samples = feature_ids.shape[1]
    steps_count = step_blocks.shape[0]
    exact = lax.Precision.HIGHEST
    first_flat = first_weight.reshape(-1, first_weight.shape[2])
    block_range = jnp.arange(owned_count, dtype=jnp.int32)
    own_blocks = owner_index * owned_count + block_range
    current_slab = hot_slab
    linear = linear_state
    square = square_state
    own_weights = jnp.take(hot_slab, own_blocks, axis=0)
    for step_index in range(steps_count):
        chosen = step_blocks[step_index]
        matches = (own_blocks[:, None] == chosen[None, :]).astype(jnp.float32)
        owned_active = jnp.sum(matches, axis=1)[:, None, None] > 0.5
        active = jnp.take(current_slab, chosen, axis=0)
        step_ids = feature_ids[step_index]
        pooled = pool_slots(step_ids, active).astype(jnp.bfloat16)
        hidden_pre = layer_one(pooled.reshape(samples, -1), first_flat)
        step_labels = click_labels[step_index]
        second_pre, logits = layer_rest(hidden_pre, second_weight, out_weight)
        logit_error = jax.nn.sigmoid(logits) - step_labels
        grad_two = (
            logit_error[:, None] * out_weight.astype(jnp.float32)[None, :] * silu_slope(second_pre)
        ).astype(jnp.bfloat16)
        back_one = jnp.dot(grad_two, second_weight.T, preferred_element_type=jnp.float32)
        grad_one = (back_one * silu_slope(hidden_pre)).astype(jnp.bfloat16)
        grad_input = jnp.dot(grad_one, first_flat.T, preferred_element_type=jnp.float32).astype(
            jnp.bfloat16
        )
        grad_input = grad_input.reshape(samples, -1, half_width)
        local_grad = spread_slots(step_ids, grad_input, active_count, block_rows)
        total_grad = lax.psum(local_grad, ("dp", "replica"))
        own_grad = jnp.einsum("ja,acr->jcr", matches, total_grad, precision=exact)
        linear_next, square_next, weights = ftrl_update(
            linear, square, own_grad, own_weights.astype(jnp.float32)
        )
        linear = jnp.where(owned_active, linear_next, linear)
        square = jnp.where(owned_active, square_next, square)
        own_weights = jnp.where(owned_active, weights.astype(jnp.bfloat16), own_weights)
        if step_index + 1 < steps_count:
            offered = jnp.einsum(
                "ja,jcr->acr", matches, own_weights.astype(jnp.float32), precision=exact
            )
            refreshed = lax.psum(offered.astype(jnp.bfloat16), "dp")
            current_slab = current_slab.at[chosen].set(refreshed)
    layout = serve_layout[0]
    owner_range = jnp.arange(owners, dtype=jnp.int32)
    inverse = jnp.sum(
        jnp.where(layout[:, None] == owner_range[None, :], owner_range[:, None], 0), axis=0
    )
    every_block = step_blocks.reshape(-1)
    slot_source = (inverse[owner_index] - block_range) % owners
    slot_block = slot_source * owned_count + block_range
    slot_touched = jnp.any(slot_block[:, None] == every_block[None, :], axis=1)[:, None, None]
    own_touched = jnp.any(own_blocks[:, None] == every_block[None, :], axis=1)
    dest_slot = (inverse - owner_index) % owners
    routing = ((dest_slot[:, None] == block_range[None, :]) & own_touched[None, :]).astype(
        jnp.float32
    )
    outgoing = jnp.einsum(
        "ej,jcr->ecr", routing, own_weights.astype(jnp.float32), precision=exact
    ).astype(jnp.bfloat16)
    received = lax.all_to_all(outgoing, "dp", split_axis=0, concat_axis=0, tiled=True)
    incoming = jnp.take(received, slot_source, axis=0)
    serve_local = jnp.where(slot_touched, incoming, serve_table[0])
    requests = request_ids[0]
    req_count = requests.shape[0]
    piece = lax.all_gather(serve_local, "dp", axis=0, tiled=True)
    counts = slot_counts(requests, jnp.int32(0) * block_rows, piece.shape[0], block_rows)
    served_pool = jnp.einsum("bfar,acr->bfc", counts, piece, preferred_element_type=jnp.float32)
    served_input = served_pool.astype(jnp.bfloat16)
    serve_pre = layer_one(served_input.reshape(req_count, -1), first_flat)
    unused_pre, serve_logits = layer_rest(serve_pre, second_weight, out_weight)
    return (linear, square, serve_local[None], serve_logits[None, :])


def solution(mesh):
    placed = (
        P(None, "mp", None),
        P("dp", "mp", None),
        P("dp", "mp", None),
        P("replica", "dp", "mp", None),
        P(None, "mp", None),
        P(),
        P(),
        P("groups", None),
        P(None, ("groups", "dp", "replica"), None, None),
        P(None, ("groups", "dp", "replica")),
        P("replica", None),
        P("replica", ("groups", "dp"), None, None),
    )
    return jax.shard_map(
        local,
        mesh=mesh,
        in_specs=placed,
        out_specs=(
            P(("groups", "dp"), "mp", None),
            P(("groups", "dp"), "mp", None),
            P(("groups", "replica"), "dp", "mp", None),
            P("replica", ("groups", "dp")),
        ),
        check_vma=False,
    )
```

profile of v0, /device:TPU:0, one launch (start us, length us, event | category | flops | bytes accessed | tf_op | source)
XLA Modules:
  0.0 272.6 jit_solution(10452675599442475538)
XLA Ops:
  7.2 1.0 copy.268
  8.2 0.9 slice_bitcast_fusion.16
  9.2 0.6 gather_fusion.1
  9.8 1.0 fusion.2
  10.9 1.0 fusion.3
  11.9 1.0 fusion.4
  13.0 1.0 fusion.5
  14.0 1.1 convolution_bitcast_fusion.1
  16.2 0.6 gather_fusion.2
  16.9 0.6 dynamic_slice.3
  17.5 0.7 iota_add_fusion
  18.5 18.3 %all-reduce.5.cloned.1.call-done = f32[256,512]{1,0:T(8,128)} async-done(((f32[256,512]{1,0:T(8,128)}), f32[256,512]{1,0:T(8,128)}) %all-reduce.5.cloned.1.call-update) | async-done | bytes 524304 | tf_op jit(solution)/shard_map/psum | solution.py:65
  36.8 1.3 fusion.92
  38.4 0.8 copy-done.8
  39.9 1.0 convolution_bitcast_fusion.18
  40.9 1.0 fusion.17
  41.8 1.0 fusion.16
  42.8 1.6 fusion.15
  44.5 69.7 %all-reduce.7.cloned.1.call-done = f32[4,32,128]{2,1,0:T(8,128)} async-done(((f32[4,32,128]{2,1,0:T(8,128)}), f32[4,32,128]{2,1,0:T(8,128)}) %all-reduce.7.cloned.1.call-update) | async-done | bytes 65552 | tf_op jit(solution)/shard_map/psum | solution.py:124
  114.3 1.2 broadcast_select_fusion
  115.8 18.0 %psum.44 = bf16[4,32,128]{2,0,1:T(4,128)(2,1)S(1)} all-reduce(bf16[4,32,128]{2,0,1:T(4,128)(2,1)S(1)} %convolution_convert_fusion.3), channel_id=1, replica_groups=mesh['groups'=2,'dp'=4,'replica'=2,'mp'=2] {'dp'}, use_global_device_ids=true, to_apply=%region_4.6 | all-reduce | flops 16384 | bytes 65536 | tf_op jit(solution)/shard_map/psum | solution.py:136
  133.8 0.6 scatter_fusion
  135.0 1.0 fusion.6
  136.1 1.0 fusion.7
  137.1 1.0 fusion.8
  138.2 1.1 fusion.9
  139.2 1.1 convolution_bitcast_fusion
  140.4 0.7 fusion.152
  141.1 16.3 %all-reduce.9.cloned.1.call-done = f32[256,512]{1,0:T(8,128)} async-done(((f32[256,512]{1,0:T(8,128)}), f32[256,512]{1,0:T(8,128)}) %all-reduce.9.cloned.1.call-update) | async-done | bytes 524304 | tf_op jit(solution)/shard_map/psum | solution.py:65
  157.4 1.3 fusion.93
  158.9 0.8 copy-done.9
  160.5 1.0 convolution_bitcast_fusion.14
  161.4 1.0 fusion.13
  162.4 1.0 fusion.12
  163.4 1.6 fusion.11
  165.0 69.8 %all-reduce.11.cloned.1.call-done = f32[4,32,128]{2,1,0:T(8,128)} async-done(((f32[4,32,128]{2,1,0:T(8,128)}), f32[4,32,128]{2,1,0:T(8,128)}) %all-reduce.11.cloned.1.call-update) | async-done | bytes 65552 | tf_op jit(solution)/shard_map/psum | solution.py:124
  234.9 1.1 fusion.119
  236.5 0.6 copy.144
  237.1 3.7 %all-to-all-start = ((bf16[4,32,128]{2,1,0:T(8,128)(2,1)}), bf16[4,32,128]{2,1,0:T(8,128)(2,1)S(1)}, u32[]{:S(2)}, u32[]{:S(2)}) async-start(bf16[4,32,128]{2,1,0:T(8,128)(2,1)} %copy.144), calls=%async_computation | async-start | bytes 65536 | tf_op jit(solution)/shard_map/all_to_all | solution.py:155
  240.8 0.7 compare_and_fusion.3
  241.4 0.6 copy.147
  242.1 0.6 copy.148
  242.7 3.7 %all-to-all-done = bf16[4,32,128]{2,1,0:T(8,128)(2,1)S(1)} async-done(((bf16[4,32,128]{2,1,0:T(8,128)(2,1)}), bf16[4,32,128]{2,1,0:T(8,128)(2,1)S(1)}, u32[]{:S(2)}, u32[]{:S(2)}) %all-to-all-start) | async-done | bytes 32800 | tf_op jit(solution)/shard_map/all_to_all | solution.py:155
  247.1 0.7 fusion.121
  247.8 13.3 %all_gather.3 = bf16[16,32,128]{2,1,0:T(8,128)(2,1)S(1)} all-gather(bf16[4,32,128]{2,1,0:T(8,128)(2,1)S(1)} %bitcast_select_fusion), channel_id=1, replica_groups=mesh['groups'=2,'dp'=4,'replica'=2,'mp'=2] {'dp'}, dimensions={0}, use_global_device_ids=true | all-gather | bytes 163840 | tf_op jit(solution)/shard_map/all_gather | solution.py:160
  261.1 0.6 fusion.18
  261.9 3.4 %psum.47 = f32[8,512]{1,0:T(8,128)S(1)} all-reduce(f32[8,512]{1,0:T(8,128)S(1)} %convolution_bitcast_fusion.19), channel_id=1, replica_groups=mesh['groups'=2,'dp'=4,'replica'=2,'mp'=2] {'mp'}, use_global_device_ids=true, to_apply=%region_11.13 | all-reduce | flops 4096 | bytes 32768 | tf_op jit(solution)/shard_map/psum | solution.py:65
  265.3 0.8 fusion.135
  (87 shorter events, 5.7 us)
Async XLA Ops:
  7.2 6.9 %copy-start = (bf16[16,32,512]{2,1,0:T(8,128)(2,1)S(1)}, bf16[16,32,512]{2,1,0:T(8,128)(2,1)}, u32[]{:S(2)}) copy-start(bf16[16,32,512]{2,1,0:T(8,128)(2,1)} %param.18) | copy-start | bytes 1572868
  7.2 2.0 copy-start.6
  7.2 29.6 %all-reduce.5.cloned.1.call-start = ((), (), s32[]{:S(2)}) async-start(), calls=%async_computation.1 | async-start | bytes 1048576 | tf_op jit(solution)/shard_map/psum | solution.py:65
  15.2 0.7 copy-start.10
  15.2 0.8 copy-start.7
  15.2 1.6 copy-start.11
  15.2 3.0 %copy-start.5 = (s32[1,8,16,4]{2,3,1,0:T(4,128)S(1)}, s32[1,8,16,4]{2,3,1,0:T(4,128)}, u32[]{:S(2)}) copy-start(s32[1,8,16,4]{2,3,1,0:T(4,128)} %param.25) | copy-start | bytes 6148
  15.2 21.7 %copy-start.1 = (bf16[512,256]{1,0:T(8,128)(2,1)S(1)}, bf16[512,256]{1,0:T(8,128)(2,1)}, u32[]{:S(2)}) copy-start(bf16[512,256]{1,0:T(8,128)(2,1)} %param.19) | copy-start | bytes 786436
  15.2 99.0 %all-reduce.7.cloned.1.call-start = ((), (), s32[]{:S(2)}) async-start(), calls=%async_computation.2 | async-start | bytes 131072 | tf_op jit(solution)/shard_map/psum | solution.py:124
  38.1 1.0 copy-start.8
  42.8 71.5 %copy-start.2 = (f32[4,32,128]{2,1,0:T(8,128)S(1)}, f32[4,32,128]{2,1,0:T(8,128)}, u32[]{:S(2)}) copy-start(f32[4,32,128]{2,1,0:T(8,128)} %param.16) | copy-start | bytes 196612
  42.8 71.5 %copy-start.4 = (f32[4,32,128]{2,1,0:T(8,128)S(1)}, f32[4,32,128]{2,1,0:T(8,128)}, u32[]{:S(2)}) copy-start(f32[4,32,128]{2,1,0:T(8,128)} %param.15) | copy-start | bytes 196612
  44.4 113.0 %all-reduce.9.cloned.1.call-start = ((), (), s32[]{:S(2)}) async-start(), calls=%async_computation.3 | async-start | bytes 1048576 | tf_op jit(solution)/shard_map/psum | solution.py:65
  140.4 94.5 %all-reduce.11.cloned.1.call-start = ((), (), s32[]{:S(2)}) async-start(), calls=%async_computation.4 | async-start | bytes 131072 | tf_op jit(solution)/shard_map/psum | solution.py:124
  158.7 1.0 copy-start.9
  236.2 10.8 %copy-start.3 = (bf16[1,4,32,128]{3,2,1,0:T(8,128)(2,1)S(1)}, bf16[1,4,32,128]{3,2,1,0:T(8,128)(2,1)}, u32[]{:S(2)}) copy-start(bf16[1,4,32,128]{3,2,1,0:T(8,128)(2,1)} %param.17) | copy-start | bytes 98308
  237.1 9.3 %all-to-all-start = ((bf16[4,32,128]{2,1,0:T(8,128)(2,1)}), bf16[4,32,128]{2,1,0:T(8,128)(2,1)S(1)}, u32[]{:S(2)}, u32[]{:S(2)}) async-start(bf16[4,32,128]{2,1,0:T(8,128)(2,1)} %copy.144), calls=%async_computation | async-start | bytes 65536 | tf_op jit(solution)/shard_map/all_to_all | solution.py:155
Sparse Core Ops, SparseCore 0:
  15.3 21.4 all-reduce.4
  44.6 69.6 all-reduce.6
  140.5 16.8 all-reduce.8
  165.1 69.6 all-reduce.10
where the time goes:
time: 273 us
  waiting for transfers between devices  178 us (65%)
  blocking collectives  34.7 us (13%)
  matrix products  28.2 us (10%)
  between operations  14.3 us (5%)
  local copies, waits for them, and re-layouts  10 us (4%)
  starting transfers between devices  3.82 us (1%)
  other arithmetic  3.59 us (1%)
    psum x2, waiting for transfers between devices, local(): total_grad = lax.psum(local_grad, ('dp', 'replica'))  140 us
    psum x2, waiting for transfers between devices, layer_one(): return lax.psum(partial_sum, 'mp')  34.6 us
    psum x1, blocking collectives, local(): refreshed = lax.psum(offered.astype(jnp.bfloat16), 'dp')  18 us
    all_gather x1, blocking collectives, local(): piece = lax.all_gather(serve_local, 'dp', axis=0, tiled=True)  13.3 us
    dot_general x8, matrix products, spread_slots(): jnp.einsum('bgar,bgc->acr', counts, grad_input[:, group_start:group_start...  9 us
    dot_general x8, matrix products, pool_slots(): jnp.einsum('bgar,acr->bgc', counts, active, preferred_element_type=jnp.fl...  8.35 us
  transfers between devices with their start and end apart: 5, of which 5 were waited for; matrix products, arithmetic and copies ran while one was open for 2% of the time, Pallas kernels for 0%

commit v1 on v0

v1 whole, which is shorter than its diff:
```python
import functools

import jax
import jax.numpy as jnp
from jax import lax
from jax.experimental import pallas as pl
from jax.experimental.pallas import tpu as pltpu
from jax.sharding import PartitionSpec as P

step_alpha = 0.5
step_beta = 1.0
sparse_penalty = 0.1
ridge_penalty = 0.05
f32 = jnp.float32
bf16 = jnp.bfloat16
VMEM = pl.BlockSpec(memory_space=pltpu.VMEM)
SMEM = pl.BlockSpec(memory_space=pltpu.SMEM)
nt_dims = (((1,), (1,)), ((), ()))


def kernel_call(body, out_shape, in_specs, scratch=(), limit=48):
    return pl.pallas_call(
        body,
        out_shape=out_shape,
        in_specs=in_specs,
        out_specs=jax.tree.map(lambda _: VMEM, out_shape),
        scratch_shapes=list(scratch),
        compiler_params=pltpu.CompilerParams(vmem_limit_bytes=limit * 1024 * 1024),
    )


def sigmoid(v):
    return 1.0 / (1.0 + jnp.exp(-v))


def ftrl_update(linear, square, gradient, current):
    grown = square + gradient * gradient
    root = jnp.sqrt(grown)
    sigma_term = (root - jnp.sqrt(square)) / step_alpha
    linear_next = linear + gradient - sigma_term * current
    shrunk = linear_next - jnp.clip(linear_next, -sparse_penalty, sparse_penalty)
    weights = -shrunk / ((step_beta + root) / step_alpha + ridge_penalty)
    return linear_next, grown, weights


def fill_counts(counts_ref, lanes_ids, column, blocks, rows):
    picks, lanes = lanes_ids.shape
    tiles = rows // 16
    level = lax.broadcasted_iota(jnp.int32, (tiles, 16, lanes), 1) + 16 * lax.broadcasted_iota(
        jnp.int32, (tiles, 16, lanes), 0
    )
    level = level.astype(bf16)
    one = jnp.ones((), bf16)
    zero = jnp.zeros((), bf16)
    for block in range(blocks):
        rel = jnp.clip(lanes_ids - block * rows, -1, rows)
        total = None
        for pick in range(picks):
            wide = jnp.broadcast_to(rel[pick : pick + 1], (16, lanes)).astype(f32).astype(bf16)
            hit = jnp.where(level == wide[None], one, zero)
            total = hit if total is None else total + hit
        counts_ref[block * rows : (block + 1) * rows, column : column + lanes] = total.reshape(
            rows, lanes
        )


def step_body(
    step,
    samples,
    ids_ref,
    labels_ref,
    table_own,
    table_other,
    w1_own,
    w1_other,
    w2_ref,
    wout_ref,
    counts_ref,
    active,
    rows,
):
    core = lax.axis_index("mp")
    slots = ids_ref.shape[1]
    half = table_own.shape[0]
    lanes = pl.ds(pl.multiple_of(core * samples, samples), samples)
    for slot in range(slots):
        fill_counts(counts_ref, ids_ref[step, slot, :, lanes], slot * samples, active, rows)
    counts = counts_ref[...]
    table = jnp.concatenate([table_own, table_other], axis=0)
    pooled = jnp.dot(table, counts, preferred_element_type=f32)

    def by_sample(low):
        stacked = jnp.concatenate(
            [
                pooled[low : low + half, slot * samples : (slot + 1) * samples]
                for slot in range(slots)
            ],
            axis=0,
        )
        return stacked.T.astype(bf16)

    first_own = w1_own[...]
    first_other = w1_other[...]
    pre_one = jnp.dot(by_sample(0), first_own, preferred_element_type=f32) + jnp.dot(
        by_sample(half), first_other, preferred_element_type=f32
    )
    sig_one = sigmoid(pre_one)
    hidden_one = (pre_one * sig_one).astype(bf16)
    second = w2_ref[...]
    pre_two = jnp.dot(hidden_one, second, preferred_element_type=f32)
    sig_two = sigmoid(pre_two)
    hidden_two = (pre_two * sig_two).astype(bf16).astype(f32)
    head = wout_ref[...].astype(f32)
    logit = jnp.sum(hidden_two * head, axis=1, keepdims=True)
    label_row = labels_ref[step : step + 1, lanes]
    label = jnp.broadcast_to(label_row, (samples, samples)).T[:, 0:1]
    error = sigmoid(logit) - label
    grad_two = (error * head * (sig_two * (1.0 + pre_two * (1.0 - sig_two)))).astype(bf16)
    back = lax.dot_general(grad_two, second, nt_dims, preferred_element_type=f32)
    grad_one = (back * (sig_one * (1.0 + pre_one * (1.0 - sig_one)))).astype(bf16)

    def by_column(first):
        spread = lax.dot_general(first, grad_one, nt_dims, preferred_element_type=f32).astype(bf16)
        return jnp.concatenate(
            [spread[slot * half : (slot + 1) * half] for slot in range(slots)], axis=1
        )

    grad_input = jnp.concatenate([by_column(first_own), by_column(first_other)], axis=0)
    return lax.dot_general(grad_input, counts, nt_dims, preferred_element_type=f32)


def first_step_kernel(
    samples,
    blocks_ref,
    ids_ref,
    labels_ref,
    slab_own,
    slab_other,
    w1_own,
    w1_other,
    w2_ref,
    wout_ref,
    share_own,
    share_other,
    rest_own,
    rest_other,
    counts_ref,
):
    active = blocks_ref.shape[1]
    rows = slab_own.shape[2]
    half = slab_own.shape[1]
    fresh = active // 2
    chosen = [blocks_ref[0, i] for i in range(active)]
    grad = step_body(
        0,
        samples,
        ids_ref,
        labels_ref,
        jnp.concatenate([slab_own[c] for c in chosen], axis=1),
        jnp.concatenate([slab_other[c] for c in chosen], axis=1),
        w1_own,
        w1_other,
        w2_ref,
        wout_ref,
        counts_ref,
        active,
        rows,
    )
    for i in range(active):
        part = grad[:, i * rows : (i + 1) * rows].astype(bf16)
        own, other, at = (rest_own, rest_other, i) if i < fresh else (share_own, share_other, i - fresh)
        own[at] = part[:half]
        other[at] = part[half:]


def second_step_kernel(
    samples,
    blocks_ref,
    ids_ref,
    labels_ref,
    slab_own,
    slab_other,
    new_own,
    new_other,
    rest_own,
    rest_other,
    w1_own,
    w1_other,
    w2_ref,
    wout_ref,
    out_own,
    out_other,
    counts_ref,
):
    active = blocks_ref.shape[1]
    rows = slab_own.shape[2]
    half = slab_own.shape[1]
    fresh = active // 2

    def tables(shared, slab):
        return jnp.concatenate(
            [shared[i] for i in range(fresh)] + [slab[blocks_ref[1, i]] for i in range(fresh, active)],
            axis=1,
        )

    grad = step_body(
        1,
        samples,
        ids_ref,
        labels_ref,
        tables(new_own, slab_own),
        tables(new_other, slab_other),
        w1_own,
        w1_other,
        w2_ref,
        wout_ref,
        counts_ref,
        active,
        rows,
    )
    out_own[0:fresh] = rest_own[...]
    out_other[0:fresh] = rest_other[...]
    for i in range(active):
        part = grad[:, i * rows : (i + 1) * rows].astype(bf16)
        out_own[fresh + i] = part[:half]
        out_other[fresh + i] = part[half:]


def pack_kernel(linear_ref, square_ref, serve_ref, out_ref):
    owned = linear_ref.shape[0]
    linear = linear_ref[...]
    high = linear.astype(bf16)
    out_ref[0:owned] = high
    out_ref[owned : 2 * owned] = (linear - high.astype(f32)).astype(bf16)
    out_ref[2 * owned : 3 * owned] = square_ref[...].astype(bf16)
    out_ref[3 * owned : 4 * owned] = serve_ref[...]


def tree_sum(parts):
    parts = list(parts)
    while len(parts) > 1:
        parts = [
            parts[i] + parts[i + 1] if i + 1 < len(parts) else parts[i]
            for i in range(0, len(parts), 2)
        ]
    return parts[0]


def fetch_state(block, me, linear_ref, square_ref, packs, linear_at, square_at, at):
    owned = linear_ref.shape[0]
    owner = block // owned
    place = block % owned

    @pl.when(owner == me)
    def _():
        linear_at[at] = linear_ref[place]
        square_at[at] = square_ref[place]

    def take(piece):
        linear_at[at] = piece(place).astype(f32) + piece(owned + place).astype(f32)
        square_at[at] = piece(2 * owned + place).astype(f32)

    if len(packs) == 1:

        @pl.when(owner != me)
        def _():
            take(lambda i: packs[0][owner, i])

    else:
        for k, pack in enumerate(packs):

            @pl.when((owner ^ me) == k + 1)
            def _():
                take(lambda i: pack[i])


def share_kernel(sums_count, packs_count, *refs):
    blocks_ref, linear_ref, square_ref, slab_own = refs[:4]
    sums = refs[4 : 4 + sums_count]
    packs = refs[4 + sums_count : 4 + sums_count + packs_count]
    new_own, linear_out, square_out, linear_at, square_at = refs[4 + sums_count + packs_count :]
    active = blocks_ref.shape[1]
    fresh = active // 2
    me = lax.axis_index("dp")
    for i in range(active - fresh):
        block = blocks_ref[0, fresh + i]
        fetch_state(block, me, linear_ref, square_ref, packs, linear_at, square_at, i)
        gradient = tree_sum([part[i].astype(f32) for part in sums])
        linear, square, weights = ftrl_update(
            linear_at[i], square_at[i], gradient, slab_own[block].astype(f32)
        )
        linear_out[i] = linear
        square_out[i] = square
        new_own[i] = weights.astype(bf16)


def finish_kernel(owners, sums_count, packs_count, *refs):
    blocks_ref, layout_ref, req_ref, linear_ref, square_ref, serve_ref, slab_own = refs[:7]
    new_own, linear_mid, square_mid, w1_own = refs[7:11]
    sums = refs[11 : 11 + sums_count]
    packs = refs[11 + sums_count : 11 + sums_count + packs_count]
    linear_out, square_out, serve_out, partial_out = refs[11 + sums_count + packs_count :][:4]
    table_at, counts_ref, linear_at, square_at = refs[11 + sums_count + packs_count + 4 :]
    active = blocks_ref.shape[1]
    owned, half, rows = linear_ref.shape
    fresh = active // 2
    me = lax.axis_index("dp")
    for k in range(owners):
        if len(packs) == 1:
            table_at[k * owned : (k + 1) * owned] = packs[0][k, 3 * owned : 4 * owned]
        elif k == 0:
            table_at[pl.ds(me * owned, owned)] = serve_ref[...]
        else:
            table_at[pl.ds((me ^ k) * owned, owned)] = packs[k - 1][3 * owned : 4 * owned]
    linear_out[...] = linear_ref[...]
    square_out[...] = square_ref[...]
    serve_out[...] = serve_ref[...]
    for i in range(active + fresh):
        block = blocks_ref[0, i] if i < fresh else blocks_ref[1, i - fresh]
        gradient = tree_sum([part[i].astype(f32) for part in sums])
        if fresh <= i < active:
            linear_old = linear_mid[i - fresh]
            square_old = square_mid[i - fresh]
            current = new_own[i - fresh]
        else:
            fetch_state(block, me, linear_ref, square_ref, packs, linear_at, square_at, i)
            linear_old = linear_at[i]
            square_old = square_at[i]
            current = slab_own[block]
        linear, square, weights = ftrl_update(
            linear_old, square_old, gradient, current.astype(f32)
        )
        weights = weights.astype(bf16)
        owner = block // owned
        place = block % owned
        target = layout_ref[0, (owner + place) % owners]
        table_at[target * owned + place] = weights

        @pl.when(owner == me)
        def _():
            linear_out[place] = linear
            square_out[place] = square

        @pl.when(target == me)
        def _():
            serve_out[place] = weights

    requests, picks, slots = req_ref.shape
    lanes = requests * slots
    lanes_ids = jnp.concatenate([req_ref[i] for i in range(requests)], axis=1)
    positions = owners * owned
    fill_counts(counts_ref, lanes_ids, 0, positions, rows)
    table = jnp.concatenate([table_at[i] for i in range(positions)], axis=1)
    pooled = jnp.dot(table, counts_ref[...], preferred_element_type=f32)
    stacked = jnp.concatenate([pooled] * slots, axis=0)
    wanted = lax.broadcasted_iota(jnp.int32, stacked.shape, 0) // half
    present = lax.broadcasted_iota(jnp.int32, stacked.shape, 1) % slots
    stacked = jnp.where(wanted == present, stacked, 0.0)
    product = jnp.dot(stacked.T.astype(bf16), w1_own[...], preferred_element_type=f32)
    partial_out[...] = jnp.sum(product.reshape(requests, slots, product.shape[1]), axis=1)


def score_kernel(own_ref, other_ref, w2_ref, wout_ref, out_ref):
    pre_one = own_ref[...] + other_ref[...]
    hidden_one = (pre_one * sigmoid(pre_one)).astype(bf16)
    pre_two = jnp.dot(hidden_one, w2_ref[...], preferred_element_type=f32)
    hidden_two = (pre_two * sigmoid(pre_two)).astype(bf16).astype(f32)
    logit = jnp.sum(hidden_two * wout_ref[...].astype(f32), axis=1, keepdims=True)
    out_ref[...] = logit


def swap(value, axes, sizes, bits):
    shape = tuple(sizes[a] for a in axes)
    count = 1
    for size in shape:
        count *= size
    pairs = []
    for index in range(count):
        rest, coords = index, []
        for size in reversed(shape):
            coords.append(rest % size)
            rest //= size
        coords = coords[::-1]
        target = 0
        for coord, bit, size in zip(coords, bits, shape):
            target = target * size + (coord ^ bit)
        pairs.append((index, target))
    return lax.ppermute(value, axes, pairs)


def reduce_halves(own, other, sizes):
    def add(parts):
        return tree_sum([p.astype(f32) for p in parts]).astype(bf16)

    replicas, owners = sizes["replica"], sizes["dp"]
    parts = [own]
    if replicas > 1:
        parts = [
            own,
            swap(own, ("replica", "mp"), sizes, (1, 0)),
            swap(other, ("replica", "mp"), sizes, (0, 1)),
            swap(other, ("replica", "mp"), sizes, (1, 1)),
        ]
    else:
        parts = [own, swap(other, ("mp",), sizes, (1,))]
    bit = 2
    while bit < replicas:
        total = add(parts)
        parts = [total, swap(total, ("replica",), sizes, (bit,))]
        bit *= 2
    bit = 1
    while bit < owners:
        total = add(parts)
        steps = [k * bit for k in range(1, 4) if k * bit < owners]
        parts = [total] + [swap(total, ("dp",), sizes, (k,)) for k in steps]
        bit *= 4
    return parts


def local(
    sizes,
    hot_slab,
    linear_state,
    square_state,
    serve_table,
    first_weight,
    second_weight,
    out_weight,
    step_blocks,
    feature_ids,
    click_labels,
    serve_layout,
    request_ids,
):
    owners = sizes["dp"]
    owned, half, rows = linear_state.shape
    active = step_blocks.shape[1]
    fresh = active // 2
    samples = feature_ids.shape[1] // sizes["mp"]
    slots = feature_ids.shape[2]
    units = first_weight.shape[2]
    ids = jnp.transpose(feature_ids, (0, 2, 3, 1))
    req = jnp.transpose(request_ids[0], (0, 2, 1))
    w1_own = first_weight.reshape(-1, units)
    w1_other = swap(w1_own, ("mp",), sizes, (1,))
    slab_other = swap(hot_slab, ("mp",), sizes, (1,))
    head = out_weight.reshape(1, -1)
    serve_own = serve_table[0]

    pack = kernel_call(
        pack_kernel, jax.ShapeDtypeStruct((4 * owned, half, rows), bf16), [VMEM] * 3
    )(linear_state, square_state, serve_own)
    if owners == 4:
        packs = [swap(pack, ("dp",), sizes, (k,)) for k in range(1, owners)]
    else:
        packs = [lax.all_gather(pack, "dp", axis=0, tiled=False)]

    counts = pltpu.VMEM((active * rows, slots * samples), bf16)
    halves = jax.ShapeDtypeStruct((fresh, half, rows), bf16)
    shared = jax.ShapeDtypeStruct((active - fresh, half, rows), bf16)
    share_own, share_other, rest_own, rest_other = kernel_call(
        functools.partial(first_step_kernel, samples),
        (shared, shared, halves, halves),
        [SMEM] + [VMEM] * 8,
        [counts],
    )(
        step_blocks,
        ids,
        click_labels,
        hot_slab,
        slab_other,
        w1_own,
        w1_other,
        second_weight,
        head,
    )
    sums = reduce_halves(share_own, share_other, sizes)
    state = jax.ShapeDtypeStruct((active - fresh, half, rows), f32)
    state_at = pltpu.VMEM((active + fresh, half, rows), f32)
    new_own, linear_mid, square_mid = kernel_call(
        functools.partial(share_kernel, len(sums), len(packs)),
        (shared, state, state),
        [SMEM] + [VMEM] * (3 + len(sums) + len(packs)),
        [state_at, state_at],
    )(step_blocks, linear_state, square_state, hot_slab, *sums, *packs)
    new_other = swap(new_own, ("mp",), sizes, (1,))

    payload = jax.ShapeDtypeStruct((active + fresh, half, rows), bf16)
    grad_own, grad_other = kernel_call(
        functools.partial(second_step_kernel, samples),
        (payload, payload),
        [SMEM] + [VMEM] * 12,
        [counts],
    )(
        step_blocks,
        ids,
        click_labels,
        hot_slab,
        slab_other,
        new_own,
        new_other,
        rest_own,
        rest_other,
        w1_own,
        w1_other,
        second_weight,
        head,
    )
    sums = reduce_halves(grad_own, grad_other, sizes)
    requests = req.shape[0]
    positions = owners * owned
    linear_out, square_out, serve_out, partial = kernel_call(
        functools.partial(finish_kernel, owners, len(sums), len(packs)),
        (
            jax.ShapeDtypeStruct(linear_state.shape, f32),
            jax.ShapeDtypeStruct(square_state.shape, f32),
            jax.ShapeDtypeStruct(serve_own.shape, bf16),
            jax.ShapeDtypeStruct((requests, units), f32),
        ),
        [SMEM, SMEM] + [VMEM] * (9 + len(sums) + len(packs)),
        [
            pltpu.VMEM((positions, half, rows), bf16),
            pltpu.VMEM((positions * rows, requests * slots), bf16),
            state_at,
            state_at,
        ],
    )(
        step_blocks,
        serve_layout,
        req,
        linear_state,
        square_state,
        serve_own,
        hot_slab,
        new_own,
        linear_mid,
        square_mid,
        w1_own,
        *sums,
        *packs,
    )
    partial_other = swap(partial, ("mp",), sizes, (1,))
    scores = kernel_call(score_kernel, jax.ShapeDtypeStruct((requests, 1), f32), [VMEM] * 4)(
        partial, partial_other, second_weight, head
    )
    return linear_out, square_out, serve_out[None], scores.reshape(1, requests)


def solution(mesh):
    sizes = dict(mesh.shape)
    placed = (
        P(None, "mp", None),
        P("dp", "mp", None),
        P("dp", "mp", None),
        P("replica", "dp", "mp", None),
        P(None, "mp", None),
        P(),
        P(),
        P("groups", None),
        P(None, ("groups", "dp", "replica"), None, None),
        P(None, ("groups", "dp", "replica")),
        P("replica", None),
        P("replica", ("groups", "dp"), None, None),
    )
    return jax.shard_map(
        functools.partial(local, sizes),
        mesh=mesh,
        in_specs=placed,
        out_specs=(
            P(("groups", "dp"), "mp", None),
            P(("groups", "dp"), "mp", None),
            P(("groups", "replica"), "dp", "mp", None),
            P("replica", ("groups", "dp")),
        ),
        check_vma=False,
    )
```

time: 273 us -> 55.9 us (0.20)
  waiting for transfers between devices: 178 us -> 13.6 us
  blocking collectives: 34.7 us -> 0 us
  matrix products: 28.2 us -> 0 us
  starting transfers between devices: 3.82 us -> 24.9 us
  between operations: 14.3 us -> 0.74 us
  Pallas kernels: 0 us -> 11.2 us
  local copies, waits for them, and re-layouts: 10 us -> 4.53 us
  other arithmetic: 3.59 us -> 0.69 us
    psum x4 -> x0, waiting for transfers between devices: 174 us -> none  [the longest x2 140 us: local(): total_grad = lax.psum(local_grad, ('dp', 'replica'))]
    dot_general x31 -> x0, matrix products: 28.2 us -> none  [the longest x8 9 us: spread_slots(): jnp.einsum('bgar,bgc->acr', counts, grad_input[:, group_start:group_start...]
    ppermute x0 -> x19, starting transfers between devices: none -> 24.9 us  [swap(): return lax.ppermute(value, axes, pairs)]
    psum x2 -> x0, blocking collectives: 21.4 us -> none  [the longest x1 18 us: local(): refreshed = lax.psum(offered.astype(jnp.bfloat16), 'dp')]
    ppermute x0 -> x19, waiting for transfers between devices: none -> 13.6 us  [swap(): return lax.ppermute(value, axes, pairs)]
    all_gather x1 -> x0, blocking collectives: 13.3 us -> none  [local(): piece = lax.all_gather(serve_local, 'dp', axis=0, tiled=True)]
    pallas_call x0 -> x6, Pallas kernels: none -> 11.2 us  [the longest x1 4.04 us: local(): kernel_call(functools.partial(second_step_kernel, samples), (payload, pay...]
    all_to_all x1 -> x0, waiting for transfers between devices: 3.72 us -> none  [local(): lax.all_to_all(outgoing, 'dp', split_axis=0, concat_axis=0, tiled=True)]
  transfers between devices with their start and end apart: 5 -> 19, of which waited for: 5 -> 9; matrix products, arithmetic and copies ran while one was open for 2% -> 0% of each run, Pallas kernels for 0% -> 0%
where the time goes in v1:
time: 55.9 us; the launch traced here: 55.6 us
  starting transfers between devices  24.9 us (45%)
  waiting for transfers between devices  13.6 us (24%)
  Pallas kernels  11.2 us (20%)
  local copies, waits for them, and re-layouts  4.53 us (8%)
  between operations  0.74 us (1%)
  other arithmetic  0.69 us (1%)
    ppermute x19, starting transfers between devices, swap(): return lax.ppermute(value, axes, pairs)  24.9 us
    ppermute x19, waiting for transfers between devices, swap(): return lax.ppermute(value, axes, pairs)  13.6 us
    unnamed x32, local copies, waits for them, and re-layouts  4.53 us
    pallas_call x1, Pallas kernels, local(): kernel_call(functools.partial(second_step_kernel, samples), (payload, pay...  4.04 us
    pallas_call x1, Pallas kernels, local(): kernel_call(functools.partial(first_step_kernel, samples), (shared, share...  4.03 us
    pallas_call x1, Pallas kernels, local(): kernel_call(functools.partial(finish_kernel, owners, len(sums), len(packs...  2.22 us
  transfers between devices with their start and end apart: 19, of which 9 were waited for; matrix products, arithmetic and copies ran while one was open for 0% of the time, Pallas kernels for 0%

profile of v1, /device:TPU:0, one launch (start us, length us, event | category | flops | bytes accessed | tf_op | source)
XLA Modules:
  0.0 55.6 jit_solution(6913708471731203101)
XLA Ops:
  0.7 0.5 collective-permute-start.1
  1.2 0.1 collective-permute-start
  1.2 0.0 copy-done.15
  1.3 1.8 %collective-permute-done.slab_other = bf16[16,32,128]{2,1,0:T(8,128)(2,1)S(1)} collective-permute-done((bf16[16,32,128]{2,1,0:T(8,128)(2,1)}, bf16[16,32,128]{2,1,0:T(8,128)(2,1)S(1)}, u32[]{:S(2)}, u32[]{:S(2)}) %collective-permute-start) | collective-permute-done | bytes 131104 | tf_op jit(solution)/shard_map/ppermute | solution.py:388
  3.1 0.0 collective-permute-done.1.w1_other
  3.1 1.0 %copy-done = bf16[16,32,512]{2,1,0:T(8,128)(2,1)S(1)} copy-done((bf16[16,32,512]{2,1,0:T(8,128)(2,1)S(1)}, bf16[16,32,512]{2,1,0:T(8,128)(2,1)}, u32[]{:S(2)}) %copy-start) | copy-done | bytes 524312
  4.2 0.9 %copy-done.2 = bf16[512,256]{1,0:T(8,128)(2,1)S(1)} copy-done((bf16[512,256]{1,0:T(8,128)(2,1)S(1)}, bf16[512,256]{1,0:T(8,128)(2,1)}, u32[]{:S(2)}) %copy-start.2) | copy-done | bytes 262168
  5.1 0.9 %copy-done.4 = bf16[16,32,128]{2,1,0:T(8,128)(2,1)S(1)} copy-done((bf16[16,32,128]{2,1,0:T(8,128)(2,1)S(1)}, bf16[16,32,128]{2,1,0:T(8,128)(2,1)}, u32[]{:S(2)}) %copy-start.4) | copy-done | bytes 131096
  6.0 0.9 %copy-done.8 = s32[2,256,16,4]{1,3,2,0:T(4,128)S(1)} copy-done((s32[2,256,16,4]{1,3,2,0:T(4,128)S(1)}, s32[2,256,16,4]{1,3,2,0:T(4,128)}, u32[]{:S(2)}) %copy-start.8) | copy-done | bytes 131096
  6.9 4.0 %shard_map.147 = (bf16[2,32,128]{2,1,0:T(8,128)(2,1)S(1)}, bf16[2,32,128]{2,1,0:T(8,128)(2,1)S(1)}, bf16[2,32,128]{2,1,0:T(8,128)(2,1)S(1)}, bf16[2,32,128]{2,1,0:T(8,128)(2,1)S(1)}) custom-call(s32[2,4]{1,0:T(2,128)S(1)} %copy-done.11, s32[2,16,4,256]{3,2,1,0:T(4,128)S(1)} %bitcast.12, f32[2,256]{1,0:T(2,128)S(1)} %copy-done.13, ...), custom_call_target="tpu_custom_call" | custom-call | tf_op jit(solution)/shard_map/pallas_call | solution.py:461
  11.0 2.9 %collective-permute-start.2 = (bf16[2,32,128]{2,1,0:T(8,128)(2,1)S(1)}, bf16[2,32,128]{2,1,0:T(8,128)(2,1)S(1)}, u32[]{:S(2)}, u32[]{:S(2)}) collective-permute-start(bf16[2,32,128]{2,1,0:T(8,128)(2,1)S(1)} %get-tuple-element.17), channel_id=1, source_target_pairs={{0,2},{1,3},{2,0},{3,1},{4,6},{5,7},{6,4},{7,5},{8,10},{9,11},{10,... | collective-permute-start | bytes 49160 | tf_op jit(solution)/shard_map/ppermute | solution.py:388
  13.9 0.0 collective-permute-start.4
  13.9 0.2 collective-permute-start.3
  14.1 0.0 copy-start.1
  14.1 4.1 %collective-permute-start.10 = (bf16[16,32,128]{2,1,0:T(8,128)(2,1)S(1)}, bf16[16,32,128]{2,1,0:T(8,128)(2,1)S(1)}, u32[]{:S(2)}, u32[]{:S(2)}) collective-permute-start(bf16[16,32,128]{2,1,0:T(8,128)(2,1)S(1)} %shard_map.148), channel_id=1, source_target_pairs={{0,12},{4,8},{8,4},{12,0},{1,13},{5,9},{9,5},{13,1},{2,14},{6,10},... | collective-permute-start | bytes 393224 | tf_op jit(solution)/shard_map/ppermute | solution.py:388
  18.2 0.0 collective-permute-start.9
  18.2 0.0 collective-permute-done.2
  18.3 0.6 %collective-permute-start.8 = (bf16[16,32,128]{2,1,0:T(8,128)(2,1)S(1)}, bf16[16,32,128]{2,1,0:T(8,128)(2,1)S(1)}, u32[]{:S(2)}, u32[]{:S(2)}) collective-permute-start(bf16[16,32,128]{2,1,0:T(8,128)(2,1)S(1)} %shard_map.148), channel_id=1, source_target_pairs={{0,4},{4,0},{8,12},{12,8},{1,5},{5,1},{9,13},{13,9},{2,6},{6,2},{1... | collective-permute-start | bytes 393224 | tf_op jit(solution)/shard_map/ppermute | solution.py:388
  18.9 0.0 collective-permute-done.4
  18.9 0.0 collective-permute-done.3
  18.9 0.0 copy-start.9
  18.9 3.8 %collective-permute-start.7 = (bf16[2,32,128]{2,1,0:T(8,128)(2,1)S(1)}, bf16[2,32,128]{2,1,0:T(8,128)(2,1)S(1)}, u32[]{:S(2)}, u32[]{:S(2)}) collective-permute-start(bf16[2,32,128]{2,1,0:T(8,128)(2,1)S(1)} %add_convert_fusion.1.refs_4_), channel_id=1, source_target_pairs={{0,12},{4,8},{8,4},{12,0},{1,13},{5,9},{9,5},{13,1},{2,14},{6,10},... | collective-permute-start | bytes 49160 | tf_op jit(solution)/shard_map/ppermute | solution.py:388
  22.7 0.0 collective-permute-start.6
  22.7 0.0 collective-permute-done.10.refs_10_.refs_17_
  22.7 5.8 %collective-permute-start.5 = (bf16[2,32,128]{2,1,0:T(8,128)(2,1)S(1)}, bf16[2,32,128]{2,1,0:T(8,128)(2,1)S(1)}, u32[]{:S(2)}, u32[]{:S(2)}) collective-permute-start(bf16[2,32,128]{2,1,0:T(8,128)(2,1)S(1)} %add_convert_fusion.1.refs_4_), channel_id=1, source_target_pairs={{0,4},{4,0},{8,12},{12,8},{1,5},{5,1},{9,13},{13,9},{2,6},{6,2},{1... | collective-permute-start | bytes 49160 | tf_op jit(solution)/shard_map/ppermute | solution.py:388
  28.5 2.1 %collective-permute-done.9.refs_9_.refs_16_ = bf16[16,32,128]{2,1,0:T(8,128)(2,1)S(1)} collective-permute-done((bf16[16,32,128]{2,1,0:T(8,128)(2,1)S(1)}, bf16[16,32,128]{2,1,0:T(8,128)(2,1)S(1)}, u32[]{:S(2)}, u32[]{:S(2)}) %collective-permute-start.9) | collective-permute-done | bytes 131104 | tf_op jit(solution)/shard_map/ppermute | solution.py:388
  30.6 0.3 collective-permute-done.6.refs_6_
  30.9 0.7 %shard_map.149 = (bf16[2,32,128]{2,1,0:T(8,128)(2,1)S(1)}, f32[2,32,128]{2,1,0:T(8,128)S(1)}, f32[2,32,128]{2,1,0:T(8,128)S(1)}) custom-call(s32[2,4]{1,0:T(2,128)S(1)} %copy-done.11, f32[4,32,128]{2,1,0:T(8,128)S(1)} %copy-done.6, f32[4,32,128]{2,1,0:T(8,128)S(1)} %copy-done.7, bf16[16,32,128]{2,1,0:T(8,128)(2,1)S(1)} %copy-done.5, ...), custom_call_target="tpu_custom_call" | custom-call | tf_op jit(solution)/shard_map/pallas_call | solution.py:480
  31.6 0.1 collective-permute-start.11
  31.7 1.2 %collective-permute-done.11.new_other = bf16[2,32,128]{2,1,0:T(8,128)(2,1)S(1)} collective-permute-done((bf16[2,32,128]{2,1,0:T(8,128)(2,1)S(1)}, bf16[2,32,128]{2,1,0:T(8,128)(2,1)S(1)}, u32[]{:S(2)}, u32[]{:S(2)}) %collective-permute-start.11) | collective-permute-done | bytes 16416 | tf_op jit(solution)/shard_map/ppermute | solution.py:388
  32.8 4.0 %shard_map.150 = (bf16[6,32,128]{2,1,0:T(8,128)(2,1)S(1)}, bf16[6,32,128]{2,1,0:T(8,128)(2,1)S(1)}) custom-call(s32[2,4]{1,0:T(2,128)S(1)} %copy-done.11, s32[2,16,4,256]{3,2,1,0:T(4,128)S(1)} %bitcast.13, f32[2,256]{1,0:T(2,128)S(1)} %copy-done.13, bf16[16,32,128]{2,1,0:T(8,128)(2,1)S(1)} %copy-done.5, ...), custom_call_target="tpu_custom_call" | custom-call | tf_op jit(solution)/shard_map/pallas_call | solution.py:489
  36.9 1.6 %collective-permute-start.12 = (bf16[6,32,128]{2,1,0:T(8,128)(2,1)S(1)}, bf16[6,32,128]{2,1,0:T(8,128)(2,1)S(1)}, u32[]{:S(2)}, u32[]{:S(2)}) collective-permute-start(bf16[6,32,128]{2,1,0:T(8,128)(2,1)S(1)} %get-tuple-element.24), channel_id=1, source_target_pairs={{0,2},{1,3},{2,0},{3,1},{4,6},{5,7},{6,4},{7,5},{8,10},{9,11},{10,... | collective-permute-start | bytes 147464 | tf_op jit(solution)/shard_map/ppermute | solution.py:388
  38.5 0.0 collective-permute-start.14
  38.5 0.6 %collective-permute-start.13 = (bf16[6,32,128]{2,1,0:T(8,128)(2,1)S(1)}, bf16[6,32,128]{2,1,0:T(8,128)(2,1)S(1)}, u32[]{:S(2)}, u32[]{:S(2)}) collective-permute-start(bf16[6,32,128]{2,1,0:T(8,128)(2,1)S(1)} %get-tuple-element.25), channel_id=1, source_target_pairs={{0,1},{1,0},{2,3},{3,2},{4,5},{5,4},{6,7},{7,6},{8,9},{9,8},{10,11... | collective-permute-start | bytes 147464 | tf_op jit(solution)/shard_map/ppermute | solution.py:388
  39.1 1.9 %collective-permute-done.12 = bf16[6,32,128]{2,1,0:T(8,128)(2,1)S(1)} collective-permute-done((bf16[6,32,128]{2,1,0:T(8,128)(2,1)S(1)}, bf16[6,32,128]{2,1,0:T(8,128)(2,1)S(1)}, u32[]{:S(2)}, u32[]{:S(2)}) %collective-permute-start.12) | collective-permute-done | bytes 49184 | tf_op jit(solution)/shard_map/ppermute | solution.py:388
  41.0 1.5 %collective-permute-done.14 = bf16[6,32,128]{2,1,0:T(8,128)(2,1)S(1)} collective-permute-done((bf16[6,32,128]{2,1,0:T(8,128)(2,1)S(1)}, bf16[6,32,128]{2,1,0:T(8,128)(2,1)S(1)}, u32[]{:S(2)}, u32[]{:S(2)}) %collective-permute-start.14) | collective-permute-done | bytes 49184 | tf_op jit(solution)/shard_map/ppermute | solution.py:388
  42.5 2.6 %collective-permute-start.17 = (bf16[6,32,128]{2,1,0:T(8,128)(2,1)S(1)}, bf16[6,32,128]{2,1,0:T(8,128)(2,1)S(1)}, u32[]{:S(2)}, u32[]{:S(2)}) collective-permute-start(bf16[6,32,128]{2,1,0:T(8,128)(2,1)S(1)} %add_convert_fusion.refs_11_), channel_id=1, source_target_pairs={{0,12},{4,8},{8,4},{12,0},{1,13},{5,9},{9,5},{13,1},{2,14},{6,10},... | collective-permute-start | bytes 147464 | tf_op jit(solution)/shard_map/ppermute | solution.py:388
  45.1 0.3 collective-permute-start.16
  45.4 1.6 %collective-permute-start.15 = (bf16[6,32,128]{2,1,0:T(8,128)(2,1)S(1)}, bf16[6,32,128]{2,1,0:T(8,128)(2,1)S(1)}, u32[]{:S(2)}, u32[]{:S(2)}) collective-permute-start(bf16[6,32,128]{2,1,0:T(8,128)(2,1)S(1)} %add_convert_fusion.refs_11_), channel_id=1, source_target_pairs={{0,4},{4,0},{8,12},{12,8},{1,5},{5,1},{9,13},{13,9},{2,6},{6,2},{1... | collective-permute-start | bytes 147464 | tf_op jit(solution)/shard_map/ppermute | solution.py:388
  47.0 2.0 %collective-permute-done.17.refs_14_ = bf16[6,32,128]{2,1,0:T(8,128)(2,1)S(1)} collective-permute-done((bf16[6,32,128]{2,1,0:T(8,128)(2,1)S(1)}, bf16[6,32,128]{2,1,0:T(8,128)(2,1)S(1)}, u32[]{:S(2)}, u32[]{:S(2)}) %collective-permute-start.17) | collective-permute-done | bytes 49184 | tf_op jit(solution)/shard_map/ppermute | solution.py:388
  49.0 1.6 %collective-permute-done.16.refs_13_ = bf16[6,32,128]{2,1,0:T(8,128)(2,1)S(1)} collective-permute-done((bf16[6,32,128]{2,1,0:T(8,128)(2,1)S(1)}, bf16[6,32,128]{2,1,0:T(8,128)(2,1)S(1)}, u32[]{:S(2)}, u32[]{:S(2)}) %collective-permute-start.16) | collective-permute-done | bytes 49184 | tf_op jit(solution)/shard_map/ppermute | solution.py:388
  50.7 0.0 collective-permute-done.15.refs_12_
  50.7 0.6 %copy-done.14 = s32[1,4]{1,0:T(1,128)S(1)} copy-done((s32[1,4]{1,0:T(1,128)S(1)}, s32[1,4]{1,0:T(1,128)}, u32[]{:S(2)}) %copy-start.14) | copy-done | bytes 40
  51.3 2.2 %shard_map.151 = (f32[4,32,128]{2,1,0:T(8,128)}, f32[4,32,128]{2,1,0:T(8,128)}, bf16[4,32,128]{2,1,0:T(8,128)(2,1)}, f32[8,512]{1,0:T(8,128)S(1)}) custom-call(s32[2,4]{1,0:T(2,128)S(1)} %copy-done.11, s32[1,4]{1,0:T(1,128)S(1)} %copy-done.14, s32[8,4,16]{2,1,0:T(4,128)S(1)} %bitcast.16, f32[4,32,128]{2,1,0:T(8,128)S(1)} %copy-done.6, ...), custom_call_target="tpu_custom_call" | custom-call | tf_op jit(solution)/shard_map/pallas_call | solution.py:512
  53.5 0.1 collective-permute-start.18
  53.6 1.1 %collective-permute-done.18.other_ref = f32[8,512]{1,0:T(8,128)S(1)} collective-permute-done((f32[8,512]{1,0:T(8,128)S(1)}, f32[8,512]{1,0:T(8,128)S(1)}, u32[]{:S(2)}, u32[]{:S(2)}) %collective-permute-start.18) | collective-permute-done | bytes 16416 | tf_op jit(solution)/shard_map/ppermute | solution.py:388
  54.7 0.2 shard_map.152
  55.0 0.6 %reduce = f32[8]{0:T(128)} reduce(f32[8,1]{1,0:T(8,128)S(1)} %shard_map.152, f32[]{:T(128)} %constant.3), dimensions={1}, to_apply=%pallas_call.49.reduce_sub_computation | reduce | bytes 68 | tf_op jit(solution)/shard_map/pallas_call | solution.py:543
  (32 shorter events, 0.1 us)
Async XLA Ops:
  0.6 0.7 %copy-start.15 = (bf16[256]{0:T(256)(128)(2,1)S(1)}, bf16[256]{0:T(256)(128)(2,1)}, u32[]{:S(2)}) copy-start(bf16[256]{0:T(256)(128)(2,1)} %param.18) | copy-start | bytes 1540
  0.6 2.5 %copy-start.13 = (f32[2,256]{1,0:T(2,128)S(1)}, f32[2,256]{1,0:T(2,128)}, u32[]{:S(2)}) copy-start(f32[2,256]{1,0:T(2,128)} %labels_ref.3) | copy-start | bytes 6148
  0.7 2.5 %collective-permute-start.1 = (bf16[512,512]{1,0:T(8,128)(2,1)}, bf16[512,512]{1,0:T(8,128)(2,1)S(1)}, u32[]{:S(2)}, u32[]{:S(2)}) collective-permute-start(bf16[512,512]{1,0:T(8,128)(2,1)} %bitcast.8), channel_id=1, source_target_pairs={{0,1},{1,0},{2,3},{3,2},{4,5},{5,4},{6,7},{7,6},{8,9},{9,8},{10,11... | collective-permute-start | bytes 1572872 | tf_op jit(solution)/shard_map/ppermute | solution.py:388
  1.2 1.9 %collective-permute-start = (bf16[16,32,128]{2,1,0:T(8,128)(2,1)}, bf16[16,32,128]{2,1,0:T(8,128)(2,1)S(1)}, u32[]{:S(2)}, u32[]{:S(2)}) collective-permute-start(bf16[16,32,128]{2,1,0:T(8,128)(2,1)} %refs_6_.1), channel_id=1, source_target_pairs={{0,1},{1,0},{2,3},{3,2},{4,5},{5,4},{6,7},{7,6},{8,9},{9,8},{10,11... | collective-permute-start | bytes 393224 | tf_op jit(solution)/shard_map/ppermute | solution.py:388
  1.3 1.8 %copy-start.11 = (s32[2,4]{1,0:T(2,128)S(1)}, s32[2,4]{1,0:T(2,128)}, u32[]{:S(2)}) copy-start(s32[2,4]{1,0:T(2,128)} %refs_0_.3) | copy-start | bytes 100
  3.1 1.0 %copy-start = (bf16[16,32,512]{2,1,0:T(8,128)(2,1)S(1)}, bf16[16,32,512]{2,1,0:T(8,128)(2,1)}, u32[]{:S(2)}) copy-start(bf16[16,32,512]{2,1,0:T(8,128)(2,1)} %param.16) | copy-start | bytes 1572868
  4.2 0.9 %copy-start.2 = (bf16[512,256]{1,0:T(8,128)(2,1)S(1)}, bf16[512,256]{1,0:T(8,128)(2,1)}, u32[]{:S(2)}) copy-start(bf16[512,256]{1,0:T(8,128)(2,1)} %w2_ref.5) | copy-start | bytes 786436
  5.1 0.9 %copy-start.4 = (bf16[16,32,128]{2,1,0:T(8,128)(2,1)S(1)}, bf16[16,32,128]{2,1,0:T(8,128)(2,1)}, u32[]{:S(2)}) copy-start(bf16[16,32,128]{2,1,0:T(8,128)(2,1)} %refs_6_.1) | copy-start | bytes 393220
  6.0 0.9 %copy-start.8 = (s32[2,256,16,4]{1,3,2,0:T(4,128)S(1)}, s32[2,256,16,4]{1,3,2,0:T(4,128)}, u32[]{:S(2)}) copy-start(s32[2,256,16,4]{1,3,2,0:T(4,128)} %param.20) | copy-start | bytes 393220
  6.9 7.2 %copy-start.6 = (f32[4,32,128]{2,1,0:T(8,128)S(1)}, f32[4,32,128]{2,1,0:T(8,128)}, u32[]{:S(2)}) copy-start(f32[4,32,128]{2,1,0:T(8,128)} %refs_3_.3) | copy-start | bytes 196612
  6.9 7.2 %copy-start.7 = (f32[4,32,128]{2,1,0:T(8,128)S(1)}, f32[4,32,128]{2,1,0:T(8,128)}, u32[]{:S(2)}) copy-start(f32[4,32,128]{2,1,0:T(8,128)} %refs_4_.1) | copy-start | bytes 196612
  6.9 7.2 %copy-start.10 = (bf16[1,4,32,128]{3,2,1,0:T(8,128)(2,1)S(1)}, bf16[1,4,32,128]{3,2,1,0:T(8,128)(2,1)}, u32[]{:S(2)}) copy-start(bf16[1,4,32,128]{3,2,1,0:T(8,128)(2,1)} %param.15) | copy-start | bytes 98308
  11.0 7.3 %collective-permute-start.2 = (bf16[2,32,128]{2,1,0:T(8,128)(2,1)S(1)}, bf16[2,32,128]{2,1,0:T(8,128)(2,1)S(1)}, u32[]{:S(2)}, u32[]{:S(2)}) collective-permute-start(bf16[2,32,128]{2,1,0:T(8,128)(2,1)S(1)} %get-tuple-element.17), channel_id=1, source_target_pairs={{0,2},{1,3},{2,0},{3,1},{4,6},{5,7},{6,4},{7,5},{8,10},{9,11},{10,... | collective-permute-start | bytes 49160 | tf_op jit(solution)/shard_map/ppermute | solution.py:388
  13.9 5.0 %collective-permute-start.4 = (bf16[2,32,128]{2,1,0:T(8,128)(2,1)S(1)}, bf16[2,32,128]{2,1,0:T(8,128)(2,1)S(1)}, u32[]{:S(2)}, u32[]{:S(2)}) collective-permute-start(bf16[2,32,128]{2,1,0:T(8,128)(2,1)S(1)} %get-tuple-element.18), channel_id=1, source_target_pairs={{0,3},{1,2},{2,1},{3,0},{4,7},{5,6},{6,5},{7,4},{8,11},{9,10},{10,... | collective-permute-start | bytes 49160 | tf_op jit(solution)/shard_map/ppermute | solution.py:388
  13.9 5.0 %collective-permute-start.3 = (bf16[2,32,128]{2,1,0:T(8,128)(2,1)S(1)}, bf16[2,32,128]{2,1,0:T(8,128)(2,1)S(1)}, u32[]{:S(2)}, u32[]{:S(2)}) collective-permute-start(bf16[2,32,128]{2,1,0:T(8,128)(2,1)S(1)} %get-tuple-element.18), channel_id=1, source_target_pairs={{0,1},{1,0},{2,3},{3,2},{4,5},{5,4},{6,7},{7,6},{8,9},{9,8},{10,11... | collective-permute-start | bytes 49160 | tf_op jit(solution)/shard_map/ppermute | solution.py:388
  14.1 16.8 %copy-start.5 = (bf16[16,32,128]{2,1,0:T(8,128)(2,1)S(1)}, bf16[16,32,128]{2,1,0:T(8,128)(2,1)}, u32[]{:S(2)}) copy-start(bf16[16,32,128]{2,1,0:T(8,128)(2,1)} %refs_6_.1) | copy-start | bytes 393220
  14.1 18.7 %copy-start.1 = (bf16[16,32,512]{2,1,0:T(8,128)(2,1)S(1)}, bf16[16,32,512]{2,1,0:T(8,128)(2,1)}, u32[]{:S(2)}) copy-start(bf16[16,32,512]{2,1,0:T(8,128)(2,1)} %param.16) | copy-start | bytes 1572868
  14.1 8.6 %collective-permute-start.10 = (bf16[16,32,128]{2,1,0:T(8,128)(2,1)S(1)}, bf16[16,32,128]{2,1,0:T(8,128)(2,1)S(1)}, u32[]{:S(2)}, u32[]{:S(2)}) collective-permute-start(bf16[16,32,128]{2,1,0:T(8,128)(2,1)S(1)} %shard_map.148), channel_id=1, source_target_pairs={{0,12},{4,8},{8,4},{12,0},{1,13},{5,9},{9,5},{13,1},{2,14},{6,10},... | collective-permute-start | bytes 393224 | tf_op jit(solution)/shard_map/ppermute | solution.py:388
  18.2 12.3 %collective-permute-start.9 = (bf16[16,32,128]{2,1,0:T(8,128)(2,1)S(1)}, bf16[16,32,128]{2,1,0:T(8,128)(2,1)S(1)}, u32[]{:S(2)}, u32[]{:S(2)}) collective-permute-start(bf16[16,32,128]{2,1,0:T(8,128)(2,1)S(1)} %shard_map.148), channel_id=1, source_target_pairs={{0,8},{4,12},{8,0},{12,4},{1,9},{5,13},{9,1},{13,5},{2,10},{6,14},... | collective-permute-start | bytes 393224 | tf_op jit(solution)/shard_map/ppermute | solution.py:388
  18.3 12.3 %collective-permute-start.8 = (bf16[16,32,128]{2,1,0:T(8,128)(2,1)S(1)}, bf16[16,32,128]{2,1,0:T(8,128)(2,1)S(1)}, u32[]{:S(2)}, u32[]{:S(2)}) collective-permute-start(bf16[16,32,128]{2,1,0:T(8,128)(2,1)S(1)} %shard_map.148), channel_id=1, source_target_pairs={{0,4},{4,0},{8,12},{12,8},{1,5},{5,1},{9,13},{13,9},{2,6},{6,2},{1... | collective-permute-start | bytes 393224 | tf_op jit(solution)/shard_map/ppermute | solution.py:388
  18.9 13.9 %copy-start.9 = (s32[2,256,16,4]{1,3,2,0:T(4,128)S(1)}, s32[2,256,16,4]{1,3,2,0:T(4,128)}, u32[]{:S(2)}) copy-start(s32[2,256,16,4]{1,3,2,0:T(4,128)} %param.20) | copy-start | bytes 393220
  18.9 11.7 %collective-permute-start.7 = (bf16[2,32,128]{2,1,0:T(8,128)(2,1)S(1)}, bf16[2,32,128]{2,1,0:T(8,128)(2,1)S(1)}, u32[]{:S(2)}, u32[]{:S(2)}) collective-permute-start(bf16[2,32,128]{2,1,0:T(8,128)(2,1)S(1)} %add_convert_fusion.1.refs_4_), channel_id=1, source_target_pairs={{0,12},{4,8},{8,4},{12,0},{1,13},{5,9},{9,5},{13,1},{2,14},{6,10},... | collective-permute-start | bytes 49160 | tf_op jit(solution)/shard_map/ppermute | solution.py:388
  22.7 8.2 %collective-permute-start.6 = (bf16[2,32,128]{2,1,0:T(8,128)(2,1)S(1)}, bf16[2,32,128]{2,1,0:T(8,128)(2,1)S(1)}, u32[]{:S(2)}, u32[]{:S(2)}) collective-permute-start(bf16[2,32,128]{2,1,0:T(8,128)(2,1)S(1)} %add_convert_fusion.1.refs_4_), channel_id=1, source_target_pairs={{0,8},{4,12},{8,0},{12,4},{1,9},{5,13},{9,1},{13,5},{2,10},{6,14},... | collective-permute-start | bytes 49160 | tf_op jit(solution)/shard_map/ppermute | solution.py:388
  22.7 8.2 %collective-permute-start.5 = (bf16[2,32,128]{2,1,0:T(8,128)(2,1)S(1)}, bf16[2,32,128]{2,1,0:T(8,128)(2,1)S(1)}, u32[]{:S(2)}, u32[]{:S(2)}) collective-permute-start(bf16[2,32,128]{2,1,0:T(8,128)(2,1)S(1)} %add_convert_fusion.1.refs_4_), channel_id=1, source_target_pairs={{0,4},{4,0},{8,12},{12,8},{1,5},{5,1},{9,13},{13,9},{2,6},{6,2},{1... | collective-permute-start | bytes 49160 | tf_op jit(solution)/shard_map/ppermute | solution.py:388
  31.6 1.2 %collective-permute-start.11 = (bf16[2,32,128]{2,1,0:T(8,128)(2,1)S(1)}, bf16[2,32,128]{2,1,0:T(8,128)(2,1)S(1)}, u32[]{:S(2)}, u32[]{:S(2)}) collective-permute-start(bf16[2,32,128]{2,1,0:T(8,128)(2,1)S(1)} %get-tuple-element.19.new_own.refs_7_), channel_id=1, source_target_pairs={{0,1},{1,0},{2,3},{3,2},{4,5},{5,4},{6,7},{7,6},{8,9},{9,8},{10,11... | collective-permute-start | bytes 49160 | tf_op jit(solution)/shard_map/ppermute | solution.py:388
  36.9 4.2 %collective-permute-start.12 = (bf16[6,32,128]{2,1,0:T(8,128)(2,1)S(1)}, bf16[6,32,128]{2,1,0:T(8,128)(2,1)S(1)}, u32[]{:S(2)}, u32[]{:S(2)}) collective-permute-start(bf16[6,32,128]{2,1,0:T(8,128)(2,1)S(1)} %get-tuple-element.24), channel_id=1, source_target_pairs={{0,2},{1,3},{2,0},{3,1},{4,6},{5,7},{6,4},{7,5},{8,10},{9,11},{10,... | collective-permute-start | bytes 147464 | tf_op jit(solution)/shard_map/ppermute | solution.py:388
  38.5 4.0 %collective-permute-start.14 = (bf16[6,32,128]{2,1,0:T(8,128)(2,1)S(1)}, bf16[6,32,128]{2,1,0:T(8,128)(2,1)S(1)}, u32[]{:S(2)}, u32[]{:S(2)}) collective-permute-start(bf16[6,32,128]{2,1,0:T(8,128)(2,1)S(1)} %get-tuple-element.25), channel_id=1, source_target_pairs={{0,3},{1,2},{2,1},{3,0},{4,7},{5,6},{6,5},{7,4},{8,11},{9,10},{10,... | collective-permute-start | bytes 147464 | tf_op jit(solution)/shard_map/ppermute | solution.py:388
  38.5 4.0 %collective-permute-start.13 = (bf16[6,32,128]{2,1,0:T(8,128)(2,1)S(1)}, bf16[6,32,128]{2,1,0:T(8,128)(2,1)S(1)}, u32[]{:S(2)}, u32[]{:S(2)}) collective-permute-start(bf16[6,32,128]{2,1,0:T(8,128)(2,1)S(1)} %get-tuple-element.25), channel_id=1, source_target_pairs={{0,1},{1,0},{2,3},{3,2},{4,5},{5,4},{6,7},{7,6},{8,9},{9,8},{10,11... | collective-permute-start | bytes 147464 | tf_op jit(solution)/shard_map/ppermute | solution.py:388
  42.5 8.2 %copy-start.12 = (s32[1,8,16,4]{2,3,1,0:T(4,128)S(1)}, s32[1,8,16,4]{2,3,1,0:T(4,128)}, u32[]{:S(2)}) copy-start(s32[1,8,16,4]{2,3,1,0:T(4,128)} %param.23) | copy-start | bytes 6148
  42.5 6.5 %collective-permute-start.17 = (bf16[6,32,128]{2,1,0:T(8,128)(2,1)S(1)}, bf16[6,32,128]{2,1,0:T(8,128)(2,1)S(1)}, u32[]{:S(2)}, u32[]{:S(2)}) collective-permute-start(bf16[6,32,128]{2,1,0:T(8,128)(2,1)S(1)} %add_convert_fusion.refs_11_), channel_id=1, source_target_pairs={{0,12},{4,8},{8,4},{12,0},{1,13},{5,9},{9,5},{13,1},{2,14},{6,10},... | collective-permute-start | bytes 147464 | tf_op jit(solution)/shard_map/ppermute | solution.py:388
  45.1 5.6 %collective-permute-start.16 = (bf16[6,32,128]{2,1,0:T(8,128)(2,1)S(1)}, bf16[6,32,128]{2,1,0:T(8,128)(2,1)S(1)}, u32[]{:S(2)}, u32[]{:S(2)}) collective-permute-start(bf16[6,32,128]{2,1,0:T(8,128)(2,1)S(1)} %add_convert_fusion.refs_11_), channel_id=1, source_target_pairs={{0,8},{4,12},{8,0},{12,4},{1,9},{5,13},{9,1},{13,5},{2,10},{6,14},... | collective-permute-start | bytes 147464 | tf_op jit(solution)/shard_map/ppermute | solution.py:388
  45.4 5.2 %collective-permute-start.15 = (bf16[6,32,128]{2,1,0:T(8,128)(2,1)S(1)}, bf16[6,32,128]{2,1,0:T(8,128)(2,1)S(1)}, u32[]{:S(2)}, u32[]{:S(2)}) collective-permute-start(bf16[6,32,128]{2,1,0:T(8,128)(2,1)S(1)} %add_convert_fusion.refs_11_), channel_id=1, source_target_pairs={{0,4},{4,0},{8,12},{12,8},{1,5},{5,1},{9,13},{13,9},{2,6},{6,2},{1... | collective-permute-start | bytes 147464 | tf_op jit(solution)/shard_map/ppermute | solution.py:388
  50.7 0.7 %copy-start.14 = (s32[1,4]{1,0:T(1,128)S(1)}, s32[1,4]{1,0:T(1,128)}, u32[]{:S(2)}) copy-start(s32[1,4]{1,0:T(1,128)} %refs_1_.3) | copy-start | bytes 52
  51.3 3.4 %copy-start.3 = (bf16[512,256]{1,0:T(8,128)(2,1)S(1)}, bf16[512,256]{1,0:T(8,128)(2,1)}, u32[]{:S(2)}) copy-start(bf16[512,256]{1,0:T(8,128)(2,1)} %w2_ref.5) | copy-start | bytes 786436
  53.5 1.2 %collective-permute-start.18 = (f32[8,512]{1,0:T(8,128)S(1)}, f32[8,512]{1,0:T(8,128)S(1)}, u32[]{:S(2)}, u32[]{:S(2)}) collective-permute-start(f32[8,512]{1,0:T(8,128)S(1)} %get-tuple-element.29.own_ref), channel_id=1, source_target_pairs={{0,1},{1,0},{2,3},{3,2},{4,5},{5,4},{6,7},{7,6},{8,9},{9,8},{10,11... | collective-permute-start | bytes 49160 | tf_op jit(solution)/shard_map/ppermute | solution.py:388

commit v2 on v1

v2 whole, which is shorter than its diff:
```python
import functools

import jax
import jax.numpy as jnp
from jax import lax
from jax.experimental import pallas as pl
from jax.experimental.pallas import tpu as pltpu
from jax.sharding import PartitionSpec as P

step_alpha = 0.5
step_beta = 1.0
sparse_penalty = 0.1
ridge_penalty = 0.05
share_owners = False
micros_default = 1.0
f32 = jnp.float32
bf16 = jnp.bfloat16
VMEM = pl.BlockSpec(memory_space=pltpu.VMEM)
HBM = pl.BlockSpec(memory_space=pltpu.HBM)
SMEM = pl.BlockSpec(memory_space=pltpu.SMEM)
nt_dims = (((1,), (1,)), ((), ()))


def kernel_call(body, out_shape, in_specs, scratch=(), out_specs=None, micros=micros_default, limit=32):
    return pl.pallas_call(
        body,
        out_shape=out_shape,
        in_specs=in_specs,
        out_specs=jax.tree.map(lambda _: VMEM, out_shape) if out_specs is None else out_specs,
        scratch_shapes=list(scratch),
        compiler_params=pltpu.CompilerParams(vmem_limit_bytes=limit * 1024 * 1024),
        cost_estimate=pl.CostEstimate(
            flops=int(micros * 1e9), bytes_accessed=int(micros * 1e6), transcendentals=0
        ),
    )


def sigmoid(v):
    return 1.0 / (1.0 + jnp.exp(-v))


def ftrl_update(linear, square, gradient, current):
    grown = square + gradient * gradient
    root = jnp.sqrt(grown)
    sigma_term = (root - jnp.sqrt(square)) / step_alpha
    linear_next = linear + gradient - sigma_term * current
    shrunk = linear_next - jnp.clip(linear_next, -sparse_penalty, sparse_penalty)
    weights = -shrunk / ((step_beta + root) / step_alpha + ridge_penalty)
    return linear_next, grown, weights


def fill_counts(counts_ref, ids, column, blocks, rows):
    picks, lanes = ids.shape
    tiles = rows // 16
    level = lax.broadcasted_iota(jnp.int32, (tiles, 16, lanes), 1) + 16 * lax.broadcasted_iota(
        jnp.int32, (tiles, 16, lanes), 0
    )
    level = level.astype(f32).astype(bf16)
    wide = [jnp.broadcast_to(ids[pick : pick + 1], (16, lanes)) for pick in range(picks)]
    times = []
    for pick in range(picks):
        total = jnp.ones((16, lanes), f32)
        for later in range(pick + 1, picks):
            total = total + jnp.where(wide[later] == wide[pick], 1.0, 0.0)
        times.append(total.astype(bf16)[None])
    zero = jnp.zeros((), bf16)
    for block in range(blocks):
        filled = None
        for pick in reversed(range(picks)):
            place = (wide[pick] - float(block * rows)).astype(bf16)[None]
            filled = jnp.where(level == place, times[pick], zero if filled is None else filled)
        counts_ref[block * rows : (block + 1) * rows, column : column + lanes] = filled.reshape(
            rows, lanes
        )


def tree_sum(parts):
    parts = list(parts)
    while len(parts) > 1:
        parts = [
            parts[i] + parts[i + 1] if i + 1 < len(parts) else parts[i]
            for i in range(0, len(parts), 2)
        ]
    return parts[0]


def step_body(table, counts, label_row, w1_own, w1_other, w2_ref, head_ref, slots):
    half = table.shape[0] // 2
    samples = counts.shape[1] // slots
    pooled = jnp.dot(table, counts, preferred_element_type=f32)

    def by_sample(low):
        stacked = jnp.concatenate(
            [
                pooled[low : low + half, slot * samples : (slot + 1) * samples]
                for slot in range(slots)
            ],
            axis=0,
        )
        return stacked.T.astype(bf16)

    first_own, first_other, second = w1_own[...], w1_other[...], w2_ref[...]
    pre_one = jnp.dot(by_sample(0), first_own, preferred_element_type=f32) + jnp.dot(
        by_sample(half), first_other, preferred_element_type=f32
    )
    sig_one = sigmoid(pre_one)
    hidden_one = (pre_one * sig_one).astype(bf16)
    pre_two = jnp.dot(hidden_one, second, preferred_element_type=f32)
    sig_two = sigmoid(pre_two)
    hidden_two = (pre_two * sig_two).astype(bf16).astype(f32)
    head = head_ref[...].astype(f32)
    logit = jnp.sum(hidden_two * head, axis=1, keepdims=True)
    label = jnp.broadcast_to(label_row, (128, samples)).T[:, 0:1]
    error = sigmoid(logit) - label
    grad_two = (error * head * (sig_two * (1.0 + pre_two * (1.0 - sig_two)))).astype(bf16)
    back = lax.dot_general(grad_two, second, nt_dims, preferred_element_type=f32)
    grad_one = (back * (sig_one * (1.0 + pre_one * (1.0 - sig_one)))).astype(bf16)

    def by_column(first):
        spread = lax.dot_general(first, grad_one, nt_dims, preferred_element_type=f32).astype(bf16)
        return jnp.concatenate(
            [spread[slot * half : (slot + 1) * half] for slot in range(slots)], axis=1
        )

    grad_input = jnp.concatenate([by_column(first_own), by_column(first_other)], axis=0)
    return lax.dot_general(grad_input, counts, nt_dims, preferred_element_type=f32)


def copies(pairs, sems):
    started = []
    for at, (source, target) in enumerate(pairs):
        copy = pltpu.make_async_copy(source, target, sems.at[at])
        copy.start()
        started.append(copy)
    return started


def lead_kernel(out_ref):
    out_ref[...] = jnp.zeros_like(out_ref)


def pick_blocks(slab_ref, blocks_ref, step, first):
    half, rows = slab_ref.shape[1:]
    tables = []
    for i in range(first, blocks_ref.shape[1]):
        chosen = jnp.broadcast_to(blocks_ref[step : step + 1, i : i + 1].astype(f32), (half, rows))
        chosen = chosen.astype(bf16)
        table = slab_ref[0]
        for block in range(1, slab_ref.shape[0]):
            table = jnp.where(chosen == jnp.asarray(block, bf16), slab_ref[block], table)
        tables.append(table)
    return jnp.concatenate(tables, axis=1)


def open_kernel(shared, lead_ref, ids_ref, labels_ref, linear_at, square_at, serve_at, pack_ref):
    steps, slots, picks, _ = ids_ref.shape
    owned, half, rows = linear_at.shape
    last = steps - 1
    pack_ref[0:owned] = linear_at[...].astype(bf16)
    pack_ref[owned : 2 * owned] = square_at[...].astype(bf16)
    pack_ref[2 * owned : 3 * owned] = serve_at[...]
    if shared:
        core = lax.axis_index("mp")
        lanes = pl.ds(pl.multiple_of(core * rows, rows), rows)
        label_rows = labels_ref[:, lanes]
        at = 3 * owned
        per = half // picks
        for part in range(slots // per):
            ids = jnp.concatenate(
                [ids_ref[last, part * per + i, :, lanes].astype(f32) for i in range(per)], axis=0
            )
            upper = jnp.floor(ids / rows)
            pack_ref[at + part] = upper.astype(bf16)
            pack_ref[at + slots // per + part] = (ids - upper * rows).astype(bf16)
        row = label_rows[last : last + 1]
        first = row.astype(bf16)
        rest = row - first.astype(f32)
        second = rest.astype(bf16)
        third = (rest - second.astype(f32)).astype(bf16)
        which = lax.broadcasted_iota(jnp.int32, (half, rows), 0)
        parts = [jnp.broadcast_to(p.astype(f32), (half, rows)) for p in (first, second, third)]
        pack_ref[at + 2 * (slots // per)] = jnp.where(
            which == 0, parts[0], jnp.where(which == 1, parts[1], parts[2])
        ).astype(bf16)


def first_step_kernel(
    samples,
    blocks_ref,
    ids_ref,
    labels_ref,
    slab_own,
    slab_other,
    w1_own,
    w1_other,
    w2_ref,
    head_ref,
    share_ref,
    rest_own,
    rest_other,
    counts_ref,
):
    active = blocks_ref.shape[1]
    half, rows = slab_other.shape[1:]
    slots = ids_ref.shape[1]
    fresh = active // 2
    core = lax.axis_index("mp")
    lanes = pl.ds(pl.multiple_of(core * samples, samples), samples)
    for slot in range(slots):
        ids = ids_ref[0, slot, :, lanes].astype(f32)
        fill_counts(counts_ref, ids, slot * samples, active, rows)
    tables = [pick_blocks(slab, blocks_ref, 0, 0) for slab in (slab_own, slab_other)]
    grad = step_body(
        jnp.concatenate(tables, axis=0),
        counts_ref[...],
        labels_ref[0:1, lanes],
        w1_own,
        w1_other,
        w2_ref,
        head_ref,
        slots,
    )
    for i in range(active):
        part = grad[:, i * rows : (i + 1) * rows].astype(bf16)
        if i < fresh:
            rest_own[i] = part[:half]
            rest_other[i] = part[half:]
        else:
            share_ref[i - fresh] = part[:half]
            share_ref[active - fresh + i - fresh] = part[half:]


def side_kernel(picks, samples, active, ids_ref, labels_ref, req_ref, *refs):
    packs = refs[:-3]
    counts_ref, labels_out, wanted_ref = refs[-3:]
    steps, slots = ids_ref.shape[:2]
    rows = counts_ref.shape[0] // active
    total = counts_ref.shape[1] // slots
    last = steps - 1
    core = lax.axis_index("mp")
    lanes = pl.ds(pl.multiple_of(core * samples, samples), samples)
    for slot in range(slots):
        fill_counts(counts_ref, ids_ref[last, slot, :, lanes].astype(f32), slot * total, active, rows)
    labels_out[0:1, 0:samples] = labels_ref[last : last + 1, lanes]
    for k, pack in enumerate(packs):
        half = pack.shape[1]
        per = half // picks
        at = pack.shape[0] - 1 - 2 * (slots // per)
        for part in range(slots // per):
            ids = pack[at + part].astype(f32) * rows + pack[at + slots // per + part].astype(f32)
            for i in range(per):
                fill_counts(
                    counts_ref,
                    ids[i * picks : (i + 1) * picks],
                    (part * per + i) * total + (k + 1) * samples,
                    active,
                    rows,
                )
        parts = pack[pack.shape[0] - 1].astype(f32)
        labels_out[0:1, (k + 1) * samples : (k + 2) * samples] = (
            parts[0:1] + parts[1:2] + parts[2:3]
        )
    requests = req_ref.shape[0]
    lanes_ids = jnp.concatenate([req_ref[i] for i in range(requests)], axis=1).astype(f32)
    fill_counts(wanted_ref, lanes_ids, 0, wanted_ref.shape[0] // rows, rows)


def state_kernel(owners, packs_count, *refs):
    blocks_ref, layout_ref, linear_ref, square_ref, serve_ref, slab_own = refs[:6]
    packs = refs[6 : 6 + packs_count]
    linear_out, square_out, weight_out, table_out, where_out, mine_out = refs[6 + packs_count :]
    active = blocks_ref.shape[1]
    owned, half, rows = linear_ref.shape
    fresh = active // 2
    touched = active + fresh
    me = lax.axis_index("dp")
    for k in range(owners):
        if packs_count == 1:
            table_out[k * owned : (k + 1) * owned] = packs[0][k, 2 * owned : 3 * owned]
        elif k == 0:
            table_out[pl.ds(me * owned, owned)] = serve_ref[...]
        else:
            table_out[pl.ds((me ^ k) * owned, owned)] = packs[k - 1][2 * owned : 3 * owned]
    for i in range(touched):
        if i < active - fresh:
            step, at = 0, fresh + i
        elif i < active:
            step, at = 0, i - (active - fresh)
        else:
            step, at = 1, i - fresh
        block = jnp.broadcast_to(blocks_ref[step : step + 1, at : at + 1], (8, rows))
        wide = jnp.broadcast_to(block[0:1], (half, rows))
        linear = jnp.zeros((half, rows), f32)
        square = jnp.zeros((half, rows), f32)
        weight = jnp.zeros((half, rows), f32)
        for k in range(owners):
            for place in range(owned):
                if packs_count == 1:
                    hit = (wide == k * owned + place) & (k != me)
                    old = packs[0][k, place].astype(f32), packs[0][k, owned + place].astype(f32)
                else:
                    hit = wide == (me ^ k) * owned + place
                    if k == 0:
                        old = linear_ref[place], square_ref[place]
                    else:
                        old = (
                            packs[k - 1][place].astype(f32),
                            packs[k - 1][owned + place].astype(f32),
                        )
                linear = jnp.where(hit, old[0], linear)
                square = jnp.where(hit, old[1], square)
                here = k * owned + place
                weight = jnp.where(wide == here, slab_own[here].astype(f32), weight)
        if packs_count == 1:
            for place in range(owned):
                hit = wide == me * owned + place
                linear = jnp.where(hit, linear_ref[place], linear)
                square = jnp.where(hit, square_ref[place], square)
        linear_out[i], square_out[i], weight_out[i] = linear, square, weight
        owner = block // owned
        place = block % owned
        turn = (owner + place) % owners
        home = jnp.zeros_like(block)
        for q in range(owners):
            home = jnp.where(turn == q, layout_ref[0:1, q : q + 1], home)
        where_out[i] = home * owned + place
        mine_out[i] = jnp.where(owner == me, place, -1)


def share_update(linear_ref, square_ref, weight_ref, sums, count, low):
    parts = []
    for i in range(count):
        gradient = tree_sum([part[low + i].astype(f32) for part in sums])
        parts.append(ftrl_update(linear_ref[i], square_ref[i], gradient, weight_ref[i]))
    return parts


def second_step_kernel(slots, sums_count, blocks_ref, counts_ref, labels_ref, *refs):
    sums = refs[:sums_count]
    linear_own, square_own, weight_own, other_state, slab_own, slab_other = refs[sums_count:][:6]
    rest_own, rest_other, w1_own, w1_other, w2_ref, head_ref = refs[sums_count + 6 :][:6]
    out_own, out_other, new_out, linear_out, square_out = refs[sums_count + 12 :]
    active = blocks_ref.shape[1]
    half, rows = slab_own.shape[1:]
    fresh = active // 2
    shared = active - fresh
    last = blocks_ref.shape[0] - 1
    own = share_update(linear_own, square_own, weight_own, sums, shared, 0)
    other = share_update(
        other_state.at[0:shared],
        other_state.at[shared : 2 * shared],
        other_state.at[2 * shared : 3 * shared],
        sums,
        shared,
        shared,
    )
    for i in range(shared):
        linear_out[i], square_out[i] = own[i][:2]
        new_out[i] = own[i][2].astype(bf16).astype(f32)

    def table(updated, slab):
        return jnp.concatenate(
            [part[2].astype(bf16) for part in updated]
            + [pick_blocks(slab, blocks_ref, last, shared)],
            axis=1,
        )

    grad = step_body(
        jnp.concatenate([table(own, slab_own), table(other, slab_other)], axis=0),
        counts_ref[...],
        labels_ref[0:1],
        w1_own,
        w1_other,
        w2_ref,
        head_ref,
        slots,
    )
    for i in range(fresh):
        out_own[shared + i] = rest_own[i]
        out_other[shared + i] = rest_other[i]
    for i in range(active):
        part = grad[:, i * rows : (i + 1) * rows].astype(bf16)
        at = i if i < shared else fresh + i
        out_own[at] = part[:half]
        out_other[at] = part[half:]


def finish_kernel(sums_count, *refs):
    linear_old, square_old, weight_old, table_ref, where_ref, mine_ref = refs[:6]
    new_ref, linear_mid, square_mid, counts_ref, w1_own = refs[6:11]
    linear_in, square_in, serve_in = refs[11:14]
    sums = refs[14 : 14 + sums_count]
    linear_hbm, square_hbm, serve_hbm, partial_out = refs[14 + sums_count :][:4]
    linear_at, square_at, serve_at, sems = refs[14 + sums_count + 4 :]
    touched, half, rows = linear_old.shape
    owned = linear_in.shape[0]
    shared = new_ref.shape[0]
    positions = table_ref.shape[0]
    me = lax.axis_index("dp")
    weights, linears, squares = [], [], []
    for i in range(touched):
        gradient = tree_sum([part[i].astype(f32) for part in sums])
        if i < shared:
            old = linear_mid[i], square_mid[i], new_ref[i]
        else:
            old = linear_old[i], square_old[i], weight_old[i]
        linear, square, weight = ftrl_update(old[0], old[1], gradient, old[2])
        linears.append(linear)
        squares.append(square)
        weights.append(weight)

    def wide(ref, i):
        return jnp.broadcast_to(ref[i][0:1], (half, rows))

    home = [wide(mine_ref, i) for i in range(touched)]
    goal = [wide(where_ref, i) for i in range(touched)]
    for place in range(owned):
        linear, square = linear_in[place], square_in[place]
        serve = serve_in[place].astype(f32)
        for i in range(touched):
            hit = home[i] == place
            linear = jnp.where(hit, linears[i], linear)
            square = jnp.where(hit, squares[i], square)
            serve = jnp.where(goal[i] == me * owned + place, weights[i], serve)
        linear_at[place] = linear
        square_at[place] = square
        serve_at[place] = serve.astype(bf16)
    started = copies(
        [(linear_at, linear_hbm), (square_at, square_hbm), (serve_at, serve_hbm)], sems
    )
    tables = []
    for position in range(positions):
        table = table_ref[position].astype(f32)
        for i in range(touched):
            table = jnp.where(goal[i] == position, weights[i], table)
        tables.append(table.astype(bf16))
    pooled = jnp.dot(jnp.concatenate(tables, axis=1), counts_ref[...], preferred_element_type=f32)
    units = w1_own.shape[1]
    slots = w1_own.shape[0] // half
    requests = counts_ref.shape[1] // slots
    stacked = jnp.concatenate([pooled] * slots, axis=0)
    wanted = lax.broadcasted_iota(jnp.int32, stacked.shape, 0) // half
    present = lax.broadcasted_iota(jnp.int32, stacked.shape, 1) % slots
    stacked = jnp.where(wanted == present, stacked, 0.0)
    product = jnp.dot(stacked.T.astype(bf16), w1_own[...], preferred_element_type=f32)
    partial_out[...] = jnp.sum(product.reshape(requests, slots, units), axis=1)
    for copy in started:
        copy.wait()


def score_kernel(own_ref, other_ref, w2_ref, head_ref, out_ref):
    pre_one = own_ref[...] + other_ref[...]
    hidden_one = (pre_one * sigmoid(pre_one)).astype(bf16)
    pre_two = jnp.dot(hidden_one, w2_ref[...], preferred_element_type=f32)
    hidden_two = (pre_two * sigmoid(pre_two)).astype(bf16).astype(f32)
    logit = jnp.sum(hidden_two * head_ref[...].astype(f32), axis=1, keepdims=True)
    requests = logit.shape[0]
    out_ref[...] = jnp.broadcast_to(logit, (requests, 128)).T[0:1, :requests]


def swap(value, axes, sizes, bits):
    shape = tuple(sizes[a] for a in axes)
    count = 1
    for size in shape:
        count *= size
    pairs = []
    for index in range(count):
        rest, coords = index, []
        for size in reversed(shape):
            coords.append(rest % size)
            rest //= size
        coords = coords[::-1]
        target = 0
        for coord, bit, size in zip(coords, bits, shape):
            target = target * size + (coord ^ bit)
        pairs.append((index, target))
    return lax.ppermute(value, axes, pairs)


def add(parts):
    return tree_sum([p.astype(f32) for p in parts]).astype(bf16)


def reduce_rest(parts, sizes, first_bit):
    replicas, owners = sizes["replica"], sizes["dp"]
    bit = 2
    while bit < replicas:
        total = add(parts)
        parts = [total, swap(total, ("replica",), sizes, (bit,))]
        bit *= 2
    bit = first_bit
    while bit < owners:
        total = add(parts)
        steps = [k * bit for k in range(1, 4) if k * bit < owners]
        parts = [total] + [swap(total, ("dp",), sizes, (k,)) for k in steps]
        bit *= 4
    return parts


def exchange_whole(both, sizes):
    count = both.shape[0] // 2

    def turned(value):
        return jnp.concatenate([value[count:], value[:count]], axis=0)

    parts = [both]
    if sizes["replica"] > 1:
        parts.append(swap(both, ("replica", "mp"), sizes, (1, 0)))
    parts.append(turned(swap(both, ("replica", "mp"), sizes, (0, 1))))
    if sizes["replica"] > 1:
        parts.append(turned(swap(both, ("replica", "mp"), sizes, (1, 1))))
    return parts


def reduce_halves(own, other, sizes, first_bit):
    parts = [own]
    if sizes["replica"] > 1:
        parts.append(swap(own, ("replica", "mp"), sizes, (1, 0)))
    parts.append(swap(other, ("replica", "mp"), sizes, (0, 1)))
    if sizes["replica"] > 1:
        parts.append(swap(other, ("replica", "mp"), sizes, (1, 1)))
    return reduce_rest(parts, sizes, first_bit)


def local(
    sizes,
    hot_slab,
    linear_state,
    square_state,
    serve_table,
    first_weight,
    second_weight,
    out_weight,
    step_blocks,
    feature_ids,
    click_labels,
    serve_layout,
    request_ids,
):
    owners = sizes["dp"]
    owned, half, rows = linear_state.shape
    steps, active = step_blocks.shape
    fresh = active // 2
    kept = active - fresh
    touched = active + fresh
    samples = feature_ids.shape[1] // sizes["mp"]
    slots, picks = feature_ids.shape[2:]
    units = first_weight.shape[2]
    ids = jnp.transpose(feature_ids, (0, 2, 3, 1))
    req = jnp.transpose(request_ids[0], (0, 2, 1))
    requests = req.shape[0]
    positions = owners * owned
    w1_own = first_weight.reshape(-1, units)
    w1_other = swap(w1_own, ("mp",), sizes, (1,))
    slab_other = swap(hot_slab, ("mp",), sizes, (1,))
    head = out_weight.reshape(1, -1)
    serve_own = serve_table[0]
    direct = owners == 4
    shared = share_owners and direct and samples == rows
    members = owners if shared else 1

    def struct(*shape, dtype=bf16):
        return jax.ShapeDtypeStruct(shape, dtype)

    extra = 2 * (slots * picks // half) + 1 if shared else 0
    lead = kernel_call(lead_kernel, struct(8, 128, dtype=f32), [], micros=20.0)()
    pack = kernel_call(
        functools.partial(open_kernel, shared),
        struct(3 * owned + extra, half, rows),
        [VMEM] * 6,
    )(lead, ids, click_labels, linear_state, square_state, serve_own)
    if direct:
        packs = [swap(pack, ("dp",), sizes, (k,)) for k in range(1, owners)]
    else:
        packs = [lax.all_gather(pack, "dp", axis=0, tiled=False)]

    share, rest_own, rest_other = kernel_call(
        functools.partial(first_step_kernel, samples),
        (struct(2 * kept, half, rows), struct(fresh, half, rows), struct(fresh, half, rows)),
        [VMEM] * 9,
        [pltpu.VMEM((active * rows, slots * samples), bf16)],
    )(
        step_blocks,
        ids,
        click_labels,
        hot_slab,
        slab_other,
        w1_own,
        w1_other,
        second_weight,
        head,
    )
    parts = exchange_whole(share, sizes)
    late_ids, late_labels = lax.optimization_barrier((parts[2], ids, click_labels))[1:]
    counts, labels, wanted = kernel_call(
        functools.partial(side_kernel, picks, samples, active),
        (
            struct(active * rows, slots * members * samples),
            struct(1, members * samples, dtype=f32),
            struct(positions * rows, requests * slots),
        ),
        [VMEM] * (3 + (len(packs) if shared else 0)),
    )(late_ids, late_labels, req, *(packs if shared else []))

    packs = lax.optimization_barrier((share, *packs))[1:]
    linear_old, square_old, weight_old, table, where, mine = kernel_call(
        functools.partial(state_kernel, owners, len(packs)),
        (
            struct(touched, half, rows, dtype=f32),
            struct(touched, half, rows, dtype=f32),
            struct(touched, half, rows, dtype=f32),
            struct(positions, half, rows),
            struct(touched, 8, rows, dtype=jnp.int32),
            struct(touched, 8, rows, dtype=jnp.int32),
        ),
        [VMEM] * (6 + len(packs)),
        micros=1.0,
    )(step_blocks, serve_layout, linear_state, square_state, serve_own, hot_slab, *packs)
    tied = lax.optimization_barrier((counts, linear_old, square_old, weight_old, *parts))
    counts, linear_old, square_old, weight_old = tied[:4]
    first_sum = add(tied[4:])
    sums = reduce_rest([first_sum], sizes, 1)
    other_state = swap(
        jnp.concatenate([linear_old[:kept], square_old[:kept], weight_old[:kept]], axis=0),
        ("mp",),
        sizes,
        (1,),
    )
    grad_own, grad_other, new_own, linear_mid, square_mid = kernel_call(
        functools.partial(second_step_kernel, slots, len(sums)),
        (
            struct(touched, half, rows),
            struct(touched, half, rows),
            struct(kept, half, rows, dtype=f32),
            struct(kept, half, rows, dtype=f32),
            struct(kept, half, rows, dtype=f32),
        ),
        [VMEM] * (3 + len(sums) + 12),
    )(
        step_blocks,
        counts,
        labels,
        *sums,
        linear_old,
        square_old,
        weight_old,
        other_state,
        hot_slab,
        slab_other,
        rest_own,
        rest_other,
        w1_own,
        w1_other,
        second_weight,
        head,
    )
    sums = reduce_halves(grad_own, grad_other, sizes, members)
    linear_out, square_out, serve_out, partial = kernel_call(
        functools.partial(finish_kernel, len(sums)),
        (
            struct(*linear_state.shape, dtype=f32),
            struct(*square_state.shape, dtype=f32),
            struct(*serve_own.shape),
            struct(requests, units, dtype=f32),
        ),
        [VMEM] * (14 + len(sums)),
        [
            pltpu.VMEM(linear_state.shape, f32),
            pltpu.VMEM(square_state.shape, f32),
            pltpu.VMEM(serve_own.shape, bf16),
            pltpu.SemaphoreType.DMA((3,)),
        ],
        (HBM, HBM, HBM, VMEM),
    )(
        linear_old,
        square_old,
        weight_old,
        table,
        where,
        mine,
        new_own,
        linear_mid,
        square_mid,
        wanted,
        w1_own,
        linear_state,
        square_state,
        serve_own,
        *sums,
    )
    partial_other = swap(partial, ("mp",), sizes, (1,))
    scores = kernel_call(score_kernel, struct(1, requests, dtype=f32), [VMEM] * 4)(
        partial, partial_other, second_weight, head
    )
    return linear_out, square_out, serve_out[None], scores


def solution(mesh):
    sizes = dict(mesh.shape)
    placed = (
        P(None, "mp", None),
        P("dp", "mp", None),
        P("dp", "mp", None),
        P("replica", "dp", "mp", None),
        P(None, "mp", None),
        P(),
        P(),
        P("groups", None),
        P(None, ("groups", "dp", "replica"), None, None),
        P(None, ("groups", "dp", "replica")),
        P("replica", None),
        P("replica", ("groups", "dp"), None, None),
    )
    return jax.shard_map(
        functools.partial(local, sizes),
        mesh=mesh,
        in_specs=placed,
        out_specs=(
            P(("groups", "dp"), "mp", None),
            P(("groups", "dp"), "mp", None),
            P(("groups", "replica"), "dp", "mp", None),
            P("replica", ("groups", "dp")),
        ),
        check_vma=False,
    )
```

time: 55.9 us -> 43.8 us (0.78)
  starting transfers between devices: 24.9 us -> 19.2 us
  local copies, waits for them, and re-layouts: 4.53 us -> 0.83 us
  Pallas kernels: 11.2 us -> 9.35 us
  other arithmetic: 0.69 us -> 0.08 us
    ppermute x19, starting transfers between devices: 24.9 us -> 19.2 us  [swap(): return lax.ppermute(value, axes, pairs)]
    unnamed x32 -> x24, local copies, waits for them, and re-layouts: 4.53 us -> 0.8 us
    pallas_call x6 -> x8, Pallas kernels: 11.2 us -> 9.35 us  [the longest x1 3.31 us: local(): kernel_call(functools.partial(first_step_kernel, samples), (struct(2 * ke...]
    pallas_call x1 -> x0, other arithmetic: 0.64 us -> none  [local(): kernel_call(score_kernel, jax.ShapeDtypeStruct((requests, 1), f32), [VMEM...]
  transfers between devices with their start and end apart: 19 -> 19, of which waited for: 9 -> 8; matrix products, arithmetic and copies ran while one was open for 0% -> 0% of each run, Pallas kernels for 0% -> 11%
where the time goes in v2:
time: 43.8 us; the launch traced here: 43.6 us
  starting transfers between devices  19.2 us (44%)
  waiting for transfers between devices  13.3 us (30%)
  Pallas kernels  9.35 us (21%)
  between operations  0.88 us (2%)
  local copies, waits for them, and re-layouts  0.83 us (2%)
    ppermute x19, starting transfers between devices, swap(): return lax.ppermute(value, axes, pairs)  19.2 us
    ppermute x19, waiting for transfers between devices, swap(): return lax.ppermute(value, axes, pairs)  13.3 us
    pallas_call x1, Pallas kernels, local(): kernel_call(functools.partial(first_step_kernel, samples), (struct(2 * ke...  3.31 us
    pallas_call x1, Pallas kernels, local(): kernel_call(functools.partial(second_step_kernel, slots, len(sums)), (str...  2.36 us
    pallas_call x1, Pallas kernels, local(): kernel_call(functools.partial(finish_kernel, len(sums)), (struct(*linear_...  1.27 us
    pallas_call x1, Pallas kernels, local(): kernel_call(functools.partial(side_kernel, picks, samples, active), (stru...  1.17 us
  transfers between devices with their start and end apart: 19, of which 8 were waited for; matrix products, arithmetic and copies ran while one was open for 0% of the time, Pallas kernels for 11%

profile of v2, /device:TPU:0, one launch (start us, length us, event | category | flops | bytes accessed | tf_op | source)
XLA Modules:
  0.0 43.6 jit_solution(4278210795666840783)
XLA Ops:
  0.6 0.5 %collective-permute-start = (bf16[16,32,128]{2,1,0:T(8,128)(2,1)}, bf16[16,32,128]{2,1,0:T(8,128)(2,1)S(1)}, u32[]{:S(2)}, u32[]{:S(2)}) collective-permute-start(bf16[16,32,128]{2,1,0:T(8,128)(2,1)} %refs_8_.1), channel_id=1, source_target_pairs={{0,1},{1,0},{2,3},{3,2},{4,5},{5,4},{6,7},{7,6},{8,9},{9,8},{10,11... | collective-permute-start | bytes 393224 | tf_op jit(solution)/shard_map/ppermute | solution.py:477
  1.2 0.1 collective-permute-start.1
  1.3 0.0 copy-start.2
  1.3 0.0 copy-start.3
  1.3 0.7 %copy-done.4 = s32[2,256,16,4]{1,3,2,0:T(4,128)S(1)} copy-done((s32[2,256,16,4]{1,3,2,0:T(4,128)S(1)}, s32[2,256,16,4]{1,3,2,0:T(4,128)}, u32[]{:S(2)}) %copy-start.4) | copy-done | bytes 131096
  2.1 0.0 copy-done.6
  2.1 0.0 copy-start.10
  2.1 4.7 %collective-permute-start.5 = (bf16[12,32,128]{2,1,0:T(8,128)(2,1)S(1)}, bf16[12,32,128]{2,1,0:T(8,128)(2,1)S(1)}, u32[]{:S(2)}, u32[]{:S(2)}) collective-permute-start(bf16[12,32,128]{2,1,0:T(8,128)(2,1)S(1)} %shard_map.150), channel_id=1, source_target_pairs={{0,12},{4,8},{8,4},{12,0},{1,13},{5,9},{9,5},{13,1},{2,14},{6,10},... | collective-permute-start | bytes 294920 | tf_op jit(solution)/shard_map/ppermute | solution.py:477
  6.8 0.0 collective-permute-start.4
  6.8 0.6 %collective-permute-start.3 = (bf16[12,32,128]{2,1,0:T(8,128)(2,1)S(1)}, bf16[12,32,128]{2,1,0:T(8,128)(2,1)S(1)}, u32[]{:S(2)}, u32[]{:S(2)}) collective-permute-start(bf16[12,32,128]{2,1,0:T(8,128)(2,1)S(1)} %shard_map.150), channel_id=1, source_target_pairs={{0,4},{4,0},{8,12},{12,8},{1,5},{5,1},{9,13},{13,9},{2,6},{6,2},{1... | collective-permute-start | bytes 294920 | tf_op jit(solution)/shard_map/ppermute | solution.py:477
  7.4 0.0 collective-permute-done.slab_other.refs_9_
  7.4 0.0 collective-permute-done.1.w1_other.refs_13_
  7.5 3.3 %shard_map.147 = (bf16[4,32,128]{2,1,0:T(8,128)(2,1)S(1)}, bf16[2,32,128]{2,1,0:T(8,128)(2,1)S(1)}, bf16[2,32,128]{2,1,0:T(8,128)(2,1)S(1)}) custom-call(s32[2,4]{1,0:T(2,128)S(1)} %copy-done.3, s32[2,16,4,256]{3,2,1,0:T(4,128)S(1)} %bitcast.12, f32[2,256]{1,0:T(2,128)S(1)} %copy-done.9, bf16[16,32,128]{2,1,0:T(8,128)(2,1)S(1)} %copy-done.2, ...), custom_call_target="tpu_custom_call" | custom-call | flops 1000000000 | bytes 1000000 | tf_op jit(solution)/shard_map/pallas_call | solution.py:577
  10.8 0.0 copy-start.8
  10.8 1.1 %collective-permute-start.7 = (bf16[4,32,128]{2,1,0:T(8,128)(2,1)S(1)}, bf16[4,32,128]{2,1,0:T(8,128)(2,1)S(1)}, u32[]{:S(2)}, u32[]{:S(2)}) collective-permute-start(bf16[4,32,128]{2,1,0:T(8,128)(2,1)S(1)} %get-tuple-element.56), channel_id=1, source_target_pairs={{0,3},{1,2},{2,1},{3,0},{4,7},{5,6},{6,5},{7,4},{8,11},{9,10},{10,... | collective-permute-start | bytes 98312 | tf_op jit(solution)/shard_map/ppermute | solution.py:477
  11.9 0.7 %collective-permute-start.6 = (bf16[4,32,128]{2,1,0:T(8,128)(2,1)S(1)}, bf16[4,32,128]{2,1,0:T(8,128)(2,1)S(1)}, u32[]{:S(2)}, u32[]{:S(2)}) collective-permute-start(bf16[4,32,128]{2,1,0:T(8,128)(2,1)S(1)} %get-tuple-element.56), channel_id=1, source_target_pairs={{0,2},{1,3},{2,0},{3,1},{4,6},{5,7},{6,4},{7,5},{8,10},{9,11},{10,... | collective-permute-start | bytes 98312 | tf_op jit(solution)/shard_map/ppermute | solution.py:477
  12.6 0.0 collective-permute-done.5.refs_8_
  12.6 0.2 collective-permute-start.2
  12.8 2.9 %collective-permute-done.4.refs_7_ = bf16[12,32,128]{2,1,0:T(8,128)(2,1)S(1)} collective-permute-done((bf16[12,32,128]{2,1,0:T(8,128)(2,1)S(1)}, bf16[12,32,128]{2,1,0:T(8,128)(2,1)S(1)}, u32[]{:S(2)}, u32[]{:S(2)}) %collective-permute-start.4) | collective-permute-done | bytes 98336 | tf_op jit(solution)/shard_map/ppermute | solution.py:477
  15.7 0.0 collective-permute-done.3.refs_6_
  15.7 0.4 shard_map.151
  16.1 0.0 collective-permute-done.7
  16.1 0.0 collective-permute-done.2
  16.2 1.2 %shard_map.148 = (bf16[512,2048]{1,0:T(8,128)(2,1)S(1)}, f32[1,128]{1,0:T(1,128)S(1)}, bf16[2048,128]{1,0:T(8,128)(2,1)S(1)}) custom-call(s32[2,16,4,256]{3,2,1,0:T(4,128)S(1)} %bitcast.13, f32[2,256]{1,0:T(2,128)S(1)} %copy-done.9, s32[8,4,16]{2,1,0:T(4,128)S(1)} %bitcast.17), custom_call_target="tpu_custom_call" | custom-call | flops 1000000000 | bytes 1000000 | tf_op jit(solution)/shard_map/pallas_call | solution.py:595
  17.4 0.0 collective-permute-done.6
  17.4 0.1 collective-permute-start.11
  17.6 2.5 %collective-permute-start.10 = (bf16[4,32,128]{2,1,0:T(8,128)(2,1)S(1)}, bf16[4,32,128]{2,1,0:T(8,128)(2,1)S(1)}, u32[]{:S(2)}, u32[]{:S(2)}) collective-permute-start(bf16[4,32,128]{2,1,0:T(8,128)(2,1)S(1)} %add_convert_fusion.1.refs_0_), channel_id=1, source_target_pairs={{0,12},{4,8},{8,4},{12,0},{1,13},{5,9},{9,5},{13,1},{2,14},{6,10},... | collective-permute-start | bytes 98312 | tf_op jit(solution)/shard_map/ppermute | solution.py:477
  20.1 0.0 collective-permute-start.9
  20.1 1.9 %collective-permute-start.8 = (bf16[4,32,128]{2,1,0:T(8,128)(2,1)S(1)}, bf16[4,32,128]{2,1,0:T(8,128)(2,1)S(1)}, u32[]{:S(2)}, u32[]{:S(2)}) collective-permute-start(bf16[4,32,128]{2,1,0:T(8,128)(2,1)S(1)} %add_convert_fusion.1.refs_0_), channel_id=1, source_target_pairs={{0,4},{4,0},{8,12},{12,8},{1,5},{5,1},{9,13},{13,9},{2,6},{6,2},{1... | collective-permute-start | bytes 98312 | tf_op jit(solution)/shard_map/ppermute | solution.py:477
  22.0 1.5 %collective-permute-done.10.refs_3_ = bf16[4,32,128]{2,1,0:T(8,128)(2,1)S(1)} collective-permute-done((bf16[4,32,128]{2,1,0:T(8,128)(2,1)S(1)}, bf16[4,32,128]{2,1,0:T(8,128)(2,1)S(1)}, u32[]{:S(2)}, u32[]{:S(2)}) %collective-permute-start.10) | collective-permute-done | bytes 32800 | tf_op jit(solution)/shard_map/ppermute | solution.py:477
  23.6 1.4 %collective-permute-done.9.refs_2_ = bf16[4,32,128]{2,1,0:T(8,128)(2,1)S(1)} collective-permute-done((bf16[4,32,128]{2,1,0:T(8,128)(2,1)S(1)}, bf16[4,32,128]{2,1,0:T(8,128)(2,1)S(1)}, u32[]{:S(2)}, u32[]{:S(2)}) %collective-permute-start.9) | collective-permute-done | bytes 32800 | tf_op jit(solution)/shard_map/ppermute | solution.py:477
  24.9 2.4 %shard_map.152 = (bf16[6,32,128]{2,1,0:T(8,128)(2,1)S(1)}, bf16[6,32,128]{2,1,0:T(8,128)(2,1)S(1)}, f32[2,32,128]{2,1,0:T(8,128)S(1)}, f32[2,32,128]{2,1,0:T(8,128)S(1)}, f32[2,32,128]{2,1,0:T(8,128)S(1)}) custom-call(s32[2,4]{1,0:T(2,128)S(1)} %copy-done.3, bf16[512,2048]{1,0:T(8,128)(2,1)S(1)} %get-tuple-element.54.counts_ref, ...), custom_call_target="tpu_custom_call" | custom-call | flops 1000000000 | bytes 1000000 | tf_op jit(solution)/shard_map/pallas_call | solution.py:629
  27.3 1.5 %collective-permute-start.12 = (bf16[6,32,128]{2,1,0:T(8,128)(2,1)S(1)}, bf16[6,32,128]{2,1,0:T(8,128)(2,1)S(1)}, u32[]{:S(2)}, u32[]{:S(2)}) collective-permute-start(bf16[6,32,128]{2,1,0:T(8,128)(2,1)S(1)} %get-tuple-element.66), channel_id=1, source_target_pairs={{0,2},{1,3},{2,0},{3,1},{4,6},{5,7},{6,4},{7,5},{8,10},{9,11},{10,... | collective-permute-start | bytes 147464 | tf_op jit(solution)/shard_map/ppermute | solution.py:477
  28.8 0.0 collective-permute-start.14
  28.8 0.7 %collective-permute-start.13 = (bf16[6,32,128]{2,1,0:T(8,128)(2,1)S(1)}, bf16[6,32,128]{2,1,0:T(8,128)(2,1)S(1)}, u32[]{:S(2)}, u32[]{:S(2)}) collective-permute-start(bf16[6,32,128]{2,1,0:T(8,128)(2,1)S(1)} %get-tuple-element.67), channel_id=1, source_target_pairs={{0,1},{1,0},{2,3},{3,2},{4,5},{5,4},{6,7},{7,6},{8,9},{9,8},{10,11... | collective-permute-start | bytes 147464 | tf_op jit(solution)/shard_map/ppermute | solution.py:477
  29.5 1.9 %collective-permute-done.12 = bf16[6,32,128]{2,1,0:T(8,128)(2,1)S(1)} collective-permute-done((bf16[6,32,128]{2,1,0:T(8,128)(2,1)S(1)}, bf16[6,32,128]{2,1,0:T(8,128)(2,1)S(1)}, u32[]{:S(2)}, u32[]{:S(2)}) %collective-permute-start.12) | collective-permute-done | bytes 49184 | tf_op jit(solution)/shard_map/ppermute | solution.py:477
  31.4 1.1 %collective-permute-done.14 = bf16[6,32,128]{2,1,0:T(8,128)(2,1)S(1)} collective-permute-done((bf16[6,32,128]{2,1,0:T(8,128)(2,1)S(1)}, bf16[6,32,128]{2,1,0:T(8,128)(2,1)S(1)}, u32[]{:S(2)}, u32[]{:S(2)}) %collective-permute-start.14) | collective-permute-done | bytes 49184 | tf_op jit(solution)/shard_map/ppermute | solution.py:477
  32.5 0.0 collective-permute-done.13
  32.5 2.6 %collective-permute-start.17 = (bf16[6,32,128]{2,1,0:T(8,128)(2,1)S(1)}, bf16[6,32,128]{2,1,0:T(8,128)(2,1)S(1)}, u32[]{:S(2)}, u32[]{:S(2)}) collective-permute-start(bf16[6,32,128]{2,1,0:T(8,128)(2,1)S(1)} %add_convert_fusion.refs_14_), channel_id=1, source_target_pairs={{0,12},{4,8},{8,4},{12,0},{1,13},{5,9},{9,5},{13,1},{2,14},{6,10},... | collective-permute-start | bytes 147464 | tf_op jit(solution)/shard_map/ppermute | solution.py:477
  35.1 0.0 collective-permute-start.16
  35.1 1.9 %collective-permute-start.15 = (bf16[6,32,128]{2,1,0:T(8,128)(2,1)S(1)}, bf16[6,32,128]{2,1,0:T(8,128)(2,1)S(1)}, u32[]{:S(2)}, u32[]{:S(2)}) collective-permute-start(bf16[6,32,128]{2,1,0:T(8,128)(2,1)S(1)} %add_convert_fusion.refs_14_), channel_id=1, source_target_pairs={{0,4},{4,0},{8,12},{12,8},{1,5},{5,1},{9,13},{13,9},{2,6},{6,2},{1... | collective-permute-start | bytes 147464 | tf_op jit(solution)/shard_map/ppermute | solution.py:477
  37.0 1.7 %collective-permute-done.17.refs_17_ = bf16[6,32,128]{2,1,0:T(8,128)(2,1)S(1)} collective-permute-done((bf16[6,32,128]{2,1,0:T(8,128)(2,1)S(1)}, bf16[6,32,128]{2,1,0:T(8,128)(2,1)S(1)}, u32[]{:S(2)}, u32[]{:S(2)}) %collective-permute-start.17) | collective-permute-done | bytes 49184 | tf_op jit(solution)/shard_map/ppermute | solution.py:477
  38.7 1.6 %collective-permute-done.16.refs_16_ = bf16[6,32,128]{2,1,0:T(8,128)(2,1)S(1)} collective-permute-done((bf16[6,32,128]{2,1,0:T(8,128)(2,1)S(1)}, bf16[6,32,128]{2,1,0:T(8,128)(2,1)S(1)}, u32[]{:S(2)}, u32[]{:S(2)}) %collective-permute-start.16) | collective-permute-done | bytes 49184 | tf_op jit(solution)/shard_map/ppermute | solution.py:477
  40.3 0.0 collective-permute-done.15.refs_15_
  40.3 1.3 %shard_map.153 = (f32[4,32,128]{2,1,0:T(8,128)}, f32[4,32,128]{2,1,0:T(8,128)}, bf16[4,32,128]{2,1,0:T(8,128)(2,1)}, f32[8,512]{1,0:T(8,128)S(1)}) custom-call(f32[6,32,128]{2,1,0:T(8,128)S(1)} %get-tuple-element.48.refs_4_.refs_0_, f32[6,32,128]{2,1,0:T(8,128)S(1)} %get-tuple-element.49.refs_5_.refs_1_, ...), custom_call_target="tpu_custom_call" | custom-call | flops 1000000000 | bytes 1000000 | tf_op jit(solution)/shard_map/pallas_call | solution.py:658
  41.6 0.1 collective-permute-start.18
  41.6 1.2 %collective-permute-done.18.other_ref = f32[8,512]{1,0:T(8,128)S(1)} collective-permute-done((f32[8,512]{1,0:T(8,128)S(1)}, f32[8,512]{1,0:T(8,128)S(1)}, u32[]{:S(2)}, u32[]{:S(2)}) %collective-permute-start.18) | collective-permute-done | bytes 16416 | tf_op jit(solution)/shard_map/ppermute | solution.py:477
  42.8 0.8 %shard_map.154 = f32[1,8]{1,0:T(1,128)} custom-call(f32[8,512]{1,0:T(8,128)S(1)} %get-tuple-element.71.own_ref, f32[8,512]{1,0:T(8,128)S(1)} %collective-permute-done.18.other_ref, bf16[512,256]{1,0:T(8,128)(2,1)S(1)} %copy-done.1, bf16[1,256]{1,0:T(2,128)(2,1)S(1)} %reshape.15.head_ref.refs_15_), custom_call_target="tpu_custom_call" | custom-call | flops 1000000000 | bytes 1000000 | tf_op jit(solution)/shard_map/pallas_call | solution.py:692
  (32 shorter events, 0.2 us)
Async XLA Ops:
  0.6 6.8 %collective-permute-start = (bf16[16,32,128]{2,1,0:T(8,128)(2,1)}, bf16[16,32,128]{2,1,0:T(8,128)(2,1)S(1)}, u32[]{:S(2)}, u32[]{:S(2)}) collective-permute-start(bf16[16,32,128]{2,1,0:T(8,128)(2,1)} %refs_8_.1), channel_id=1, source_target_pairs={{0,1},{1,0},{2,3},{3,2},{4,5},{5,4},{6,7},{7,6},{8,9},{9,8},{10,11... | collective-permute-start | bytes 393224 | tf_op jit(solution)/shard_map/ppermute | solution.py:477
  1.2 0.9 %copy-start.4 = (s32[2,256,16,4]{1,3,2,0:T(4,128)S(1)}, s32[2,256,16,4]{1,3,2,0:T(4,128)}, u32[]{:S(2)}) copy-start(s32[2,256,16,4]{1,3,2,0:T(4,128)} %param.20) | copy-start | bytes 393220
  1.2 0.9 %copy-start.5 = (f32[4,32,128]{2,1,0:T(8,128)S(1)}, f32[4,32,128]{2,1,0:T(8,128)}, u32[]{:S(2)}) copy-start(f32[4,32,128]{2,1,0:T(8,128)} %refs_11_.1) | copy-start | bytes 196612
  1.2 0.9 %copy-start.6 = (f32[4,32,128]{2,1,0:T(8,128)S(1)}, f32[4,32,128]{2,1,0:T(8,128)}, u32[]{:S(2)}) copy-start(f32[4,32,128]{2,1,0:T(8,128)} %refs_12_.1) | copy-start | bytes 196612
  1.2 0.9 %copy-start.7 = (bf16[1,4,32,128]{3,2,1,0:T(8,128)(2,1)S(1)}, bf16[1,4,32,128]{3,2,1,0:T(8,128)(2,1)}, u32[]{:S(2)}) copy-start(bf16[1,4,32,128]{3,2,1,0:T(8,128)(2,1)} %param.15) | copy-start | bytes 98308
  1.2 0.9 %copy-start.9 = (f32[2,256]{1,0:T(2,128)S(1)}, f32[2,256]{1,0:T(2,128)}, u32[]{:S(2)}) copy-start(f32[2,256]{1,0:T(2,128)} %labels_ref.4) | copy-start | bytes 6148
  1.2 6.3 %collective-permute-start.1 = (bf16[512,512]{1,0:T(8,128)(2,1)}, bf16[512,512]{1,0:T(8,128)(2,1)S(1)}, u32[]{:S(2)}, u32[]{:S(2)}) collective-permute-start(bf16[512,512]{1,0:T(8,128)(2,1)} %bitcast.7), channel_id=1, source_target_pairs={{0,1},{1,0},{2,3},{3,2},{4,5},{5,4},{6,7},{7,6},{8,9},{9,8},{10,11... | collective-permute-start | bytes 1572872 | tf_op jit(solution)/shard_map/ppermute | solution.py:477
  1.3 6.1 %copy-start.11 = (bf16[256]{0:T(256)(128)(2,1)S(1)}, bf16[256]{0:T(256)(128)(2,1)}, u32[]{:S(2)}) copy-start(bf16[256]{0:T(256)(128)(2,1)} %param.18) | copy-start | bytes 1540
  1.3 6.2 %copy-start = (bf16[16,32,512]{2,1,0:T(8,128)(2,1)S(1)}, bf16[16,32,512]{2,1,0:T(8,128)(2,1)}, u32[]{:S(2)}) copy-start(bf16[16,32,512]{2,1,0:T(8,128)(2,1)} %param.16) | copy-start | bytes 1572868
  1.3 6.2 %copy-start.1 = (bf16[512,256]{1,0:T(8,128)(2,1)S(1)}, bf16[512,256]{1,0:T(8,128)(2,1)}, u32[]{:S(2)}) copy-start(bf16[512,256]{1,0:T(8,128)(2,1)} %w2_ref.3) | copy-start | bytes 786436
  1.3 6.2 %copy-start.2 = (bf16[16,32,128]{2,1,0:T(8,128)(2,1)S(1)}, bf16[16,32,128]{2,1,0:T(8,128)(2,1)}, u32[]{:S(2)}) copy-start(bf16[16,32,128]{2,1,0:T(8,128)(2,1)} %refs_8_.1) | copy-start | bytes 393220
  1.3 6.2 %copy-start.3 = (s32[2,4]{1,0:T(2,128)S(1)}, s32[2,4]{1,0:T(2,128)}, u32[]{:S(2)}) copy-start(s32[2,4]{1,0:T(2,128)} %blocks_ref.3) | copy-start | bytes 100
  2.1 13.6 %copy-start.10 = (s32[1,4]{1,0:T(1,128)S(1)}, s32[1,4]{1,0:T(1,128)}, u32[]{:S(2)}) copy-start(s32[1,4]{1,0:T(1,128)} %refs_1_.1) | copy-start | bytes 52
  2.1 10.5 %collective-permute-start.5 = (bf16[12,32,128]{2,1,0:T(8,128)(2,1)S(1)}, bf16[12,32,128]{2,1,0:T(8,128)(2,1)S(1)}, u32[]{:S(2)}, u32[]{:S(2)}) collective-permute-start(bf16[12,32,128]{2,1,0:T(8,128)(2,1)S(1)} %shard_map.150), channel_id=1, source_target_pairs={{0,12},{4,8},{8,4},{12,0},{1,13},{5,9},{9,5},{13,1},{2,14},{6,10},... | collective-permute-start | bytes 294920 | tf_op jit(solution)/shard_map/ppermute | solution.py:477
  6.8 8.9 %collective-permute-start.4 = (bf16[12,32,128]{2,1,0:T(8,128)(2,1)S(1)}, bf16[12,32,128]{2,1,0:T(8,128)(2,1)S(1)}, u32[]{:S(2)}, u32[]{:S(2)}) collective-permute-start(bf16[12,32,128]{2,1,0:T(8,128)(2,1)S(1)} %shard_map.150), channel_id=1, source_target_pairs={{0,8},{4,12},{8,0},{12,4},{1,9},{5,13},{9,1},{13,5},{2,10},{6,14},... | collective-permute-start | bytes 294920 | tf_op jit(solution)/shard_map/ppermute | solution.py:477
  6.8 8.9 %collective-permute-start.3 = (bf16[12,32,128]{2,1,0:T(8,128)(2,1)S(1)}, bf16[12,32,128]{2,1,0:T(8,128)(2,1)S(1)}, u32[]{:S(2)}, u32[]{:S(2)}) collective-permute-start(bf16[12,32,128]{2,1,0:T(8,128)(2,1)S(1)} %shard_map.150), channel_id=1, source_target_pairs={{0,4},{4,0},{8,12},{12,8},{1,5},{5,1},{9,13},{13,9},{2,6},{6,2},{1... | collective-permute-start | bytes 294920 | tf_op jit(solution)/shard_map/ppermute | solution.py:477
  10.8 5.4 %copy-start.8 = (s32[1,8,16,4]{2,3,1,0:T(4,128)S(1)}, s32[1,8,16,4]{2,3,1,0:T(4,128)}, u32[]{:S(2)}) copy-start(s32[1,8,16,4]{2,3,1,0:T(4,128)} %param.23) | copy-start | bytes 6148
  10.8 5.3 %collective-permute-start.7 = (bf16[4,32,128]{2,1,0:T(8,128)(2,1)S(1)}, bf16[4,32,128]{2,1,0:T(8,128)(2,1)S(1)}, u32[]{:S(2)}, u32[]{:S(2)}) collective-permute-start(bf16[4,32,128]{2,1,0:T(8,128)(2,1)S(1)} %get-tuple-element.56), channel_id=1, source_target_pairs={{0,3},{1,2},{2,1},{3,0},{4,7},{5,6},{6,5},{7,4},{8,11},{9,10},{10,... | collective-permute-start | bytes 98312 | tf_op jit(solution)/shard_map/ppermute | solution.py:477
  11.9 5.5 %collective-permute-start.6 = (bf16[4,32,128]{2,1,0:T(8,128)(2,1)S(1)}, bf16[4,32,128]{2,1,0:T(8,128)(2,1)S(1)}, u32[]{:S(2)}, u32[]{:S(2)}) collective-permute-start(bf16[4,32,128]{2,1,0:T(8,128)(2,1)S(1)} %get-tuple-element.56), channel_id=1, source_target_pairs={{0,2},{1,3},{2,0},{3,1},{4,6},{5,7},{6,4},{7,5},{8,10},{9,11},{10,... | collective-permute-start | bytes 98312 | tf_op jit(solution)/shard_map/ppermute | solution.py:477
  12.6 3.5 %collective-permute-start.2 = (bf16[4,32,128]{2,1,0:T(8,128)(2,1)S(1)}, bf16[4,32,128]{2,1,0:T(8,128)(2,1)S(1)}, u32[]{:S(2)}, u32[]{:S(2)}) collective-permute-start(bf16[4,32,128]{2,1,0:T(8,128)(2,1)S(1)} %get-tuple-element.56), channel_id=1, source_target_pairs={{0,1},{1,0},{2,3},{3,2},{4,5},{5,4},{6,7},{7,6},{8,9},{9,8},{10,11... | collective-permute-start | bytes 98312 | tf_op jit(solution)/shard_map/ppermute | solution.py:477
  17.4 7.5 %collective-permute-start.11 = (f32[6,32,128]{2,1,0:T(8,128)S(1)}, f32[6,32,128]{2,1,0:T(8,128)S(1)}, u32[]{:S(2)}, u32[]{:S(2)}) collective-permute-start(f32[6,32,128]{2,1,0:T(8,128)S(1)} %pad_maximum_fusion), channel_id=1, source_target_pairs={{0,1},{1,0},{2,3},{3,2},{4,5},{5,4},{6,7},{7,6},{8,9},{9,8},{10,11... | collective-permute-start | bytes 294920 | tf_op jit(solution)/shard_map/ppermute | solution.py:477
  17.6 6.0 %collective-permute-start.10 = (bf16[4,32,128]{2,1,0:T(8,128)(2,1)S(1)}, bf16[4,32,128]{2,1,0:T(8,128)(2,1)S(1)}, u32[]{:S(2)}, u32[]{:S(2)}) collective-permute-start(bf16[4,32,128]{2,1,0:T(8,128)(2,1)S(1)} %add_convert_fusion.1.refs_0_), channel_id=1, source_target_pairs={{0,12},{4,8},{8,4},{12,0},{1,13},{5,9},{9,5},{13,1},{2,14},{6,10},... | collective-permute-start | bytes 98312 | tf_op jit(solution)/shard_map/ppermute | solution.py:477
  20.1 4.8 %collective-permute-start.9 = (bf16[4,32,128]{2,1,0:T(8,128)(2,1)S(1)}, bf16[4,32,128]{2,1,0:T(8,128)(2,1)S(1)}, u32[]{:S(2)}, u32[]{:S(2)}) collective-permute-start(bf16[4,32,128]{2,1,0:T(8,128)(2,1)S(1)} %add_convert_fusion.1.refs_0_), channel_id=1, source_target_pairs={{0,8},{4,12},{8,0},{12,4},{1,9},{5,13},{9,1},{13,5},{2,10},{6,14},... | collective-permute-start | bytes 98312 | tf_op jit(solution)/shard_map/ppermute | solution.py:477
  20.1 4.8 %collective-permute-start.8 = (bf16[4,32,128]{2,1,0:T(8,128)(2,1)S(1)}, bf16[4,32,128]{2,1,0:T(8,128)(2,1)S(1)}, u32[]{:S(2)}, u32[]{:S(2)}) collective-permute-start(bf16[4,32,128]{2,1,0:T(8,128)(2,1)S(1)} %add_convert_fusion.1.refs_0_), channel_id=1, source_target_pairs={{0,4},{4,0},{8,12},{12,8},{1,5},{5,1},{9,13},{13,9},{2,6},{6,2},{1... | collective-permute-start | bytes 98312 | tf_op jit(solution)/shard_map/ppermute | solution.py:477
  27.3 4.2 %collective-permute-start.12 = (bf16[6,32,128]{2,1,0:T(8,128)(2,1)S(1)}, bf16[6,32,128]{2,1,0:T(8,128)(2,1)S(1)}, u32[]{:S(2)}, u32[]{:S(2)}) collective-permute-start(bf16[6,32,128]{2,1,0:T(8,128)(2,1)S(1)} %get-tuple-element.66), channel_id=1, source_target_pairs={{0,2},{1,3},{2,0},{3,1},{4,6},{5,7},{6,4},{7,5},{8,10},{9,11},{10,... | collective-permute-start | bytes 147464 | tf_op jit(solution)/shard_map/ppermute | solution.py:477
  28.8 3.7 %collective-permute-start.14 = (bf16[6,32,128]{2,1,0:T(8,128)(2,1)S(1)}, bf16[6,32,128]{2,1,0:T(8,128)(2,1)S(1)}, u32[]{:S(2)}, u32[]{:S(2)}) collective-permute-start(bf16[6,32,128]{2,1,0:T(8,128)(2,1)S(1)} %get-tuple-element.67), channel_id=1, source_target_pairs={{0,3},{1,2},{2,1},{3,0},{4,7},{5,6},{6,5},{7,4},{8,11},{9,10},{10,... | collective-permute-start | bytes 147464 | tf_op jit(solution)/shard_map/ppermute | solution.py:477
  28.8 3.7 %collective-permute-start.13 = (bf16[6,32,128]{2,1,0:T(8,128)(2,1)S(1)}, bf16[6,32,128]{2,1,0:T(8,128)(2,1)S(1)}, u32[]{:S(2)}, u32[]{:S(2)}) collective-permute-start(bf16[6,32,128]{2,1,0:T(8,128)(2,1)S(1)} %get-tuple-element.67), channel_id=1, source_target_pairs={{0,1},{1,0},{2,3},{3,2},{4,5},{5,4},{6,7},{7,6},{8,9},{9,8},{10,11... | collective-permute-start | bytes 147464 | tf_op jit(solution)/shard_map/ppermute | solution.py:477
  32.5 6.1 %collective-permute-start.17 = (bf16[6,32,128]{2,1,0:T(8,128)(2,1)S(1)}, bf16[6,32,128]{2,1,0:T(8,128)(2,1)S(1)}, u32[]{:S(2)}, u32[]{:S(2)}) collective-permute-start(bf16[6,32,128]{2,1,0:T(8,128)(2,1)S(1)} %add_convert_fusion.refs_14_), channel_id=1, source_target_pairs={{0,12},{4,8},{8,4},{12,0},{1,13},{5,9},{9,5},{13,1},{2,14},{6,10},... | collective-permute-start | bytes 147464 | tf_op jit(solution)/shard_map/ppermute | solution.py:477
  35.1 5.2 %collective-permute-start.16 = (bf16[6,32,128]{2,1,0:T(8,128)(2,1)S(1)}, bf16[6,32,128]{2,1,0:T(8,128)(2,1)S(1)}, u32[]{:S(2)}, u32[]{:S(2)}) collective-permute-start(bf16[6,32,128]{2,1,0:T(8,128)(2,1)S(1)} %add_convert_fusion.refs_14_), channel_id=1, source_target_pairs={{0,8},{4,12},{8,0},{12,4},{1,9},{5,13},{9,1},{13,5},{2,10},{6,14},... | collective-permute-start | bytes 147464 | tf_op jit(solution)/shard_map/ppermute | solution.py:477
  35.1 5.2 %collective-permute-start.15 = (bf16[6,32,128]{2,1,0:T(8,128)(2,1)S(1)}, bf16[6,32,128]{2,1,0:T(8,128)(2,1)S(1)}, u32[]{:S(2)}, u32[]{:S(2)}) collective-permute-start(bf16[6,32,128]{2,1,0:T(8,128)(2,1)S(1)} %add_convert_fusion.refs_14_), channel_id=1, source_target_pairs={{0,4},{4,0},{8,12},{12,8},{1,5},{5,1},{9,13},{13,9},{2,6},{6,2},{1... | collective-permute-start | bytes 147464 | tf_op jit(solution)/shard_map/ppermute | solution.py:477
  41.6 1.2 %collective-permute-start.18 = (f32[8,512]{1,0:T(8,128)S(1)}, f32[8,512]{1,0:T(8,128)S(1)}, u32[]{:S(2)}, u32[]{:S(2)}) collective-permute-start(f32[8,512]{1,0:T(8,128)S(1)} %get-tuple-element.71.own_ref), channel_id=1, source_target_pairs={{0,1},{1,0},{2,3},{3,2},{4,5},{5,4},{6,7},{7,6},{8,9},{9,8},{10,11... | collective-permute-start | bytes 49160 | tf_op jit(solution)/shard_map/ppermute | solution.py:477

commit v3 on v2

v3 whole, which is shorter than its diff:
```python
import functools

import jax
import jax.numpy as jnp
from jax import lax
from jax.experimental import pallas as pl
from jax.experimental.pallas import tpu as pltpu
from jax.sharding import PartitionSpec as P

step_alpha = 0.5
step_beta = 1.0
sparse_penalty = 0.1
ridge_penalty = 0.05
f32 = jnp.float32
bf16 = jnp.bfloat16
VMEM = pl.BlockSpec(memory_space=pltpu.VMEM)
HBM = pl.BlockSpec(memory_space=pltpu.HBM)
nt_dims = (((1,), (1,)), ((), ()))


def kernel_call(body, out_shape, in_specs, scratch=(), out_specs=None, micros=1.0, limit=32):
    return pl.pallas_call(
        body,
        out_shape=out_shape,
        in_specs=in_specs,
        out_specs=jax.tree.map(lambda _: VMEM, out_shape) if out_specs is None else out_specs,
        scratch_shapes=list(scratch),
        compiler_params=pltpu.CompilerParams(vmem_limit_bytes=limit * 1024 * 1024),
        cost_estimate=pl.CostEstimate(
            flops=int(micros * 1e9), bytes_accessed=int(micros * 1e6), transcendentals=0
        ),
    )


def sigmoid(v):
    return 0.5 * jnp.tanh(0.5 * v) + 0.5


def ftrl_update(linear, square, gradient, current):
    grown = square + gradient * gradient
    root = jnp.sqrt(grown)
    sigma_term = (root - jnp.sqrt(square)) / step_alpha
    linear_next = linear + gradient - sigma_term * current
    shrunk = linear_next - jnp.clip(linear_next, -sparse_penalty, sparse_penalty)
    weights = -shrunk / ((step_beta + root) / step_alpha + ridge_penalty)
    return linear_next, grown, weights


def fill_counts(counts_ref, ids, column, blocks, rows):
    picks, lanes = ids.shape
    tiles = rows // 16
    level = lax.broadcasted_iota(jnp.int32, (tiles, 16, lanes), 1) + 16 * lax.broadcasted_iota(
        jnp.int32, (tiles, 16, lanes), 0
    )
    level = level.astype(f32).astype(bf16)
    wide = [jnp.broadcast_to(ids[pick : pick + 1], (16, lanes)) for pick in range(picks)]
    times = []
    for pick in range(picks):
        total = jnp.ones((16, lanes), f32)
        for later in range(pick + 1, picks):
            total = total + jnp.where(wide[later] == wide[pick], 1.0, 0.0)
        times.append(total.astype(bf16)[None])
    zero = jnp.zeros((), bf16)
    for block in range(blocks):
        filled = None
        for pick in reversed(range(picks)):
            place = (wide[pick] - float(block * rows)).astype(bf16)[None]
            filled = jnp.where(level == place, times[pick], zero if filled is None else filled)
        counts_ref[block * rows : (block + 1) * rows, column : column + lanes] = filled.reshape(
            rows, lanes
        )


def tree_sum(parts):
    parts = list(parts)
    while len(parts) > 1:
        parts = [
            parts[i] + parts[i + 1] if i + 1 < len(parts) else parts[i]
            for i in range(0, len(parts), 2)
        ]
    return parts[0]


def copies(pairs, sems):
    started = []
    for at, (source, target) in enumerate(pairs):
        copy = pltpu.make_async_copy(source, target, sems.at[at])
        copy.start()
        started.append(copy)
    return started


def lead_kernel(out_ref):
    out_ref[...] = jnp.zeros_like(out_ref)


def pick_blocks(slab_ref, blocks_ref, step, first):
    half, rows = slab_ref.shape[1:]
    tables = []
    for i in range(first, blocks_ref.shape[1]):
        chosen = jnp.broadcast_to(blocks_ref[step : step + 1, i : i + 1].astype(f32), (half, rows))
        chosen = chosen.astype(bf16)
        table = slab_ref[0]
        for block in range(1, slab_ref.shape[0]):
            table = jnp.where(chosen == jnp.asarray(block, bf16), slab_ref[block], table)
        tables.append(table)
    return jnp.concatenate(tables, axis=1)


def lead_kernel(out_ref):
    out_ref[...] = jnp.zeros_like(out_ref)


def open_kernel(lead_ref, ids_ref, labels_ref, linear_ref, square_ref, serve_ref, out_ref, pack_ref):
    owned = linear_ref.shape[0]
    pack_ref[0:owned] = linear_ref[...].astype(bf16)
    pack_ref[owned : 2 * owned] = square_ref[...].astype(bf16)
    pack_ref[2 * owned : 3 * owned] = serve_ref[...]
    steps, slots, picks, _ = ids_ref.shape
    samples = out_ref.shape[1]
    core = lax.axis_index("mp")
    lanes = pl.ds(pl.multiple_of(core * samples, samples), samples)
    for step in range(steps):
        for slot in range(slots):
            low = (step * slots + slot) * picks
            out_ref[low : low + picks] = ids_ref[step, slot, :, lanes].astype(f32)
    low = steps * slots * picks
    out_ref[low:] = jnp.zeros((out_ref.shape[0] - low, samples), f32)
    out_ref[low : low + steps] = labels_ref[:, lanes]


def fill_step(counts_ref, note_ref, step, slots, picks, active, rows):
    samples = note_ref.shape[1]
    for slot in range(slots):
        low = (step * slots + slot) * picks
        fill_counts(counts_ref, note_ref[low : low + picks], slot * samples, active, rows)


def by_sample(pooled, slots):
    half = pooled.shape[0] // 2
    samples = pooled.shape[1] // slots
    out = []
    for low in (0, half):
        stacked = jnp.concatenate(
            [
                pooled[low : low + half, slot * samples : (slot + 1) * samples]
                for slot in range(slots)
            ],
            axis=0,
        )
        out.append(stacked.T.astype(bf16))
    return out


def network(inputs, label_rows, counts, w1_own, w1_other, w2_ref, head_ref, slots):
    half = w1_own.shape[0] // slots
    first_own, first_other, second = w1_own[...], w1_other[...], w2_ref[...]
    inputs_own = jnp.concatenate([part[0] for part in inputs], axis=0)
    inputs_other = jnp.concatenate([part[1] for part in inputs], axis=0)
    pre_one = jnp.dot(inputs_own, first_own, preferred_element_type=f32) + jnp.dot(
        inputs_other, first_other, preferred_element_type=f32
    )
    sig_one = sigmoid(pre_one)
    hidden_one = (pre_one * sig_one).astype(bf16)
    pre_two = jnp.dot(hidden_one, second, preferred_element_type=f32)
    sig_two = sigmoid(pre_two)
    hidden_two = (pre_two * sig_two).astype(bf16).astype(f32)
    head = head_ref[...].astype(f32)
    logit = jnp.sum(hidden_two * head, axis=1, keepdims=True)
    label = jnp.concatenate(
        [jnp.broadcast_to(row, (128, row.shape[1])).T[:, 0:1] for row in label_rows], axis=0
    )
    error = sigmoid(logit) - label
    grad_two = (error * head * (sig_two * (1.0 + pre_two * (1.0 - sig_two)))).astype(bf16)
    back = lax.dot_general(grad_two, second, nt_dims, preferred_element_type=f32)
    grad_one = (back * (sig_one * (1.0 + pre_one * (1.0 - sig_one)))).astype(bf16)
    spread = [
        lax.dot_general(first, grad_one, nt_dims, preferred_element_type=f32).astype(bf16)
        for first in (first_own, first_other)
    ]
    samples = spread[0].shape[1] // len(counts)
    total = None
    for group, group_counts in enumerate(counts):
        lanes = slice(group * samples, (group + 1) * samples)
        grad_input = jnp.concatenate(
            [
                jnp.concatenate(
                    [part[slot * half : (slot + 1) * half, lanes] for slot in range(slots)], axis=1
                )
                for part in spread
            ],
            axis=0,
        )
        grad = lax.dot_general(grad_input, group_counts, nt_dims, preferred_element_type=f32)
        grad = grad.astype(bf16).astype(f32)
        total = grad if total is None else total + grad
    return total


def first_step_kernel(slots, picks, groups, blocks_ref, *refs):
    notes = refs[:groups]
    slab_own, slab_other, w1_own, w1_other, w2_ref, head_ref = refs[groups : groups + 6]
    share_ref, rest_own = refs[groups + 6 : groups + 8]
    counts_refs = refs[groups + 8 :]
    active = blocks_ref.shape[1]
    half, rows = slab_other.shape[1:]
    fresh = active // 2
    kept = active - fresh
    labels = notes[0].shape[0] // 8 * 8 - 8
    table = jnp.concatenate(
        [pick_blocks(slab, blocks_ref, 0, 0) for slab in (slab_own, slab_other)], axis=0
    )
    inputs = []
    for note, counts_ref in zip(notes, counts_refs):
        fill_step(counts_ref, note, 0, slots, picks, active, rows)
        pooled = jnp.dot(table, counts_ref[...], preferred_element_type=f32)
        inputs.append(by_sample(pooled, slots))
    grad = network(
        inputs,
        [note[labels : labels + 1] for note in notes],
        [ref[...] for ref in counts_refs],
        w1_own,
        w1_other,
        w2_ref,
        head_ref,
        slots,
    )
    for i in range(active):
        part = grad[:, i * rows : (i + 1) * rows].astype(bf16)
        if i < fresh:
            rest_own[i] = part[:half]
            share_ref[2 * kept + i] = part[half:]
        else:
            share_ref[i - fresh] = part[:half]
            share_ref[kept + i - fresh] = part[half:]


def side_kernel(slots, picks, active, groups, rows, *refs):
    notes = refs[:groups]
    req_ref = refs[groups]
    counts_refs = refs[groups + 1 : 2 * groups + 1]
    wanted_ref = refs[2 * groups + 1]
    for note, counts_ref in zip(notes, counts_refs):
        fill_step(counts_ref, note, 1, slots, picks, active, rows)
    requests = req_ref.shape[0]
    lanes_ids = jnp.concatenate([req_ref[i] for i in range(requests)], axis=1).astype(f32)
    fill_counts(wanted_ref, lanes_ids, 0, wanted_ref.shape[0] // rows, rows)


def join_kernel(turned, *refs):
    *sums, out_ref = refs
    if turned:
        first, second, rest = sums
        half = (first.shape[0] - rest.shape[0]) // 2
        low = first[0:half].astype(f32) + second[half : 2 * half].astype(f32)
        high = first[half : 2 * half].astype(f32) + second[0:half].astype(f32)
        out_ref[0:half] = low.astype(bf16)
        out_ref[half : 2 * half] = high.astype(bf16)
        rest = rest[...].astype(f32) + second[2 * half :].astype(f32)
        out_ref[2 * half :] = rest.astype(bf16)
    else:
        out_ref[...] = tree_sum([part[...].astype(f32) for part in sums]).astype(bf16)


def tree_sum(parts):
    parts = list(parts)
    while len(parts) > 1:
        parts = [
            parts[i] + parts[i + 1] if i + 1 < len(parts) else parts[i]
            for i in range(0, len(parts), 2)
        ]
    return parts[0]


def old_state(block, me, owners, linear_ref, square_ref, slab_own, packs):
    owned, half, rows = linear_ref.shape
    linear = jnp.zeros((half, rows), f32)
    square = jnp.zeros((half, rows), f32)
    weight = jnp.zeros((half, rows), f32)
    gathered = len(packs) == 1
    for k in range(owners):
        for place in range(owned):
            here = k * owned + place
            weight = jnp.where(block == here, slab_own[here].astype(f32), weight)
            if gathered:
                hit = block == here
                old = packs[0][k, place].astype(f32), packs[0][k, owned + place].astype(f32)
            else:
                hit = block == (me ^ k) * owned + place
                if k == 0:
                    old = linear_ref[place], square_ref[place]
                else:
                    pack = packs[k - 1]
                    old = (
                        pack[place].astype(f32),
                        pack[owned + place].astype(f32),
                    )
            linear = jnp.where(hit, old[0], linear)
            square = jnp.where(hit, old[1], square)
    if gathered:
        for place in range(owned):
            hit = block == me * owned + place
            linear = jnp.where(hit, linear_ref[place], linear)
            square = jnp.where(hit, square_ref[place], square)
    return linear, square, weight


def state_kernel(owners, blocks_ref, layout_ref, linear_ref, square_ref, slab_own, *refs):
    packs = refs[:-6]
    linear_out, square_out, weight_out, where_out, mine_out, cross_out = refs[-6:]
    active = blocks_ref.shape[1]
    owned, half, rows = linear_ref.shape
    fresh = active // 2
    kept = active - fresh
    me = lax.axis_index("dp")
    for i in range(active + fresh):
        step, at = (1, i) if i < active else (0, i - active)
        block = jnp.broadcast_to(blocks_ref[step : step + 1, at : at + 1], (8, rows))
        wide = jnp.broadcast_to(block[0:1], (half, rows))
        old = old_state(wide, me, owners, linear_ref, square_ref, slab_own, packs)
        linear_out[i], square_out[i], weight_out[i] = old
        if i < kept:
            cross_out[i], cross_out[kept + i], cross_out[2 * kept + i] = old
        owner = block // owned
        place = block % owned
        turn = (owner + place) % owners
        home = jnp.zeros_like(block)
        for q in range(owners):
            home = jnp.where(turn == q, layout_ref[0:1, q : q + 1], home)
        where_out[i] = home * owned + place
        mine_out[i] = jnp.where(owner == me, place, -1)


def second_step_kernel(slots, picks, groups, steps, sums_count, blocks_ref, *refs):
    counts_refs = refs[:groups]
    notes = refs[groups : 2 * groups]
    sums = refs[2 * groups : 2 * groups + sums_count]
    refs = refs[2 * groups + sums_count :]
    linear_own, square_own, weight_own, cross, slab_own, slab_other = refs[:6]
    w1_own, w1_other, w2_ref, head_ref = refs[6:10]
    out_own, out_other, new_out, linear_out, square_out = refs[10:]
    active = blocks_ref.shape[1]
    half, rows = slab_own.shape[1:]
    fresh = active // 2
    kept = active - fresh
    labels = notes[0].shape[0] // 8 * 8 - 8 + 1

    new_own, new_other = [], []
    for i in range(kept):
        gradient = tree_sum([part[i].astype(f32) for part in sums])
        linear, square, weights = ftrl_update(linear_own[i], square_own[i], gradient, weight_own[i])
        linear_out[i] = linear
        square_out[i] = square
        new_own.append(weights.astype(bf16))
        new_out[i] = new_own[i]
        gradient = tree_sum([part[kept + i].astype(f32) for part in sums])
        weights = ftrl_update(cross[i], cross[kept + i], gradient, cross[2 * kept + i])[2]
        new_other.append(weights.astype(bf16))

    def table(new, slab):
        return jnp.concatenate(new + [pick_blocks(slab, blocks_ref, steps - 1, kept)], axis=1)

    full = jnp.concatenate([table(new_own, slab_own), table(new_other, slab_other)], axis=0)
    counts = [ref[...] for ref in counts_refs]
    inputs = [
        by_sample(jnp.dot(full, group, preferred_element_type=f32), slots) for group in counts
    ]
    grad = network(
        inputs,
        [note[labels : labels + 1] for note in notes],
        counts,
        w1_own,
        w1_other,
        w2_ref,
        head_ref,
        slots,
    )
    for i in range(active):
        part = grad[:, i * rows : (i + 1) * rows].astype(bf16)
        out_own[i] = part[:half]
        out_other[i] = part[half:]


def finish_kernel(owners, sums_count, early_count, *refs):
    linear_old, square_old, weight_old, where_ref, mine_ref = refs[:5]
    new_ref, linear_mid, square_mid, counts_ref, w1_own = refs[5:10]
    linear_in, square_in, serve_in = refs[10:13]
    sums = refs[13 : 13 + sums_count]
    early = refs[13 + sums_count : 13 + sums_count + early_count]
    packs = refs[13 + sums_count + early_count : -5]
    linear_at, square_at, serve_at, partial_out, table_at = refs[-5:]
    touched, _, rows = where_ref.shape
    owned, half, _ = linear_in.shape
    kept = new_ref.shape[0]
    active = sums[0].shape[0]
    positions = table_at.shape[0]
    me = lax.axis_index("dp")
    for k in range(owners):
        if len(packs) == 1:
            table_at[k * owned : (k + 1) * owned] = packs[0][k, 2 * owned : 3 * owned]
        elif k == 0:
            table_at[pl.ds(me * owned, owned)] = serve_in[...]
        else:
            table_at[pl.ds((me ^ k) * owned, owned)] = packs[k - 1][2 * owned : 3 * owned]
    weights, linears, squares = [], [], []
    for i in range(touched):
        parts = [p[i] for p in sums] if i < active else [p[2 * kept + i - active] for p in early]
        gradient = tree_sum([part.astype(f32) for part in parts])
        if i < kept:
            old = linear_mid[i], square_mid[i], new_ref[i].astype(f32)
        else:
            old = linear_old[i], square_old[i], weight_old[i]
        linear, square, weight = ftrl_update(old[0], old[1], gradient, old[2])
        linears.append(linear)
        squares.append(square)
        weights.append(weight)

    def wide(ref, i):
        return jnp.broadcast_to(ref[i][0:1], (half, rows))

    home = [wide(mine_ref, i) for i in range(touched)]
    goal = [wide(where_ref, i) for i in range(touched)]
    for place in range(owned):
        linear, square = linear_in[place], square_in[place]
        serve = serve_in[place].astype(f32)
        for i in range(touched):
            hit = home[i] == place
            linear = jnp.where(hit, linears[i], linear)
            square = jnp.where(hit, squares[i], square)
            serve = jnp.where(goal[i] == me * owned + place, weights[i], serve)
        linear_at[place] = linear
        square_at[place] = square
        serve_at[place] = serve.astype(bf16)
    tables = []
    for position in range(positions):
        table = table_at[position].astype(f32)
        for i in range(touched):
            table = jnp.where(goal[i] == position, weights[i], table)
        tables.append(table.astype(bf16))
    pooled = jnp.dot(jnp.concatenate(tables, axis=1), counts_ref[...], preferred_element_type=f32)
    units = w1_own.shape[1]
    slots = w1_own.shape[0] // half
    requests = counts_ref.shape[1] // slots
    stacked = jnp.concatenate([pooled] * slots, axis=0)
    wanted = lax.broadcasted_iota(jnp.int32, stacked.shape, 0) // half
    present = lax.broadcasted_iota(jnp.int32, stacked.shape, 1) % slots
    stacked = jnp.where(wanted == present, stacked, 0.0)
    product = jnp.dot(stacked.T.astype(bf16), w1_own[...], preferred_element_type=f32)
    partial_out[...] = jnp.sum(product.reshape(requests, slots, units), axis=1)


def write_kernel(*refs):
    count = len(refs) // 2
    for copy in copies(list(zip(refs[:count], refs[count : 2 * count])), refs[-1]):
        copy.wait()


def score_kernel(own_ref, other_ref, w2_ref, head_ref, out_ref):
    pre_one = own_ref[...] + other_ref[...]
    hidden_one = (pre_one * sigmoid(pre_one)).astype(bf16)
    pre_two = jnp.dot(hidden_one, w2_ref[...], preferred_element_type=f32)
    hidden_two = (pre_two * sigmoid(pre_two)).astype(bf16).astype(f32)
    logit = jnp.sum(hidden_two * head_ref[...].astype(f32), axis=1, keepdims=True)
    requests = logit.shape[0]
    out_ref[...] = jnp.broadcast_to(logit, (requests, 128)).T[0:1, :requests]


def swap(value, axes, sizes, bits):
    shape = tuple(sizes[a] for a in axes)
    count = 1
    for size in shape:
        count *= size
    pairs = []
    for index in range(count):
        rest, coords = index, []
        for size in reversed(shape):
            coords.append(rest % size)
            rest //= size
        coords = coords[::-1]
        target = 0
        for coord, bit, size in zip(coords, bits, shape):
            target = target * size + (coord ^ bit)
        pairs.append((index, target))
    return lax.ppermute(value, axes, pairs)


def join(parts, turned=False):
    return kernel_call(
        functools.partial(join_kernel, turned),
        jax.ShapeDtypeStruct(parts[0].shape, bf16),
        [VMEM] * len(parts),
    )(*parts)


def reduce_rest(total, sizes, groups):
    parts = [total]
    bit = groups
    while bit < sizes["replica"]:
        total = join(parts) if len(parts) > 1 else total
        parts = [total, swap(total, ("replica",), sizes, (bit,))]
        bit *= 2
    bit = 1
    while bit < sizes["dp"]:
        total = join(parts) if len(parts) > 1 else total
        steps = [k * bit for k in range(1, 4) if k * bit < sizes["dp"]]
        parts = [total] + [swap(total, ("dp",), sizes, (k,)) for k in steps]
        bit *= 4
    return parts


def local(
    sizes,
    hot_slab,
    linear_state,
    square_state,
    serve_table,
    first_weight,
    second_weight,
    out_weight,
    step_blocks,
    feature_ids,
    click_labels,
    serve_layout,
    request_ids,
):
    owners = sizes["dp"]
    owned, half, rows = linear_state.shape
    steps, active = step_blocks.shape
    fresh = active // 2
    kept = active - fresh
    touched = active + fresh
    samples = feature_ids.shape[1] // sizes["mp"]
    slots, picks = feature_ids.shape[2:]
    units = first_weight.shape[2]
    ids = jnp.transpose(feature_ids, (0, 2, 3, 1))
    req = jnp.transpose(request_ids[0], (0, 2, 1))
    requests = req.shape[0]
    positions = owners * owned
    groups = 2 if sizes["replica"] > 1 else 1
    direct = owners == 4

    def struct(*shape, dtype=bf16):
        return jax.ShapeDtypeStruct(shape, dtype)

    w1_own = first_weight.reshape(-1, units)
    w1_other = swap(w1_own, ("mp",), sizes, (1,))
    slab_other = swap(hot_slab, ("mp",), sizes, (1,))
    head = out_weight.reshape(1, -1)
    serve_own = serve_table[0]

    lead = kernel_call(lead_kernel, struct(8, 128, dtype=f32), [], micros=20.0)()
    note, pack = kernel_call(
        open_kernel,
        (struct(steps * slots * picks + 8, samples, dtype=f32), struct(3 * owned, half, rows)),
        [VMEM] * 6,
    )(lead, ids, click_labels, linear_state, square_state, serve_own)
    if direct:
        packs = [swap(pack, ("dp",), sizes, (k,)) for k in range(1, owners)]
    else:
        packs = [lax.all_gather(pack, "dp", axis=0, tiled=False)]
    notes = [note]
    if groups > 1:
        notes.append(swap(note, ("replica",), sizes, (1,)))

    counts_shape = struct(active * rows, slots * samples)
    share, rest_own = kernel_call(
        functools.partial(first_step_kernel, slots, picks, groups),
        (struct(2 * kept + fresh, half, rows), struct(fresh, half, rows)),
        [VMEM] * (7 + groups),
        [pltpu.VMEM(counts_shape.shape, bf16)] * groups,
    )(
        step_blocks,
        *notes,
        hot_slab,
        slab_other,
        w1_own,
        w1_other,
        second_weight,
        head,
    )
    share_turned = swap(share, ("mp",), sizes, (1,))
    late = lax.optimization_barrier((share, *packs))[1:]
    old_shape = struct(touched, half, rows, dtype=f32)
    index_shape = struct(touched, 8, rows, dtype=jnp.int32)
    linear_old, square_old, weight_old, where, mine, cross = kernel_call(
        functools.partial(state_kernel, owners),
        (old_shape, old_shape, old_shape, index_shape, index_shape)
        + (struct(3 * kept, half, rows, dtype=f32),),
        [VMEM] * (5 + len(packs)),
    )(step_blocks, serve_layout, linear_state, square_state, hot_slab, *late)
    cross, share_turned = lax.optimization_barrier((cross, share_turned))
    total = join([share, share_turned, rest_own], True)
    sums = early = reduce_rest(total, sizes, groups)
    cross = swap(cross, ("mp",), sizes, (1,))
    late = lax.optimization_barrier((total, *notes))[1:]
    *counts, wanted = kernel_call(
        functools.partial(side_kernel, slots, picks, active, groups, rows),
        (counts_shape,) * groups + (struct(positions * rows, requests * slots),),
        [VMEM] * (groups + 1),
    )(*late, req)
    shared = struct(kept, half, rows)
    state_shape = struct(kept, half, rows, dtype=f32)
    payload = struct(active, half, rows)
    grad_own, grad_other, new_own, linear_mid, square_mid = kernel_call(
        functools.partial(second_step_kernel, slots, picks, groups, steps, len(sums)),
        (payload, payload, shared, state_shape, state_shape),
        [VMEM] * (11 + 2 * groups + len(sums)),
    )(
        step_blocks,
        *counts,
        *notes,
        *sums,
        linear_old,
        square_old,
        weight_old,
        cross,
        hot_slab,
        slab_other,
        w1_own,
        w1_other,
        second_weight,
        head,
    )
    total = join([grad_own, swap(grad_other, ("mp",), sizes, (1,))])
    sums = reduce_rest(total, sizes, groups)
    results = (
        struct(*linear_state.shape, dtype=f32),
        struct(*square_state.shape, dtype=f32),
        struct(*serve_own.shape),
    )
    *results_at, partial = kernel_call(
        functools.partial(finish_kernel, owners, len(sums), len(early)),
        results + (struct(requests, units, dtype=f32),),
        [VMEM] * (13 + len(sums) + len(early) + len(packs)),
        [pltpu.VMEM((positions, half, rows), bf16)],
    )(
        linear_old,
        square_old,
        weight_old,
        where,
        mine,
        new_own,
        linear_mid,
        square_mid,
        wanted,
        w1_own,
        linear_state,
        square_state,
        serve_own,
        *sums,
        *early,
        *packs,
    )
    partial_other = swap(partial, ("mp",), sizes, (1,))
    linear_out, square_out, serve_out = kernel_call(
        write_kernel, results, [VMEM] * 3, [pltpu.SemaphoreType.DMA((3,))], (HBM, HBM, HBM)
    )(*results_at)
    scores = kernel_call(score_kernel, struct(1, requests, dtype=f32), [VMEM] * 4)(
        partial, partial_other, second_weight, head
    )
    return linear_out, square_out, serve_out[None], scores


def solution(mesh):
    sizes = dict(mesh.shape)
    placed = (
        P(None, "mp", None),
        P("dp", "mp", None),
        P("dp", "mp", None),
        P("replica", "dp", "mp", None),
        P(None, "mp", None),
        P(),
        P(),
        P("groups", None),
        P(None, ("groups", "dp", "replica"), None, None),
        P(None, ("groups", "dp", "replica")),
        P("replica", None),
        P("replica", ("groups", "dp"), None, None),
    )
    return jax.shard_map(
        functools.partial(local, sizes),
        mesh=mesh,
        in_specs=placed,
        out_specs=(
            P(("groups", "dp"), "mp", None),
            P(("groups", "dp"), "mp", None),
            P(("groups", "replica"), "dp", "mp", None),
            P("replica", ("groups", "dp")),
        ),
        check_vma=False,
    )
```

time: 43.8 us -> 40.7 us (0.929)
  waiting for transfers between devices: 13.3 us -> 8.19 us
  Pallas kernels: 9.35 us -> 13.6 us
  starting transfers between devices: 19.2 us -> 17.1 us
    ppermute x19 -> x16, waiting for transfers between devices: 13.3 us -> 8.19 us  [swap(): return lax.ppermute(value, axes, pairs)]
    pallas_call x6 -> x9, Pallas kernels: 8.52 us -> 12.8 us  [the longest x1 5.31 us: local(): kernel_call(functools.partial(first_step_kernel, slots, picks, groups), (...]
    ppermute x19 -> x16, starting transfers between devices: 19.2 us -> 17.1 us  [swap(): return lax.ppermute(value, axes, pairs)]
  transfers between devices with their start and end apart: 19 -> 16, of which waited for: 8 -> 6; matrix products, arithmetic and copies ran while one was open for 0% -> 0% of each run, Pallas kernels for 11% -> 21%
where the time goes in v3:
time: 40.7 us; the launch traced here: 40.5 us
  starting transfers between devices  17.1 us (42%)
  Pallas kernels  13.6 us (33%)
  waiting for transfers between devices  8.19 us (20%)
  between operations  0.83 us (2%)
  local copies, waits for them, and re-layouts  0.81 us (2%)
    ppermute x16, starting transfers between devices, swap(): return lax.ppermute(value, axes, pairs)  17.1 us
    ppermute x16, waiting for transfers between devices, swap(): return lax.ppermute(value, axes, pairs)  8.19 us
    pallas_call x1, Pallas kernels, local(): kernel_call(functools.partial(first_step_kernel, slots, picks, groups), (...  5.31 us
    pallas_call x1, Pallas kernels, local(): kernel_call(functools.partial(second_step_kernel, slots, picks, groups, s...  3.59 us
    pallas_call x1, Pallas kernels, local(): kernel_call(functools.partial(side_kernel, slots, picks, active, groups,...  2.11 us
    pallas_call x1, Pallas kernels, local(): kernel_call(score_kernel, struct(1, requests, dtype=f32), [VMEM] * 4)  0.82 us
  transfers between devices with their start and end apart: 16, of which 6 were waited for; matrix products, arithmetic and copies ran while one was open for 0% of the time, Pallas kernels for 21%

profile of v3, /device:TPU:0, one launch (start us, length us, event | category | flops | bytes accessed | tf_op | source)
XLA Modules:
  0.0 40.5 jit_solution(15322536825814699689)
XLA Ops:
  0.6 0.5 %collective-permute-start.1 = (bf16[16,32,128]{2,1,0:T(8,128)(2,1)}, bf16[16,32,128]{2,1,0:T(8,128)(2,1)S(1)}, u32[]{:S(2)}, u32[]{:S(2)}) collective-permute-start(bf16[16,32,128]{2,1,0:T(8,128)(2,1)} %refs_12_.1), channel_id=1, source_target_pairs={{0,1},{1,0},{2,3},{3,2},{4,5},{5,4},{6,7},{7,6},{8,9},{9,8},{10,11... | collective-permute-start | bytes 393224 | tf_op jit(solution)/shard_map/ppermute | solution.py:484
  1.2 0.0 copy-start.9
  1.2 0.1 collective-permute-start.2
  1.3 0.0 copy-start.2
  1.3 0.0 copy-start.3
  1.3 0.7 %copy-done.4 = s32[2,256,16,4]{1,3,2,0:T(4,128)S(1)} copy-done((s32[2,256,16,4]{1,3,2,0:T(4,128)S(1)}, s32[2,256,16,4]{1,3,2,0:T(4,128)}, u32[]{:S(2)}) %copy-start.4) | copy-done | bytes 131096
  2.1 0.0 copy-done.5
  2.1 0.0 copy-done.6
  2.1 0.0 copy-done.7
  2.1 0.0 copy-start.10
  2.1 2.6 %collective-permute-start = (f32[136,128]{1,0:T(8,128)S(1)}, f32[136,128]{1,0:T(8,128)S(1)}, u32[]{:S(2)}, u32[]{:S(2)}) collective-permute-start(f32[136,128]{1,0:T(8,128)S(1)} %get-tuple-element.50.refs_0_.refs_2_), channel_id=1, source_target_pairs={{0,2},{2,0},{1,3},{3,1},{4,6},{6,4},{5,7},{7,5},{8,10},{10,8},{9,1... | collective-permute-start | bytes 208904 | tf_op jit(solution)/shard_map/ppermute | solution.py:484
  4.7 3.6 %collective-permute-start.5 = (bf16[12,32,128]{2,1,0:T(8,128)(2,1)S(1)}, bf16[12,32,128]{2,1,0:T(8,128)(2,1)S(1)}, u32[]{:S(2)}, u32[]{:S(2)}) collective-permute-start(bf16[12,32,128]{2,1,0:T(8,128)(2,1)S(1)} %get-tuple-element.38), channel_id=1, source_target_pairs={{0,12},{4,8},{8,4},{12,0},{1,13},{5,9},{9,5},{13,1},{2,14},{6,10},... | collective-permute-start | bytes 294920 | tf_op jit(solution)/shard_map/ppermute | solution.py:484
  8.3 0.0 collective-permute-start.4
  8.3 0.0 collective-permute-done.refs_1_.refs_3_
  8.3 1.1 %collective-permute-start.3 = (bf16[12,32,128]{2,1,0:T(8,128)(2,1)S(1)}, bf16[12,32,128]{2,1,0:T(8,128)(2,1)S(1)}, u32[]{:S(2)}, u32[]{:S(2)}) collective-permute-start(bf16[12,32,128]{2,1,0:T(8,128)(2,1)S(1)} %get-tuple-element.38), channel_id=1, source_target_pairs={{0,4},{4,0},{8,12},{12,8},{1,5},{5,1},{9,13},{13,9},{2,6},{6,2},{1... | collective-permute-start | bytes 294920 | tf_op jit(solution)/shard_map/ppermute | solution.py:484
  9.4 0.0 collective-permute-done.1.refs_3_.refs_13_
  9.4 0.0 collective-permute-done.2.refs_5_.refs_15_
  9.4 5.3 %shard_map.149 = (bf16[6,32,128]{2,1,0:T(8,128)(2,1)S(1)}, bf16[2,32,128]{2,1,0:T(8,128)(2,1)S(1)}) custom-call(s32[2,4]{1,0:T(2,128)S(1)} %copy-done.3, f32[136,128]{1,0:T(8,128)S(1)} %get-tuple-element.50.refs_0_.refs_2_, f32[136,128]{1,0:T(8,128)S(1)} %collective-permute-done.refs_1_.refs_3_, bf16[16,32,128]{2,1,0:T(8,128)(2,1)S(1)} %copy-done.2, ...), custom_call_target="tpu_custom_call" | custom-call | flops 1000000000 | bytes 1000000 | tf_op jit(solution)/shard_map/pallas_call | solution.py:566
  14.7 0.1 collective-permute-start.6
  14.8 0.0 collective-permute-done.5.refs_2_.refs_23_
  14.8 2.1 %collective-permute-done.4.refs_1_.refs_22_ = bf16[12,32,128]{2,1,0:T(8,128)(2,1)S(1)} collective-permute-done((bf16[12,32,128]{2,1,0:T(8,128)(2,1)S(1)}, bf16[12,32,128]{2,1,0:T(8,128)(2,1)S(1)}, u32[]{:S(2)}, u32[]{:S(2)}) %collective-permute-start.4) | collective-permute-done | bytes 98336 | tf_op jit(solution)/shard_map/ppermute | solution.py:484
  16.9 0.0 collective-permute-done.3.refs_0_.refs_21_
  16.9 0.4 shard_map.150
  17.3 0.0 copy-start.8
  17.3 0.0 collective-permute-done.6.refs_1_
  17.4 0.1 collective-permute-start.10
  17.5 2.5 %collective-permute-start.9 = (bf16[6,32,128]{2,1,0:T(8,128)(2,1)S(1)}, bf16[6,32,128]{2,1,0:T(8,128)(2,1)S(1)}, u32[]{:S(2)}, u32[]{:S(2)}) collective-permute-start(bf16[6,32,128]{2,1,0:T(8,128)(2,1)S(1)} %shard_map.151.refs_4_.refs_17_), channel_id=1, source_target_pairs={{0,12},{4,8},{8,4},{12,0},{1,13},{5,9},{9,5},{13,1},{2,14},{6,10},... | collective-permute-start | bytes 147464 | tf_op jit(solution)/shard_map/ppermute | solution.py:484
  20.0 0.0 collective-permute-start.8
  20.0 1.9 %collective-permute-start.7 = (bf16[6,32,128]{2,1,0:T(8,128)(2,1)S(1)}, bf16[6,32,128]{2,1,0:T(8,128)(2,1)S(1)}, u32[]{:S(2)}, u32[]{:S(2)}) collective-permute-start(bf16[6,32,128]{2,1,0:T(8,128)(2,1)S(1)} %shard_map.151.refs_4_.refs_17_), channel_id=1, source_target_pairs={{0,4},{4,0},{8,12},{12,8},{1,5},{5,1},{9,13},{13,9},{2,6},{6,2},{1... | collective-permute-start | bytes 147464 | tf_op jit(solution)/shard_map/ppermute | solution.py:484
  21.9 2.1 %shard_map.152 = (bf16[512,2048]{1,0:T(8,128)(2,1)S(1)}, bf16[512,2048]{1,0:T(8,128)(2,1)S(1)}, bf16[2048,128]{1,0:T(8,128)(2,1)S(1)}) custom-call(f32[136,128]{1,0:T(8,128)S(1)} %get-tuple-element.50.refs_0_.refs_2_, f32[136,128]{1,0:T(8,128)S(1)} %collective-permute-done.refs_1_.refs_3_, s32[8,4,16]{2,1,0:T(4,128)S(1)} %bitcast.14), custom_call_target="tpu_custom_call" | custom-call | flops 1000000000 | bytes 1000000 | tf_op jit(solution)/shard_map/pallas_call | solution.py:596
  24.0 0.0 collective-permute-done.9.refs_7_.refs_20_
  24.0 1.5 %collective-permute-done.8.refs_6_.refs_19_ = bf16[6,32,128]{2,1,0:T(8,128)(2,1)S(1)} collective-permute-done((bf16[6,32,128]{2,1,0:T(8,128)(2,1)S(1)}, bf16[6,32,128]{2,1,0:T(8,128)(2,1)S(1)}, u32[]{:S(2)}, u32[]{:S(2)}) %collective-permute-start.8) | collective-permute-done | bytes 49184 | tf_op jit(solution)/shard_map/ppermute | solution.py:484
  25.6 0.0 collective-permute-done.7.refs_5_.refs_18_
  25.6 0.0 collective-permute-done.10.refs_11_
  25.6 3.6 %shard_map.153 = (bf16[4,32,128]{2,1,0:T(8,128)(2,1)S(1)}, bf16[4,32,128]{2,1,0:T(8,128)(2,1)S(1)}, bf16[2,32,128]{2,1,0:T(8,128)(2,1)S(1)}, f32[2,32,128]{2,1,0:T(8,128)S(1)}, f32[2,32,128]{2,1,0:T(8,128)S(1)}) custom-call(s32[2,4]{1,0:T(2,128)S(1)} %copy-done.3, bf16[512,2048]{1,0:T(8,128)(2,1)S(1)} %get-tuple-element.52.refs_0_, ...), custom_call_target="tpu_custom_call" | custom-call | flops 1000000000 | bytes 1000000 | tf_op jit(solution)/shard_map/pallas_call | solution.py:604
  29.2 0.1 collective-permute-start.11
  29.3 1.1 %collective-permute-done.11.refs_1_ = bf16[4,32,128]{2,1,0:T(8,128)(2,1)S(1)} collective-permute-done((bf16[4,32,128]{2,1,0:T(8,128)(2,1)S(1)}, bf16[4,32,128]{2,1,0:T(8,128)(2,1)S(1)}, u32[]{:S(2)}, u32[]{:S(2)}) %collective-permute-start.11) | collective-permute-done | bytes 32800 | tf_op jit(solution)/shard_map/ppermute | solution.py:484
  30.4 2.5 %collective-permute-start.14 = (bf16[4,32,128]{2,1,0:T(8,128)(2,1)S(1)}, bf16[4,32,128]{2,1,0:T(8,128)(2,1)S(1)}, u32[]{:S(2)}, u32[]{:S(2)}) collective-permute-start(bf16[4,32,128]{2,1,0:T(8,128)(2,1)S(1)} %shard_map.154.refs_13_), channel_id=1, source_target_pairs={{0,12},{4,8},{8,4},{12,0},{1,13},{5,9},{9,5},{13,1},{2,14},{6,10},... | collective-permute-start | bytes 98312 | tf_op jit(solution)/shard_map/ppermute | solution.py:484
  33.0 0.0 collective-permute-start.13
  33.0 1.9 %collective-permute-start.12 = (bf16[4,32,128]{2,1,0:T(8,128)(2,1)S(1)}, bf16[4,32,128]{2,1,0:T(8,128)(2,1)S(1)}, u32[]{:S(2)}, u32[]{:S(2)}) collective-permute-start(bf16[4,32,128]{2,1,0:T(8,128)(2,1)S(1)} %shard_map.154.refs_13_), channel_id=1, source_target_pairs={{0,4},{4,0},{8,12},{12,8},{1,5},{5,1},{9,13},{13,9},{2,6},{6,2},{1... | collective-permute-start | bytes 98312 | tf_op jit(solution)/shard_map/ppermute | solution.py:484
  34.9 1.3 %collective-permute-done.14.refs_16_ = bf16[4,32,128]{2,1,0:T(8,128)(2,1)S(1)} collective-permute-done((bf16[4,32,128]{2,1,0:T(8,128)(2,1)S(1)}, bf16[4,32,128]{2,1,0:T(8,128)(2,1)S(1)}, u32[]{:S(2)}, u32[]{:S(2)}) %collective-permute-start.14) | collective-permute-done | bytes 32800 | tf_op jit(solution)/shard_map/ppermute | solution.py:484
  36.2 1.6 %collective-permute-done.13.refs_15_ = bf16[4,32,128]{2,1,0:T(8,128)(2,1)S(1)} collective-permute-done((bf16[4,32,128]{2,1,0:T(8,128)(2,1)S(1)}, bf16[4,32,128]{2,1,0:T(8,128)(2,1)S(1)}, u32[]{:S(2)}, u32[]{:S(2)}) %collective-permute-start.13) | collective-permute-done | bytes 32800 | tf_op jit(solution)/shard_map/ppermute | solution.py:484
  37.8 0.0 collective-permute-done.12.refs_14_
  37.8 0.7 %shard_map.155 = (f32[4,32,128]{2,1,0:T(8,128)S(1)}, f32[4,32,128]{2,1,0:T(8,128)S(1)}, bf16[4,32,128]{2,1,0:T(8,128)(2,1)S(1)}, f32[8,512]{1,0:T(8,128)S(1)}) custom-call(f32[6,32,128]{2,1,0:T(8,128)S(1)} %get-tuple-element.42.refs_8_.refs_0_, f32[6,32,128]{2,1,0:T(8,128)S(1)} %get-tuple-element.43.refs_9_.refs_1_, ...), custom_call_target="tpu_custom_call" | custom-call | flops 1000000000 | bytes 1000000 | tf_op jit(solution)/shard_map/pallas_call | solution.py:631
  38.5 0.1 collective-permute-start.15
  38.6 0.7 %shard_map.156 = (f32[4,32,128]{2,1,0:T(8,128)}, f32[4,32,128]{2,1,0:T(8,128)}, bf16[4,32,128]{2,1,0:T(8,128)(2,1)}) custom-call(f32[4,32,128]{2,1,0:T(8,128)S(1)} %get-tuple-element.61.refs_0_, f32[4,32,128]{2,1,0:T(8,128)S(1)} %get-tuple-element.62.refs_1_, bf16[4,32,128]{2,1,0:T(8,128)(2,1)S(1)} %get-tuple-element.63.refs_2_), custom_call_target="tpu_custom_call" | custom-call | flops 1000000000 | bytes 1000000 | tf_op jit(solution)/shard_map/pallas_call | solution.py:655
  39.3 0.5 %collective-permute-done.15.other_ref = f32[8,512]{1,0:T(8,128)S(1)} collective-permute-done((f32[8,512]{1,0:T(8,128)S(1)}, f32[8,512]{1,0:T(8,128)S(1)}, u32[]{:S(2)}, u32[]{:S(2)}) %collective-permute-start.15) | collective-permute-done | bytes 16416 | tf_op jit(solution)/shard_map/ppermute | solution.py:484
  39.7 0.8 %shard_map.157 = f32[1,8]{1,0:T(1,128)} custom-call(f32[8,512]{1,0:T(8,128)S(1)} %get-tuple-element.67.own_ref, f32[8,512]{1,0:T(8,128)S(1)} %collective-permute-done.15.other_ref, bf16[512,256]{1,0:T(8,128)(2,1)S(1)} %copy-done.1, bf16[1,256]{1,0:T(2,128)(2,1)S(1)} %reshape.15.refs_7_.refs_17_.head_ref), custom_call_target="tpu_custom_call" | custom-call | flops 1000000000 | bytes 1000000 | tf_op jit(solution)/shard_map/pallas_call | solution.py:658
  (20 shorter events, 0.1 us)
Async XLA Ops:
  0.6 8.7 %collective-permute-start.1 = (bf16[16,32,128]{2,1,0:T(8,128)(2,1)}, bf16[16,32,128]{2,1,0:T(8,128)(2,1)S(1)}, u32[]{:S(2)}, u32[]{:S(2)}) collective-permute-start(bf16[16,32,128]{2,1,0:T(8,128)(2,1)} %refs_12_.1), channel_id=1, source_target_pairs={{0,1},{1,0},{2,3},{3,2},{4,5},{5,4},{6,7},{7,6},{8,9},{9,8},{10,11... | collective-permute-start | bytes 393224 | tf_op jit(solution)/shard_map/ppermute | solution.py:484
  1.2 0.9 %copy-start.4 = (s32[2,256,16,4]{1,3,2,0:T(4,128)S(1)}, s32[2,256,16,4]{1,3,2,0:T(4,128)}, u32[]{:S(2)}) copy-start(s32[2,256,16,4]{1,3,2,0:T(4,128)} %param.20) | copy-start | bytes 393220
  1.2 0.9 %copy-start.5 = (f32[4,32,128]{2,1,0:T(8,128)S(1)}, f32[4,32,128]{2,1,0:T(8,128)}, u32[]{:S(2)}) copy-start(f32[4,32,128]{2,1,0:T(8,128)} %refs_10_.1) | copy-start | bytes 196612
  1.2 0.9 %copy-start.6 = (f32[4,32,128]{2,1,0:T(8,128)S(1)}, f32[4,32,128]{2,1,0:T(8,128)}, u32[]{:S(2)}) copy-start(f32[4,32,128]{2,1,0:T(8,128)} %refs_11_.1) | copy-start | bytes 196612
  1.2 0.9 %copy-start.7 = (bf16[1,4,32,128]{3,2,1,0:T(8,128)(2,1)S(1)}, bf16[1,4,32,128]{3,2,1,0:T(8,128)(2,1)}, u32[]{:S(2)}) copy-start(bf16[1,4,32,128]{3,2,1,0:T(8,128)(2,1)} %param.15) | copy-start | bytes 98308
  1.2 0.9 %copy-start.9 = (f32[2,256]{1,0:T(2,128)S(1)}, f32[2,256]{1,0:T(2,128)}, u32[]{:S(2)}) copy-start(f32[2,256]{1,0:T(2,128)} %labels_ref.1) | copy-start | bytes 6148
  1.2 8.2 %collective-permute-start.2 = (bf16[512,512]{1,0:T(8,128)(2,1)}, bf16[512,512]{1,0:T(8,128)(2,1)S(1)}, u32[]{:S(2)}, u32[]{:S(2)}) collective-permute-start(bf16[512,512]{1,0:T(8,128)(2,1)} %bitcast.7), channel_id=1, source_target_pairs={{0,1},{1,0},{2,3},{3,2},{4,5},{5,4},{6,7},{7,6},{8,9},{9,8},{10,11... | collective-permute-start | bytes 1572872 | tf_op jit(solution)/shard_map/ppermute | solution.py:484
  1.3 8.1 %copy-start.11 = (bf16[256]{0:T(256)(128)(2,1)S(1)}, bf16[256]{0:T(256)(128)(2,1)}, u32[]{:S(2)}) copy-start(bf16[256]{0:T(256)(128)(2,1)} %param.18) | copy-start | bytes 1540
  1.3 8.1 %copy-start = (bf16[16,32,512]{2,1,0:T(8,128)(2,1)S(1)}, bf16[16,32,512]{2,1,0:T(8,128)(2,1)}, u32[]{:S(2)}) copy-start(bf16[16,32,512]{2,1,0:T(8,128)(2,1)} %param.16) | copy-start | bytes 1572868
  1.3 8.1 %copy-start.1 = (bf16[512,256]{1,0:T(8,128)(2,1)S(1)}, bf16[512,256]{1,0:T(8,128)(2,1)}, u32[]{:S(2)}) copy-start(bf16[512,256]{1,0:T(8,128)(2,1)} %w2_ref.1) | copy-start | bytes 786436
  1.3 8.1 %copy-start.2 = (bf16[16,32,128]{2,1,0:T(8,128)(2,1)S(1)}, bf16[16,32,128]{2,1,0:T(8,128)(2,1)}, u32[]{:S(2)}) copy-start(bf16[16,32,128]{2,1,0:T(8,128)(2,1)} %refs_12_.1) | copy-start | bytes 393220
  1.3 8.1 %copy-start.3 = (s32[2,4]{1,0:T(2,128)S(1)}, s32[2,4]{1,0:T(2,128)}, u32[]{:S(2)}) copy-start(s32[2,4]{1,0:T(2,128)} %blocks_ref.5) | copy-start | bytes 100
  2.1 14.8 %copy-start.10 = (s32[1,4]{1,0:T(1,128)S(1)}, s32[1,4]{1,0:T(1,128)}, u32[]{:S(2)}) copy-start(s32[1,4]{1,0:T(1,128)} %layout_ref.1) | copy-start | bytes 52
  2.1 6.2 %collective-permute-start = (f32[136,128]{1,0:T(8,128)S(1)}, f32[136,128]{1,0:T(8,128)S(1)}, u32[]{:S(2)}, u32[]{:S(2)}) collective-permute-start(f32[136,128]{1,0:T(8,128)S(1)} %get-tuple-element.50.refs_0_.refs_2_), channel_id=1, source_target_pairs={{0,2},{2,0},{1,3},{3,1},{4,6},{6,4},{5,7},{7,5},{8,10},{10,8},{9,1... | collective-permute-start | bytes 208904 | tf_op jit(solution)/shard_map/ppermute | solution.py:484
  4.7 10.1 %collective-permute-start.5 = (bf16[12,32,128]{2,1,0:T(8,128)(2,1)S(1)}, bf16[12,32,128]{2,1,0:T(8,128)(2,1)S(1)}, u32[]{:S(2)}, u32[]{:S(2)}) collective-permute-start(bf16[12,32,128]{2,1,0:T(8,128)(2,1)S(1)} %get-tuple-element.38), channel_id=1, source_target_pairs={{0,12},{4,8},{8,4},{12,0},{1,13},{5,9},{9,5},{13,1},{2,14},{6,10},... | collective-permute-start | bytes 294920 | tf_op jit(solution)/shard_map/ppermute | solution.py:484
  8.3 8.6 %collective-permute-start.4 = (bf16[12,32,128]{2,1,0:T(8,128)(2,1)S(1)}, bf16[12,32,128]{2,1,0:T(8,128)(2,1)S(1)}, u32[]{:S(2)}, u32[]{:S(2)}) collective-permute-start(bf16[12,32,128]{2,1,0:T(8,128)(2,1)S(1)} %get-tuple-element.38), channel_id=1, source_target_pairs={{0,8},{4,12},{8,0},{12,4},{1,9},{5,13},{9,1},{13,5},{2,10},{6,14},... | collective-permute-start | bytes 294920 | tf_op jit(solution)/shard_map/ppermute | solution.py:484
  8.3 8.6 %collective-permute-start.3 = (bf16[12,32,128]{2,1,0:T(8,128)(2,1)S(1)}, bf16[12,32,128]{2,1,0:T(8,128)(2,1)S(1)}, u32[]{:S(2)}, u32[]{:S(2)}) collective-permute-start(bf16[12,32,128]{2,1,0:T(8,128)(2,1)S(1)} %get-tuple-element.38), channel_id=1, source_target_pairs={{0,4},{4,0},{8,12},{12,8},{1,5},{5,1},{9,13},{13,9},{2,6},{6,2},{1... | collective-permute-start | bytes 294920 | tf_op jit(solution)/shard_map/ppermute | solution.py:484
  14.7 2.6 %collective-permute-start.6 = (bf16[6,32,128]{2,1,0:T(8,128)(2,1)S(1)}, bf16[6,32,128]{2,1,0:T(8,128)(2,1)S(1)}, u32[]{:S(2)}, u32[]{:S(2)}) collective-permute-start(bf16[6,32,128]{2,1,0:T(8,128)(2,1)S(1)} %get-tuple-element.37.refs_0_), channel_id=1, source_target_pairs={{0,1},{1,0},{2,3},{3,2},{4,5},{5,4},{6,7},{7,6},{8,9},{9,8},{10,11... | collective-permute-start | bytes 147464 | tf_op jit(solution)/shard_map/ppermute | solution.py:484
  17.3 4.6 %copy-start.8 = (s32[1,8,16,4]{2,3,1,0:T(4,128)S(1)}, s32[1,8,16,4]{2,3,1,0:T(4,128)}, u32[]{:S(2)}) copy-start(s32[1,8,16,4]{2,3,1,0:T(4,128)} %param.23) | copy-start | bytes 6148
  17.4 8.2 %collective-permute-start.10 = (f32[6,32,128]{2,1,0:T(8,128)S(1)}, f32[6,32,128]{2,1,0:T(8,128)S(1)}, u32[]{:S(2)}, u32[]{:S(2)}) collective-permute-start(f32[6,32,128]{2,1,0:T(8,128)S(1)} %get-tuple-element.54), channel_id=1, source_target_pairs={{0,1},{1,0},{2,3},{3,2},{4,5},{5,4},{6,7},{7,6},{8,9},{9,8},{10,11... | collective-permute-start | bytes 294920 | tf_op jit(solution)/shard_map/ppermute | solution.py:484
  17.5 6.6 %collective-permute-start.9 = (bf16[6,32,128]{2,1,0:T(8,128)(2,1)S(1)}, bf16[6,32,128]{2,1,0:T(8,128)(2,1)S(1)}, u32[]{:S(2)}, u32[]{:S(2)}) collective-permute-start(bf16[6,32,128]{2,1,0:T(8,128)(2,1)S(1)} %shard_map.151.refs_4_.refs_17_), channel_id=1, source_target_pairs={{0,12},{4,8},{8,4},{12,0},{1,13},{5,9},{9,5},{13,1},{2,14},{6,10},... | collective-permute-start | bytes 147464 | tf_op jit(solution)/shard_map/ppermute | solution.py:484
  20.0 5.6 %collective-permute-start.8 = (bf16[6,32,128]{2,1,0:T(8,128)(2,1)S(1)}, bf16[6,32,128]{2,1,0:T(8,128)(2,1)S(1)}, u32[]{:S(2)}, u32[]{:S(2)}) collective-permute-start(bf16[6,32,128]{2,1,0:T(8,128)(2,1)S(1)} %shard_map.151.refs_4_.refs_17_), channel_id=1, source_target_pairs={{0,8},{4,12},{8,0},{12,4},{1,9},{5,13},{9,1},{13,5},{2,10},{6,14},... | collective-permute-start | bytes 147464 | tf_op jit(solution)/shard_map/ppermute | solution.py:484
  20.0 5.6 %collective-permute-start.7 = (bf16[6,32,128]{2,1,0:T(8,128)(2,1)S(1)}, bf16[6,32,128]{2,1,0:T(8,128)(2,1)S(1)}, u32[]{:S(2)}, u32[]{:S(2)}) collective-permute-start(bf16[6,32,128]{2,1,0:T(8,128)(2,1)S(1)} %shard_map.151.refs_4_.refs_17_), channel_id=1, source_target_pairs={{0,4},{4,0},{8,12},{12,8},{1,5},{5,1},{9,13},{13,9},{2,6},{6,2},{1... | collective-permute-start | bytes 147464 | tf_op jit(solution)/shard_map/ppermute | solution.py:484
  29.2 1.3 %collective-permute-start.11 = (bf16[4,32,128]{2,1,0:T(8,128)(2,1)S(1)}, bf16[4,32,128]{2,1,0:T(8,128)(2,1)S(1)}, u32[]{:S(2)}, u32[]{:S(2)}) collective-permute-start(bf16[4,32,128]{2,1,0:T(8,128)(2,1)S(1)} %get-tuple-element.60), channel_id=1, source_target_pairs={{0,1},{1,0},{2,3},{3,2},{4,5},{5,4},{6,7},{7,6},{8,9},{9,8},{10,11... | collective-permute-start | bytes 98312 | tf_op jit(solution)/shard_map/ppermute | solution.py:484
  30.4 5.8 %collective-permute-start.14 = (bf16[4,32,128]{2,1,0:T(8,128)(2,1)S(1)}, bf16[4,32,128]{2,1,0:T(8,128)(2,1)S(1)}, u32[]{:S(2)}, u32[]{:S(2)}) collective-permute-start(bf16[4,32,128]{2,1,0:T(8,128)(2,1)S(1)} %shard_map.154.refs_13_), channel_id=1, source_target_pairs={{0,12},{4,8},{8,4},{12,0},{1,13},{5,9},{9,5},{13,1},{2,14},{6,10},... | collective-permute-start | bytes 98312 | tf_op jit(solution)/shard_map/ppermute | solution.py:484
  33.0 4.8 %collective-permute-start.13 = (bf16[4,32,128]{2,1,0:T(8,128)(2,1)S(1)}, bf16[4,32,128]{2,1,0:T(8,128)(2,1)S(1)}, u32[]{:S(2)}, u32[]{:S(2)}) collective-permute-start(bf16[4,32,128]{2,1,0:T(8,128)(2,1)S(1)} %shard_map.154.refs_13_), channel_id=1, source_target_pairs={{0,8},{4,12},{8,0},{12,4},{1,9},{5,13},{9,1},{13,5},{2,10},{6,14},... | collective-permute-start | bytes 98312 | tf_op jit(solution)/shard_map/ppermute | solution.py:484
  33.0 4.8 %collective-permute-start.12 = (bf16[4,32,128]{2,1,0:T(8,128)(2,1)S(1)}, bf16[4,32,128]{2,1,0:T(8,128)(2,1)S(1)}, u32[]{:S(2)}, u32[]{:S(2)}) collective-permute-start(bf16[4,32,128]{2,1,0:T(8,128)(2,1)S(1)} %shard_map.154.refs_13_), channel_id=1, source_target_pairs={{0,4},{4,0},{8,12},{12,8},{1,5},{5,1},{9,13},{13,9},{2,6},{6,2},{1... | collective-permute-start | bytes 98312 | tf_op jit(solution)/shard_map/ppermute | solution.py:484
  38.5 1.2 %collective-permute-start.15 = (f32[8,512]{1,0:T(8,128)S(1)}, f32[8,512]{1,0:T(8,128)S(1)}, u32[]{:S(2)}, u32[]{:S(2)}) collective-permute-start(f32[8,512]{1,0:T(8,128)S(1)} %get-tuple-element.67.own_ref), channel_id=1, source_target_pairs={{0,1},{1,0},{2,3},{3,2},{4,5},{5,4},{6,7},{7,6},{8,9},{9,8},{10,11... | collective-permute-start | bytes 49160 | tf_op jit(solution)/shard_map/ppermute | solution.py:484

commit v4 on v3

--- a/solution.py
+++ b/solution.py
@@ -111,7 +111,7 @@
     out_ref[...] = jnp.zeros_like(out_ref)
 
 
-def open_kernel(lead_ref, ids_ref, labels_ref, linear_ref, square_ref, serve_ref, out_ref, pack_ref):
+def open_kernel(lead_ref, ids_ref, labels_ref, linear_ref, square_ref, serve_ref, out_ref, pack_ref, coded_ref):
     owned = linear_ref.shape[0]
     pack_ref[0:owned] = linear_ref[...].astype(bf16)
     pack_ref[owned : 2 * owned] = square_ref[...].astype(bf16)
@@ -125,8 +125,22 @@
             low = (step * slots + slot) * picks
             out_ref[low : low + picks] = ids_ref[step, slot, :, lanes].astype(f32)
     low = steps * slots * picks
-    out_ref[low:] = jnp.zeros((out_ref.shape[0] - low, samples), f32)
-    out_ref[low : low + steps] = labels_ref[:, lanes]
+    labels = labels_ref[:, lanes]
+    per = slots * picks
+    coded_ref[0:per] = out_ref[0:per].astype(jnp.int32) + 65536 * out_ref[per:low].astype(jnp.int32)
+    fixed = jnp.floor(labels * float(1 << 30) + 0.5).astype(jnp.int32)
+    coded_ref[per:] = jnp.zeros((8, samples), jnp.int32)
+    coded_ref[per : per + steps] = fixed
+    out_ref[low:] = jnp.zeros((8, samples), f32)
+    out_ref[low : low + steps] = fixed.astype(f32) * (1.0 / (1 << 30))
+
+
+def decode_note(coded_ref, note_ref, steps):
+    per = coded_ref.shape[0] - 8
+    pairs = coded_ref[0:per]
+    note_ref[0:per] = (pairs & 65535).astype(f32)
+    note_ref[per : 2 * per] = (pairs >> 16).astype(f32)
+    note_ref[2 * per :] = coded_ref[per:].astype(f32) * (1.0 / (1 << 30))
 
 
 def fill_step(counts_ref, note_ref, step, slots, picks, active, rows):
@@ -164,13 +178,15 @@
     hidden_one = (pre_one * sig_one).astype(bf16)
     pre_two = jnp.dot(hidden_one, second, preferred_element_type=f32)
     sig_two = sigmoid(pre_two)
-    hidden_two = (pre_two * sig_two).astype(bf16).astype(f32)
+    hidden_two = (pre_two * sig_two).astype(bf16)
     head = head_ref[...].astype(f32)
-    logit = jnp.sum(hidden_two * head, axis=1, keepdims=True)
+    heads = jnp.broadcast_to(head, (128, head.shape[1])).astype(bf16)
+    logit = lax.dot_general(hidden_two, heads, nt_dims, preferred_element_type=f32)
     label = jnp.concatenate(
-        [jnp.broadcast_to(row, (128, row.shape[1])).T[:, 0:1] for row in label_rows], axis=0
+        [jnp.broadcast_to(row, (128, row.shape[1])).T for row in label_rows], axis=0
     )
     error = sigmoid(logit) - label
+    error = jnp.concatenate([error] * (head.shape[1] // 128), axis=1)
     grad_two = (error * head * (sig_two * (1.0 + pre_two * (1.0 - sig_two)))).astype(bf16)
     back = lax.dot_general(grad_two, second, nt_dims, preferred_element_type=f32)
     grad_one = (back * (sig_one * (1.0 + pre_one * (1.0 - sig_one)))).astype(bf16)
@@ -197,28 +213,29 @@
     return total
 
 
-def first_step_kernel(slots, picks, groups, blocks_ref, *refs):
-    notes = refs[:groups]
-    slab_own, slab_other, w1_own, w1_other, w2_ref, head_ref = refs[groups : groups + 6]
-    share_ref, rest_own = refs[groups + 6 : groups + 8]
-    counts_refs = refs[groups + 8 :]
+def first_step_kernel(slots, picks, groups, blocks_ref, note_ref, *refs):
+    coded = refs[: groups - 1]
+    slab_own, slab_other, w1_own, w1_other, w2_ref, head_ref = refs[groups - 1 : groups + 5]
+    share_ref, rest_own, note_at, *counts_at = refs[groups + 5 :]
     active = blocks_ref.shape[1]
     half, rows = slab_other.shape[1:]
     fresh = active // 2
     kept = active - fresh
-    labels = notes[0].shape[0] // 8 * 8 - 8
+    labels = note_ref.shape[0] - 8
     table = jnp.concatenate(
         [pick_blocks(slab, blocks_ref, 0, 0) for slab in (slab_own, slab_other)], axis=0
     )
+    if coded:
+        decode_note(coded[0], note_at, blocks_ref.shape[0])
     inputs = []
-    for note, counts_ref in zip(notes, counts_refs):
+    for note, counts_ref in zip((note_ref, note_at), counts_at):
         fill_step(counts_ref, note, 0, slots, picks, active, rows)
         pooled = jnp.dot(table, counts_ref[...], preferred_element_type=f32)
         inputs.append(by_sample(pooled, slots))
     grad = network(
         inputs,
-        [note[labels : labels + 1] for note in notes],
-        [ref[...] for ref in counts_refs],
+        [note[labels : labels + 1] for note in (note_ref, note_at)[:groups]],
+        [ref[...] for ref in counts_at],
         w1_own,
         w1_other,
         w2_ref,
@@ -235,13 +252,22 @@
             share_ref[kept + i - fresh] = part[half:]
 
 
-def side_kernel(slots, picks, active, groups, rows, *refs):
+def side_kernel(slots, picks, groups, blocks_ref, slab_own, slab_other, *refs):
     notes = refs[:groups]
-    req_ref = refs[groups]
-    counts_refs = refs[groups + 1 : 2 * groups + 1]
-    wanted_ref = refs[2 * groups + 1]
-    for note, counts_ref in zip(notes, counts_refs):
+    counts_refs = refs[groups : 2 * groups]
+    fresh_refs = refs[2 * groups :]
+    steps, active = blocks_ref.shape
+    rows = slab_own.shape[2]
+    kept = active - active // 2
+    table = jnp.concatenate(
+        [pick_blocks(slab, blocks_ref, steps - 1, kept) for slab in (slab_own, slab_other)], axis=0
+    )
+    for note, counts_ref, fresh_ref in zip(notes, counts_refs, fresh_refs):
         fill_step(counts_ref, note, 1, slots, picks, active, rows)
+        fresh_ref[...] = jnp.dot(table, counts_ref[kept * rows :], preferred_element_type=f32)
+
+
+def wanted_kernel(rows, req_ref, wanted_ref):
     requests = req_ref.shape[0]
     lanes_ids = jnp.concatenate([req_ref[i] for i in range(requests)], axis=1).astype(f32)
     fill_counts(wanted_ref, lanes_ids, 0, wanted_ref.shape[0] // rows, rows)
@@ -333,17 +359,18 @@
 
 def second_step_kernel(slots, picks, groups, steps, sums_count, blocks_ref, *refs):
     counts_refs = refs[:groups]
-    notes = refs[groups : 2 * groups]
-    sums = refs[2 * groups : 2 * groups + sums_count]
-    refs = refs[2 * groups + sums_count :]
-    linear_own, square_own, weight_own, cross, slab_own, slab_other = refs[:6]
-    w1_own, w1_other, w2_ref, head_ref = refs[6:10]
-    out_own, out_other, new_out, linear_out, square_out = refs[10:]
+    fresh_refs = refs[groups : 2 * groups]
+    notes = refs[2 * groups : 3 * groups]
+    sums = refs[3 * groups : 3 * groups + sums_count]
+    refs = refs[3 * groups + sums_count :]
+    linear_own, square_own, weight_own, cross = refs[:4]
+    w1_own, w1_other, w2_ref, head_ref = refs[4:8]
+    out_own, out_other, new_out, linear_out, square_out = refs[8:]
     active = blocks_ref.shape[1]
-    half, rows = slab_own.shape[1:]
+    half, rows = cross.shape[1:]
     fresh = active // 2
     kept = active - fresh
-    labels = notes[0].shape[0] // 8 * 8 - 8 + 1
+    labels = notes[0].shape[0] - 8 + steps - 1
 
     new_own, new_other = [], []
     for i in range(kept):
@@ -357,13 +384,14 @@
         weights = ftrl_update(cross[i], cross[kept + i], gradient, cross[2 * kept + i])[2]
         new_other.append(weights.astype(bf16))
 
-    def table(new, slab):
-        return jnp.concatenate(new + [pick_blocks(slab, blocks_ref, steps - 1, kept)], axis=1)
-
-    full = jnp.concatenate([table(new_own, slab_own), table(new_other, slab_other)], axis=0)
+    new = [jnp.concatenate(blocks, axis=1) for blocks in (new_own, new_other)]
+    table = jnp.concatenate(new, axis=0)
     counts = [ref[...] for ref in counts_refs]
     inputs = [
-        by_sample(jnp.dot(full, group, preferred_element_type=f32), slots) for group in counts
+        by_sample(
+            fresh_ref[...] + jnp.dot(table, group[: kept * rows], preferred_element_type=f32), slots
+        )
+        for group, fresh_ref in zip(counts, fresh_refs)
     ]
     grad = network(
         inputs,
@@ -459,10 +487,10 @@
     pre_one = own_ref[...] + other_ref[...]
     hidden_one = (pre_one * sigmoid(pre_one)).astype(bf16)
     pre_two = jnp.dot(hidden_one, w2_ref[...], preferred_element_type=f32)
-    hidden_two = (pre_two * sigmoid(pre_two)).astype(bf16).astype(f32)
-    logit = jnp.sum(hidden_two * head_ref[...].astype(f32), axis=1, keepdims=True)
-    requests = logit.shape[0]
-    out_ref[...] = jnp.broadcast_to(logit, (requests, 128)).T[0:1, :requests]
+    hidden_two = (pre_two * sigmoid(pre_two)).astype(bf16)
+    heads = jnp.broadcast_to(head_ref[...].astype(f32), (8, head_ref.shape[1])).astype(bf16)
+    logit = lax.dot_general(heads, hidden_two, nt_dims, preferred_element_type=f32)
+    out_ref[...] = logit[0:1]
 
 
 def swap(value, axes, sizes, bits):
@@ -549,28 +577,32 @@
     serve_own = serve_table[0]
 
     lead = kernel_call(lead_kernel, struct(8, 128, dtype=f32), [], micros=20.0)()
-    note, pack = kernel_call(
+    per = slots * picks
+    note, pack, coded = kernel_call(
         open_kernel,
-        (struct(steps * slots * picks + 8, samples, dtype=f32), struct(3 * owned, half, rows)),
+        (
+            struct(steps * per + 8, samples, dtype=f32),
+            struct(3 * owned, half, rows),
+            struct(per + 8, samples, dtype=jnp.int32),
+        ),
         [VMEM] * 6,
     )(lead, ids, click_labels, linear_state, square_state, serve_own)
     if direct:
         packs = [swap(pack, ("dp",), sizes, (k,)) for k in range(1, owners)]
     else:
         packs = [lax.all_gather(pack, "dp", axis=0, tiled=False)]
-    notes = [note]
-    if groups > 1:
-        notes.append(swap(note, ("replica",), sizes, (1,)))
-
+    coded = [swap(coded, ("replica",), sizes, (1,))] if groups > 1 else []
     counts_shape = struct(active * rows, slots * samples)
-    share, rest_own = kernel_call(
+    others = struct(fresh, half, rows)
+    share, rest_own, note_other = kernel_call(
         functools.partial(first_step_kernel, slots, picks, groups),
-        (struct(2 * kept + fresh, half, rows), struct(fresh, half, rows)),
+        (struct(2 * kept + fresh, half, rows), others, struct(*note.shape, dtype=f32)),
         [VMEM] * (7 + groups),
         [pltpu.VMEM(counts_shape.shape, bf16)] * groups,
     )(
         step_blocks,
-        *notes,
+        note,
+        *coded,
         hot_slab,
         slab_other,
         w1_own,
@@ -578,6 +610,7 @@
         second_weight,
         head,
     )
+    notes = [note, note_other][:groups]
     share_turned = swap(share, ("mp",), sizes, (1,))
     late = lax.optimization_barrier((share, *packs))[1:]
     old_shape = struct(touched, half, rows, dtype=f32)
@@ -593,18 +626,19 @@
     sums = early = reduce_rest(total, sizes, groups)
     cross = swap(cross, ("mp",), sizes, (1,))
     late = lax.optimization_barrier((total, *notes))[1:]
-    *counts, wanted = kernel_call(
-        functools.partial(side_kernel, slots, picks, active, groups, rows),
-        (counts_shape,) * groups + (struct(positions * rows, requests * slots),),
-        [VMEM] * (groups + 1),
-    )(*late, req)
+    counts = kernel_call(
+        functools.partial(side_kernel, slots, picks, groups),
+        (counts_shape,) * groups
+        + (struct(2 * half, slots * samples, dtype=f32),) * groups,
+        [VMEM] * (groups + 3),
+    )(step_blocks, hot_slab, slab_other, *late)
     shared = struct(kept, half, rows)
     state_shape = struct(kept, half, rows, dtype=f32)
     payload = struct(active, half, rows)
     grad_own, grad_other, new_own, linear_mid, square_mid = kernel_call(
         functools.partial(second_step_kernel, slots, picks, groups, steps, len(sums)),
         (payload, payload, shared, state_shape, state_shape),
-        [VMEM] * (11 + 2 * groups + len(sums)),
+        [VMEM] * (9 + 3 * groups + len(sums)),
     )(
         step_blocks,
         *counts,
@@ -614,8 +648,6 @@
         square_old,
         weight_old,
         cross,
-        hot_slab,
-        slab_other,
         w1_own,
         w1_other,
         second_weight,
@@ -623,6 +655,10 @@
     )
     total = join([grad_own, swap(grad_other, ("mp",), sizes, (1,))])
     sums = reduce_rest(total, sizes, groups)
+    late = lax.optimization_barrier((total, req))[1]
+    wanted = kernel_call(
+        functools.partial(wanted_kernel, rows), struct(positions * rows, requests * slots), [VMEM]
+    )(late)
     results = (
         struct(*linear_state.shape, dtype=f32),
         struct(*square_state.shape, dtype=f32),

time: 40.7 us -> 40.1 us (0.985)
    pallas_call x1, Pallas kernels: 3.59 us -> 3.03 us  [local(): kernel_call(functools.partial(second_step_kernel, slots, picks, groups, s...]
    pallas_call x2 -> x3, Pallas kernels: 2.14 us -> 2.66 us  [the longest x1 2.36 us: local(): kernel_call(functools.partial(side_kernel, slots, picks, groups), (counts...]
  transfers between devices with their start and end apart: 16 -> 16, of which waited for: 6 -> 6; matrix products, arithmetic and copies ran while one was open for 0% -> 0% of each run, Pallas kernels for 21% -> 22%
where the time goes in v4:
time: 40.1 us; the launch traced here: 40 us
  starting transfers between devices  16.8 us (42%)
  Pallas kernels  13.4 us (33%)
  waiting for transfers between devices  8.12 us (20%)
  between operations  0.83 us (2%)
  local copies, waits for them, and re-layouts  0.81 us (2%)
    ppermute x16, starting transfers between devices, swap(): return lax.ppermute(value, axes, pairs)  16.8 us
    ppermute x16, waiting for transfers between devices, swap(): return lax.ppermute(value, axes, pairs)  8.12 us
    pallas_call x1, Pallas kernels, local(): kernel_call(functools.partial(first_step_kernel, slots, picks, groups), (...  5.15 us
    pallas_call x1, Pallas kernels, local(): kernel_call(functools.partial(second_step_kernel, slots, picks, groups, s...  3.03 us
    pallas_call x1, Pallas kernels, local(): kernel_call(functools.partial(side_kernel, slots, picks, groups), (counts...  2.36 us
  transfers between devices with their start and end apart: 16, of which 6 were waited for; matrix products, arithmetic and copies ran while one was open for 0% of the time, Pallas kernels for 22%

profile of v4, /device:TPU:0, one launch (start us, length us, event | category | flops | bytes accessed | tf_op | source)
XLA Modules:
  0.0 40.0 jit_solution(11624471536284334906)
XLA Ops:
  0.6 0.5 %collective-permute-start.1 = (bf16[16,32,128]{2,1,0:T(8,128)(2,1)}, bf16[16,32,128]{2,1,0:T(8,128)(2,1)S(1)}, u32[]{:S(2)}, u32[]{:S(2)}) collective-permute-start(bf16[16,32,128]{2,1,0:T(8,128)(2,1)} %slab_own.3), channel_id=1, source_target_pairs={{0,1},{1,0},{2,3},{3,2},{4,5},{5,4},{6,7},{7,6},{8,9},{9,8},{10,11... | collective-permute-start | bytes 393224 | tf_op jit(solution)/shard_map/ppermute | solution.py:512
  1.2 0.0 copy-start.9
  1.2 0.1 collective-permute-start.2
  1.3 0.0 copy-start.2
  1.3 0.0 copy-start.4
  1.3 0.7 %copy-done.3 = s32[2,256,16,4]{1,3,2,0:T(4,128)S(1)} copy-done((s32[2,256,16,4]{1,3,2,0:T(4,128)S(1)}, s32[2,256,16,4]{1,3,2,0:T(4,128)}, u32[]{:S(2)}) %copy-start.3) | copy-done | bytes 131096
  2.1 0.0 copy-done.6
  2.1 0.0 copy-start.10
  2.1 2.6 %collective-permute-start = (s32[72,128]{1,0:T(8,128)S(1)}, s32[72,128]{1,0:T(8,128)S(1)}, u32[]{:S(2)}, u32[]{:S(2)}) collective-permute-start(s32[72,128]{1,0:T(8,128)S(1)} %get-tuple-element.41), channel_id=1, source_target_pairs={{0,2},{2,0},{1,3},{3,1},{4,6},{6,4},{5,7},{7,5},{8,10},{10,8},{9,1... | collective-permute-start | bytes 110600 | tf_op jit(solution)/shard_map/ppermute | solution.py:512
  4.7 3.6 %collective-permute-start.5 = (bf16[12,32,128]{2,1,0:T(8,128)(2,1)S(1)}, bf16[12,32,128]{2,1,0:T(8,128)(2,1)S(1)}, u32[]{:S(2)}, u32[]{:S(2)}) collective-permute-start(bf16[12,32,128]{2,1,0:T(8,128)(2,1)S(1)} %get-tuple-element.43), channel_id=1, source_target_pairs={{0,12},{4,8},{8,4},{12,0},{1,13},{5,9},{9,5},{13,1},{2,14},{6,10},... | collective-permute-start | bytes 294920 | tf_op jit(solution)/shard_map/ppermute | solution.py:512
  8.3 0.0 collective-permute-start.4
  8.3 0.0 collective-permute-done.refs_0_
  8.3 0.8 %collective-permute-start.3 = (bf16[12,32,128]{2,1,0:T(8,128)(2,1)S(1)}, bf16[12,32,128]{2,1,0:T(8,128)(2,1)S(1)}, u32[]{:S(2)}, u32[]{:S(2)}) collective-permute-start(bf16[12,32,128]{2,1,0:T(8,128)(2,1)S(1)} %get-tuple-element.43), channel_id=1, source_target_pairs={{0,4},{4,0},{8,12},{12,8},{1,5},{5,1},{9,13},{13,9},{2,6},{6,2},{1... | collective-permute-start | bytes 294920 | tf_op jit(solution)/shard_map/ppermute | solution.py:512
  9.1 0.0 collective-permute-done.1.refs_2_.slab_other
  9.1 0.0 collective-permute-done.2.refs_4_.refs_15_
  9.1 0.0 copy-done
  9.2 5.2 %shard_map.149 = (bf16[6,32,128]{2,1,0:T(8,128)(2,1)S(1)}, bf16[2,32,128]{2,1,0:T(8,128)(2,1)S(1)}, f32[136,128]{1,0:T(8,128)S(1)}) custom-call(s32[2,4]{1,0:T(2,128)S(1)} %copy-done.2, f32[136,128]{1,0:T(8,128)S(1)} %get-tuple-element.56.note_ref.refs_0_.refs_4_, s32[72,128]{1,0:T(8,128)S(1)} %collective-permute-done.refs_0_, ...), custom_call_target="tpu_custom_call" | custom-call | flops 1000000000 | bytes 1000000 | tf_op jit(solution)/shard_map/pallas_call | solution.py:597
  14.3 0.1 collective-permute-start.6
  14.4 0.0 collective-permute-done.5.refs_2_.refs_23_
  14.4 2.5 %collective-permute-done.4.refs_1_.refs_22_ = bf16[12,32,128]{2,1,0:T(8,128)(2,1)S(1)} collective-permute-done((bf16[12,32,128]{2,1,0:T(8,128)(2,1)S(1)}, bf16[12,32,128]{2,1,0:T(8,128)(2,1)S(1)}, u32[]{:S(2)}, u32[]{:S(2)}) %collective-permute-start.4) | collective-permute-done | bytes 98336 | tf_op jit(solution)/shard_map/ppermute | solution.py:512
  17.0 0.0 collective-permute-done.3.refs_0_.refs_21_
  17.0 0.4 shard_map.150
  17.3 0.0 collective-permute-done.6.refs_1_
  17.3 0.1 collective-permute-start.10
  17.5 2.5 %collective-permute-start.9 = (bf16[6,32,128]{2,1,0:T(8,128)(2,1)S(1)}, bf16[6,32,128]{2,1,0:T(8,128)(2,1)S(1)}, u32[]{:S(2)}, u32[]{:S(2)}) collective-permute-start(bf16[6,32,128]{2,1,0:T(8,128)(2,1)S(1)} %shard_map.151.refs_6_.refs_17_), channel_id=1, source_target_pairs={{0,12},{4,8},{8,4},{12,0},{1,13},{5,9},{9,5},{13,1},{2,14},{6,10},... | collective-permute-start | bytes 147464 | tf_op jit(solution)/shard_map/ppermute | solution.py:512
  20.0 0.0 collective-permute-start.8
  20.0 1.9 %collective-permute-start.7 = (bf16[6,32,128]{2,1,0:T(8,128)(2,1)S(1)}, bf16[6,32,128]{2,1,0:T(8,128)(2,1)S(1)}, u32[]{:S(2)}, u32[]{:S(2)}) collective-permute-start(bf16[6,32,128]{2,1,0:T(8,128)(2,1)S(1)} %shard_map.151.refs_6_.refs_17_), channel_id=1, source_target_pairs={{0,4},{4,0},{8,12},{12,8},{1,5},{5,1},{9,13},{13,9},{2,6},{6,2},{1... | collective-permute-start | bytes 147464 | tf_op jit(solution)/shard_map/ppermute | solution.py:512
  21.9 2.4 %shard_map.152 = (bf16[512,2048]{1,0:T(8,128)(2,1)S(1)}, bf16[512,2048]{1,0:T(8,128)(2,1)S(1)}, f32[64,2048]{1,0:T(8,128)S(1)}, f32[64,2048]{1,0:T(8,128)S(1)}) custom-call(s32[2,4]{1,0:T(2,128)S(1)} %copy-done.2, bf16[16,32,128]{2,1,0:T(8,128)(2,1)S(1)} %copy-done.4, bf16[16,32,128]{2,1,0:T(8,128)(2,1)S(1)} %collective-permute-done.1.refs_2_.slab_other, ...), custom_call_target="tpu_custom_call" | custom-call | flops 1000000000 | bytes 1000000 | tf_op jit(solution)/shard_map/pallas_call | solution.py:629
  24.3 0.0 collective-permute-done.9.refs_9_.refs_20_
  24.3 1.3 %collective-permute-done.8.refs_8_.refs_19_ = bf16[6,32,128]{2,1,0:T(8,128)(2,1)S(1)} collective-permute-done((bf16[6,32,128]{2,1,0:T(8,128)(2,1)S(1)}, bf16[6,32,128]{2,1,0:T(8,128)(2,1)S(1)}, u32[]{:S(2)}, u32[]{:S(2)}) %collective-permute-start.8) | collective-permute-done | bytes 49184 | tf_op jit(solution)/shard_map/ppermute | solution.py:512
  25.6 0.0 collective-permute-done.7.refs_7_.refs_18_
  25.6 0.0 collective-permute-done.10.refs_13_
  25.6 3.0 %shard_map.153 = (bf16[4,32,128]{2,1,0:T(8,128)(2,1)S(1)}, bf16[4,32,128]{2,1,0:T(8,128)(2,1)S(1)}, bf16[2,32,128]{2,1,0:T(8,128)(2,1)S(1)}, f32[2,32,128]{2,1,0:T(8,128)S(1)}, f32[2,32,128]{2,1,0:T(8,128)S(1)}) custom-call(s32[2,4]{1,0:T(2,128)S(1)} %copy-done.2, bf16[512,2048]{1,0:T(8,128)(2,1)S(1)} %get-tuple-element.58.refs_0_, ...), custom_call_target="tpu_custom_call" | custom-call | flops 1000000000 | bytes 1000000 | tf_op jit(solution)/shard_map/pallas_call | solution.py:638
  28.6 0.0 copy-start.8
  28.6 0.1 collective-permute-start.11
  28.7 1.2 %collective-permute-done.11.refs_1_ = bf16[4,32,128]{2,1,0:T(8,128)(2,1)S(1)} collective-permute-done((bf16[4,32,128]{2,1,0:T(8,128)(2,1)S(1)}, bf16[4,32,128]{2,1,0:T(8,128)(2,1)S(1)}, u32[]{:S(2)}, u32[]{:S(2)}) %collective-permute-start.11) | collective-permute-done | bytes 32800 | tf_op jit(solution)/shard_map/ppermute | solution.py:512
  29.9 2.5 %collective-permute-start.14 = (bf16[4,32,128]{2,1,0:T(8,128)(2,1)S(1)}, bf16[4,32,128]{2,1,0:T(8,128)(2,1)S(1)}, u32[]{:S(2)}, u32[]{:S(2)}) collective-permute-start(bf16[4,32,128]{2,1,0:T(8,128)(2,1)S(1)} %shard_map.154.refs_13_), channel_id=1, source_target_pairs={{0,12},{4,8},{8,4},{12,0},{1,13},{5,9},{9,5},{13,1},{2,14},{6,10},... | collective-permute-start | bytes 98312 | tf_op jit(solution)/shard_map/ppermute | solution.py:512
  32.4 0.0 collective-permute-start.13
  32.4 1.9 %collective-permute-start.12 = (bf16[4,32,128]{2,1,0:T(8,128)(2,1)S(1)}, bf16[4,32,128]{2,1,0:T(8,128)(2,1)S(1)}, u32[]{:S(2)}, u32[]{:S(2)}) collective-permute-start(bf16[4,32,128]{2,1,0:T(8,128)(2,1)S(1)} %shard_map.154.refs_13_), channel_id=1, source_target_pairs={{0,4},{4,0},{8,12},{12,8},{1,5},{5,1},{9,13},{13,9},{2,6},{6,2},{1... | collective-permute-start | bytes 98312 | tf_op jit(solution)/shard_map/ppermute | solution.py:512
  34.4 0.3 shard_map.155.refs_8_
  34.6 1.0 %collective-permute-done.14.refs_16_ = bf16[4,32,128]{2,1,0:T(8,128)(2,1)S(1)} collective-permute-done((bf16[4,32,128]{2,1,0:T(8,128)(2,1)S(1)}, bf16[4,32,128]{2,1,0:T(8,128)(2,1)S(1)}, u32[]{:S(2)}, u32[]{:S(2)}) %collective-permute-start.14) | collective-permute-done | bytes 32800 | tf_op jit(solution)/shard_map/ppermute | solution.py:512
  35.7 1.6 %collective-permute-done.13.refs_15_ = bf16[4,32,128]{2,1,0:T(8,128)(2,1)S(1)} collective-permute-done((bf16[4,32,128]{2,1,0:T(8,128)(2,1)S(1)}, bf16[4,32,128]{2,1,0:T(8,128)(2,1)S(1)}, u32[]{:S(2)}, u32[]{:S(2)}) %collective-permute-start.13) | collective-permute-done | bytes 32800 | tf_op jit(solution)/shard_map/ppermute | solution.py:512
  37.3 0.0 collective-permute-done.12.refs_14_
  37.3 0.7 %shard_map.156 = (f32[4,32,128]{2,1,0:T(8,128)S(1)}, f32[4,32,128]{2,1,0:T(8,128)S(1)}, bf16[4,32,128]{2,1,0:T(8,128)(2,1)S(1)}, f32[8,512]{1,0:T(8,128)S(1)}) custom-call(f32[6,32,128]{2,1,0:T(8,128)S(1)} %get-tuple-element.47.refs_10_.refs_0_, f32[6,32,128]{2,1,0:T(8,128)S(1)} %get-tuple-element.48.refs_11_.refs_1_, ...), custom_call_target="tpu_custom_call" | custom-call | flops 1000000000 | bytes 1000000 | tf_op jit(solution)/shard_map/pallas_call | solution.py:667
  37.9 0.1 collective-permute-start.15
  38.0 0.7 %shard_map.157 = (f32[4,32,128]{2,1,0:T(8,128)}, f32[4,32,128]{2,1,0:T(8,128)}, bf16[4,32,128]{2,1,0:T(8,128)(2,1)}) custom-call(f32[4,32,128]{2,1,0:T(8,128)S(1)} %get-tuple-element.69.refs_0_, f32[4,32,128]{2,1,0:T(8,128)S(1)} %get-tuple-element.70.refs_1_, bf16[4,32,128]{2,1,0:T(8,128)(2,1)S(1)} %get-tuple-element.71.refs_2_), custom_call_target="tpu_custom_call" | custom-call | flops 1000000000 | bytes 1000000 | tf_op jit(solution)/shard_map/pallas_call | solution.py:691
  38.7 0.5 %collective-permute-done.15.other_ref = f32[8,512]{1,0:T(8,128)S(1)} collective-permute-done((f32[8,512]{1,0:T(8,128)S(1)}, f32[8,512]{1,0:T(8,128)S(1)}, u32[]{:S(2)}, u32[]{:S(2)}) %collective-permute-start.15) | collective-permute-done | bytes 16416 | tf_op jit(solution)/shard_map/ppermute | solution.py:512
  39.2 0.8 %shard_map.158 = f32[1,8]{1,0:T(1,128)} custom-call(f32[8,512]{1,0:T(8,128)S(1)} %get-tuple-element.75.own_ref, f32[8,512]{1,0:T(8,128)S(1)} %collective-permute-done.15.other_ref, bf16[512,256]{1,0:T(8,128)(2,1)S(1)} %copy-done.1, bf16[1,256]{1,0:T(2,128)(2,1)S(1)} %reshape.15.refs_6_.refs_17_.head_ref), custom_call_target="tpu_custom_call" | custom-call | flops 1000000000 | bytes 1000000 | tf_op jit(solution)/shard_map/pallas_call | solution.py:694
  (21 shorter events, 0.1 us)
Async XLA Ops:
  0.6 8.5 %collective-permute-start.1 = (bf16[16,32,128]{2,1,0:T(8,128)(2,1)}, bf16[16,32,128]{2,1,0:T(8,128)(2,1)S(1)}, u32[]{:S(2)}, u32[]{:S(2)}) collective-permute-start(bf16[16,32,128]{2,1,0:T(8,128)(2,1)} %slab_own.3), channel_id=1, source_target_pairs={{0,1},{1,0},{2,3},{3,2},{4,5},{5,4},{6,7},{7,6},{8,9},{9,8},{10,11... | collective-permute-start | bytes 393224 | tf_op jit(solution)/shard_map/ppermute | solution.py:512
  1.2 0.9 %copy-start.3 = (s32[2,256,16,4]{1,3,2,0:T(4,128)S(1)}, s32[2,256,16,4]{1,3,2,0:T(4,128)}, u32[]{:S(2)}) copy-start(s32[2,256,16,4]{1,3,2,0:T(4,128)} %param.20) | copy-start | bytes 393220
  1.2 0.9 %copy-start.5 = (f32[4,32,128]{2,1,0:T(8,128)S(1)}, f32[4,32,128]{2,1,0:T(8,128)}, u32[]{:S(2)}) copy-start(f32[4,32,128]{2,1,0:T(8,128)} %refs_10_.1) | copy-start | bytes 196612
  1.2 0.9 %copy-start.6 = (f32[4,32,128]{2,1,0:T(8,128)S(1)}, f32[4,32,128]{2,1,0:T(8,128)}, u32[]{:S(2)}) copy-start(f32[4,32,128]{2,1,0:T(8,128)} %refs_11_.1) | copy-start | bytes 196612
  1.2 0.9 %copy-start.7 = (bf16[1,4,32,128]{3,2,1,0:T(8,128)(2,1)S(1)}, bf16[1,4,32,128]{3,2,1,0:T(8,128)(2,1)}, u32[]{:S(2)}) copy-start(bf16[1,4,32,128]{3,2,1,0:T(8,128)(2,1)} %param.15) | copy-start | bytes 98308
  1.2 0.9 %copy-start.9 = (f32[2,256]{1,0:T(2,128)S(1)}, f32[2,256]{1,0:T(2,128)}, u32[]{:S(2)}) copy-start(f32[2,256]{1,0:T(2,128)} %labels_ref.1) | copy-start | bytes 6148
  1.2 7.9 %collective-permute-start.2 = (bf16[512,512]{1,0:T(8,128)(2,1)}, bf16[512,512]{1,0:T(8,128)(2,1)S(1)}, u32[]{:S(2)}, u32[]{:S(2)}) collective-permute-start(bf16[512,512]{1,0:T(8,128)(2,1)} %bitcast.7), channel_id=1, source_target_pairs={{0,1},{1,0},{2,3},{3,2},{4,5},{5,4},{6,7},{7,6},{8,9},{9,8},{10,11... | collective-permute-start | bytes 1572872 | tf_op jit(solution)/shard_map/ppermute | solution.py:512
  1.3 7.8 %copy-start.11 = (bf16[256]{0:T(256)(128)(2,1)S(1)}, bf16[256]{0:T(256)(128)(2,1)}, u32[]{:S(2)}) copy-start(bf16[256]{0:T(256)(128)(2,1)} %param.18) | copy-start | bytes 1540
  1.3 7.8 %copy-start = (bf16[16,32,512]{2,1,0:T(8,128)(2,1)S(1)}, bf16[16,32,512]{2,1,0:T(8,128)(2,1)}, u32[]{:S(2)}) copy-start(bf16[16,32,512]{2,1,0:T(8,128)(2,1)} %param.16) | copy-start | bytes 1572868
  1.3 7.8 %copy-start.1 = (bf16[512,256]{1,0:T(8,128)(2,1)S(1)}, bf16[512,256]{1,0:T(8,128)(2,1)}, u32[]{:S(2)}) copy-start(bf16[512,256]{1,0:T(8,128)(2,1)} %w2_ref.1) | copy-start | bytes 786436
  1.3 7.8 %copy-start.2 = (s32[2,4]{1,0:T(2,128)S(1)}, s32[2,4]{1,0:T(2,128)}, u32[]{:S(2)}) copy-start(s32[2,4]{1,0:T(2,128)} %blocks_ref.7) | copy-start | bytes 100
  1.3 7.8 %copy-start.4 = (bf16[16,32,128]{2,1,0:T(8,128)(2,1)S(1)}, bf16[16,32,128]{2,1,0:T(8,128)(2,1)}, u32[]{:S(2)}) copy-start(bf16[16,32,128]{2,1,0:T(8,128)(2,1)} %slab_own.3) | copy-start | bytes 393220
  2.1 14.8 %copy-start.10 = (s32[1,4]{1,0:T(1,128)S(1)}, s32[1,4]{1,0:T(1,128)}, u32[]{:S(2)}) copy-start(s32[1,4]{1,0:T(1,128)} %layout_ref.1) | copy-start | bytes 52
  2.1 6.2 %collective-permute-start = (s32[72,128]{1,0:T(8,128)S(1)}, s32[72,128]{1,0:T(8,128)S(1)}, u32[]{:S(2)}, u32[]{:S(2)}) collective-permute-start(s32[72,128]{1,0:T(8,128)S(1)} %get-tuple-element.41), channel_id=1, source_target_pairs={{0,2},{2,0},{1,3},{3,1},{4,6},{6,4},{5,7},{7,5},{8,10},{10,8},{9,1... | collective-permute-start | bytes 110600 | tf_op jit(solution)/shard_map/ppermute | solution.py:512
  4.7 9.7 %collective-permute-start.5 = (bf16[12,32,128]{2,1,0:T(8,128)(2,1)S(1)}, bf16[12,32,128]{2,1,0:T(8,128)(2,1)S(1)}, u32[]{:S(2)}, u32[]{:S(2)}) collective-permute-start(bf16[12,32,128]{2,1,0:T(8,128)(2,1)S(1)} %get-tuple-element.43), channel_id=1, source_target_pairs={{0,12},{4,8},{8,4},{12,0},{1,13},{5,9},{9,5},{13,1},{2,14},{6,10},... | collective-permute-start | bytes 294920 | tf_op jit(solution)/shard_map/ppermute | solution.py:512
  8.3 8.6 %collective-permute-start.4 = (bf16[12,32,128]{2,1,0:T(8,128)(2,1)S(1)}, bf16[12,32,128]{2,1,0:T(8,128)(2,1)S(1)}, u32[]{:S(2)}, u32[]{:S(2)}) collective-permute-start(bf16[12,32,128]{2,1,0:T(8,128)(2,1)S(1)} %get-tuple-element.43), channel_id=1, source_target_pairs={{0,8},{4,12},{8,0},{12,4},{1,9},{5,13},{9,1},{13,5},{2,10},{6,14},... | collective-permute-start | bytes 294920 | tf_op jit(solution)/shard_map/ppermute | solution.py:512
  8.3 8.6 %collective-permute-start.3 = (bf16[12,32,128]{2,1,0:T(8,128)(2,1)S(1)}, bf16[12,32,128]{2,1,0:T(8,128)(2,1)S(1)}, u32[]{:S(2)}, u32[]{:S(2)}) collective-permute-start(bf16[12,32,128]{2,1,0:T(8,128)(2,1)S(1)} %get-tuple-element.43), channel_id=1, source_target_pairs={{0,4},{4,0},{8,12},{12,8},{1,5},{5,1},{9,13},{13,9},{2,6},{6,2},{1... | collective-permute-start | bytes 294920 | tf_op jit(solution)/shard_map/ppermute | solution.py:512
  14.3 3.0 %collective-permute-start.6 = (bf16[6,32,128]{2,1,0:T(8,128)(2,1)S(1)}, bf16[6,32,128]{2,1,0:T(8,128)(2,1)S(1)}, u32[]{:S(2)}, u32[]{:S(2)}) collective-permute-start(bf16[6,32,128]{2,1,0:T(8,128)(2,1)S(1)} %get-tuple-element.42.refs_0_), channel_id=1, source_target_pairs={{0,1},{1,0},{2,3},{3,2},{4,5},{5,4},{6,7},{7,6},{8,9},{9,8},{10,11... | collective-permute-start | bytes 147464 | tf_op jit(solution)/shard_map/ppermute | solution.py:512
  17.3 8.2 %collective-permute-start.10 = (f32[6,32,128]{2,1,0:T(8,128)S(1)}, f32[6,32,128]{2,1,0:T(8,128)S(1)}, u32[]{:S(2)}, u32[]{:S(2)}) collective-permute-start(f32[6,32,128]{2,1,0:T(8,128)S(1)} %get-tuple-element.62), channel_id=1, source_target_pairs={{0,1},{1,0},{2,3},{3,2},{4,5},{5,4},{6,7},{7,6},{8,9},{9,8},{10,11... | collective-permute-start | bytes 294920 | tf_op jit(solution)/shard_map/ppermute | solution.py:512
  17.5 6.8 %collective-permute-start.9 = (bf16[6,32,128]{2,1,0:T(8,128)(2,1)S(1)}, bf16[6,32,128]{2,1,0:T(8,128)(2,1)S(1)}, u32[]{:S(2)}, u32[]{:S(2)}) collective-permute-start(bf16[6,32,128]{2,1,0:T(8,128)(2,1)S(1)} %shard_map.151.refs_6_.refs_17_), channel_id=1, source_target_pairs={{0,12},{4,8},{8,4},{12,0},{1,13},{5,9},{9,5},{13,1},{2,14},{6,10},... | collective-permute-start | bytes 147464 | tf_op jit(solution)/shard_map/ppermute | solution.py:512
  20.0 5.6 %collective-permute-start.8 = (bf16[6,32,128]{2,1,0:T(8,128)(2,1)S(1)}, bf16[6,32,128]{2,1,0:T(8,128)(2,1)S(1)}, u32[]{:S(2)}, u32[]{:S(2)}) collective-permute-start(bf16[6,32,128]{2,1,0:T(8,128)(2,1)S(1)} %shard_map.151.refs_6_.refs_17_), channel_id=1, source_target_pairs={{0,8},{4,12},{8,0},{12,4},{1,9},{5,13},{9,1},{13,5},{2,10},{6,14},... | collective-permute-start | bytes 147464 | tf_op jit(solution)/shard_map/ppermute | solution.py:512
  20.0 5.6 %collective-permute-start.7 = (bf16[6,32,128]{2,1,0:T(8,128)(2,1)S(1)}, bf16[6,32,128]{2,1,0:T(8,128)(2,1)S(1)}, u32[]{:S(2)}, u32[]{:S(2)}) collective-permute-start(bf16[6,32,128]{2,1,0:T(8,128)(2,1)S(1)} %shard_map.151.refs_6_.refs_17_), channel_id=1, source_target_pairs={{0,4},{4,0},{8,12},{12,8},{1,5},{5,1},{9,13},{13,9},{2,6},{6,2},{1... | collective-permute-start | bytes 147464 | tf_op jit(solution)/shard_map/ppermute | solution.py:512
  28.6 5.8 %copy-start.8 = (s32[1,8,16,4]{2,3,1,0:T(4,128)S(1)}, s32[1,8,16,4]{2,3,1,0:T(4,128)}, u32[]{:S(2)}) copy-start(s32[1,8,16,4]{2,3,1,0:T(4,128)} %param.23) | copy-start | bytes 6148
  28.6 1.3 %collective-permute-start.11 = (bf16[4,32,128]{2,1,0:T(8,128)(2,1)S(1)}, bf16[4,32,128]{2,1,0:T(8,128)(2,1)S(1)}, u32[]{:S(2)}, u32[]{:S(2)}) collective-permute-start(bf16[4,32,128]{2,1,0:T(8,128)(2,1)S(1)} %get-tuple-element.67), channel_id=1, source_target_pairs={{0,1},{1,0},{2,3},{3,2},{4,5},{5,4},{6,7},{7,6},{8,9},{9,8},{10,11... | collective-permute-start | bytes 98312 | tf_op jit(solution)/shard_map/ppermute | solution.py:512
  29.9 5.8 %collective-permute-start.14 = (bf16[4,32,128]{2,1,0:T(8,128)(2,1)S(1)}, bf16[4,32,128]{2,1,0:T(8,128)(2,1)S(1)}, u32[]{:S(2)}, u32[]{:S(2)}) collective-permute-start(bf16[4,32,128]{2,1,0:T(8,128)(2,1)S(1)} %shard_map.154.refs_13_), channel_id=1, source_target_pairs={{0,12},{4,8},{8,4},{12,0},{1,13},{5,9},{9,5},{13,1},{2,14},{6,10},... | collective-permute-start | bytes 98312 | tf_op jit(solution)/shard_map/ppermute | solution.py:512
  32.4 4.8 %collective-permute-start.13 = (bf16[4,32,128]{2,1,0:T(8,128)(2,1)S(1)}, bf16[4,32,128]{2,1,0:T(8,128)(2,1)S(1)}, u32[]{:S(2)}, u32[]{:S(2)}) collective-permute-start(bf16[4,32,128]{2,1,0:T(8,128)(2,1)S(1)} %shard_map.154.refs_13_), channel_id=1, source_target_pairs={{0,8},{4,12},{8,0},{12,4},{1,9},{5,13},{9,1},{13,5},{2,10},{6,14},... | collective-permute-start | bytes 98312 | tf_op jit(solution)/shard_map/ppermute | solution.py:512
  32.4 4.8 %collective-permute-start.12 = (bf16[4,32,128]{2,1,0:T(8,128)(2,1)S(1)}, bf16[4,32,128]{2,1,0:T(8,128)(2,1)S(1)}, u32[]{:S(2)}, u32[]{:S(2)}) collective-permute-start(bf16[4,32,128]{2,1,0:T(8,128)(2,1)S(1)} %shard_map.154.refs_13_), channel_id=1, source_target_pairs={{0,4},{4,0},{8,12},{12,8},{1,5},{5,1},{9,13},{13,9},{2,6},{6,2},{1... | collective-permute-start | bytes 98312 | tf_op jit(solution)/shard_map/ppermute | solution.py:512
  37.9 1.2 %collective-permute-start.15 = (f32[8,512]{1,0:T(8,128)S(1)}, f32[8,512]{1,0:T(8,128)S(1)}, u32[]{:S(2)}, u32[]{:S(2)}) collective-permute-start(f32[8,512]{1,0:T(8,128)S(1)} %get-tuple-element.75.own_ref), channel_id=1, source_target_pairs={{0,1},{1,0},{2,3},{3,2},{4,5},{5,4},{6,7},{7,6},{8,9},{9,8},{10,11... | collective-permute-start | bytes 49160 | tf_op jit(solution)/shard_map/ppermute | solution.py:512

commit v5 on v4

--- a/solution.py
+++ b/solution.py
@@ -331,9 +331,24 @@
     return linear, square, weight
 
 
+def shared_kernel(owners, blocks_ref, linear_ref, square_ref, slab_own, *refs):
+    packs = refs[:-4]
+    linear_out, square_out, weight_out, cross_out = refs[-4:]
+    active = blocks_ref.shape[1]
+    half, rows = linear_ref.shape[1:]
+    kept = linear_out.shape[0]
+    me = lax.axis_index("dp")
+    for i in range(kept):
+        at = active - kept + i
+        block = jnp.broadcast_to(blocks_ref[0:1, at : at + 1], (half, rows))
+        old = old_state(block, me, owners, linear_ref, square_ref, slab_own, packs)
+        linear_out[i], square_out[i], weight_out[i] = old
+        cross_out[i], cross_out[kept + i], cross_out[2 * kept + i] = old
+
+
 def state_kernel(owners, blocks_ref, layout_ref, linear_ref, square_ref, slab_own, *refs):
-    packs = refs[:-6]
-    linear_out, square_out, weight_out, where_out, mine_out, cross_out = refs[-6:]
+    packs = refs[:-5]
+    linear_out, square_out, weight_out, where_out, mine_out = refs[-5:]
     active = blocks_ref.shape[1]
     owned, half, rows = linear_ref.shape
     fresh = active // 2
@@ -342,11 +357,10 @@
     for i in range(active + fresh):
         step, at = (1, i) if i < active else (0, i - active)
         block = jnp.broadcast_to(blocks_ref[step : step + 1, at : at + 1], (8, rows))
-        wide = jnp.broadcast_to(block[0:1], (half, rows))
-        old = old_state(wide, me, owners, linear_ref, square_ref, slab_own, packs)
-        linear_out[i], square_out[i], weight_out[i] = old
-        if i < kept:
-            cross_out[i], cross_out[kept + i], cross_out[2 * kept + i] = old
+        if i >= kept:
+            wide = jnp.broadcast_to(block[0:1], (half, rows))
+            old = old_state(wide, me, owners, linear_ref, square_ref, slab_own, packs)
+            linear_out[i - kept], square_out[i - kept], weight_out[i - kept] = old
         owner = block // owned
         place = block % owned
         turn = (owner + place) % owners
@@ -437,7 +451,7 @@
         if i < kept:
             old = linear_mid[i], square_mid[i], new_ref[i].astype(f32)
         else:
-            old = linear_old[i], square_old[i], weight_old[i]
+            old = linear_old[i - kept], square_old[i - kept], weight_old[i - kept]
         linear, square, weight = ftrl_update(old[0], old[1], gradient, old[2])
         linears.append(linear)
         squares.append(square)
@@ -469,11 +483,13 @@
     units = w1_own.shape[1]
     slots = w1_own.shape[0] // half
     requests = counts_ref.shape[1] // slots
-    stacked = jnp.concatenate([pooled] * slots, axis=0)
-    wanted = lax.broadcasted_iota(jnp.int32, stacked.shape, 0) // half
-    present = lax.broadcasted_iota(jnp.int32, stacked.shape, 1) % slots
-    stacked = jnp.where(wanted == present, stacked, 0.0)
-    product = jnp.dot(stacked.T.astype(bf16), w1_own[...], preferred_element_type=f32)
+    copies_high = 128 // half
+    turned = jnp.concatenate([pooled] * copies_high, axis=0).T
+    spread = jnp.concatenate([turned] * (slots // copies_high), axis=1)
+    wanted = lax.broadcasted_iota(jnp.int32, spread.shape, 1) // half
+    present = lax.broadcasted_iota(jnp.int32, spread.shape, 0) % slots
+    spread = jnp.where(wanted == present, spread, 0.0).astype(bf16)
+    product = jnp.dot(spread, w1_own[...], preferred_element_type=f32)
     partial_out[...] = jnp.sum(product.reshape(requests, slots, units), axis=1)
 
 
@@ -613,14 +629,12 @@
     notes = [note, note_other][:groups]
     share_turned = swap(share, ("mp",), sizes, (1,))
     late = lax.optimization_barrier((share, *packs))[1:]
-    old_shape = struct(touched, half, rows, dtype=f32)
-    index_shape = struct(touched, 8, rows, dtype=jnp.int32)
-    linear_old, square_old, weight_old, where, mine, cross = kernel_call(
-        functools.partial(state_kernel, owners),
-        (old_shape, old_shape, old_shape, index_shape, index_shape)
-        + (struct(3 * kept, half, rows, dtype=f32),),
-        [VMEM] * (5 + len(packs)),
-    )(step_blocks, serve_layout, linear_state, square_state, hot_slab, *late)
+    shared_shape = struct(kept, half, rows, dtype=f32)
+    linear_old, square_old, weight_old, cross = kernel_call(
+        functools.partial(shared_kernel, owners),
+        (shared_shape, shared_shape, shared_shape, struct(3 * kept, half, rows, dtype=f32)),
+        [VMEM] * (4 + len(packs)),
+    )(step_blocks, linear_state, square_state, hot_slab, *late)
     cross, share_turned = lax.optimization_barrier((cross, share_turned))
     total = join([share, share_turned, rest_own], True)
     sums = early = reduce_rest(total, sizes, groups)
@@ -659,6 +673,14 @@
     wanted = kernel_call(
         functools.partial(wanted_kernel, rows), struct(positions * rows, requests * slots), [VMEM]
     )(late)
+    late = lax.optimization_barrier((total, *packs))[1:]
+    old_shape = struct(touched - kept, half, rows, dtype=f32)
+    index_shape = struct(touched, 8, rows, dtype=jnp.int32)
+    linear_old, square_old, weight_old, where, mine = kernel_call(
+        functools.partial(state_kernel, owners),
+        (old_shape, old_shape, old_shape, index_shape, index_shape),
+        [VMEM] * (5 + len(packs)),
+    )(step_blocks, serve_layout, linear_state, square_state, hot_slab, *late)
     results = (
         struct(*linear_state.shape, dtype=f32),
         struct(*square_state.shape, dtype=f32),

time: 40.1 us -> 40 us (level)
  transfers between devices with their start and end apart: 16 -> 16, of which waited for: 6 -> 6; matrix products, arithmetic and copies ran while one was open for 0% -> 0% of each run, Pallas kernels for 22% -> 23%
where the time goes in v5:
time: 40 us; the launch traced here: 39.8 us
  starting transfers between devices  16.8 us (42%)
  Pallas kernels  13.6 us (34%)
  waiting for transfers between devices  7.76 us (19%)
  between operations  0.85 us (2%)
  local copies, waits for them, and re-layouts  0.81 us (2%)
    ppermute x16, starting transfers between devices, swap(): return lax.ppermute(value, axes, pairs)  16.8 us
    ppermute x16, waiting for transfers between devices, swap(): return lax.ppermute(value, axes, pairs)  7.76 us
    pallas_call x1, Pallas kernels, local(): kernel_call(functools.partial(first_step_kernel, slots, picks, groups), (...  5.15 us
    pallas_call x1, Pallas kernels, local(): kernel_call(functools.partial(second_step_kernel, slots, picks, groups, s...  3.04 us
    pallas_call x1, Pallas kernels, local(): kernel_call(functools.partial(side_kernel, slots, picks, groups), (counts...  2.36 us
    unnamed x24, local copies, waits for them, and re-layouts  0.8 us
  transfers between devices with their start and end apart: 16, of which 6 were waited for; matrix products, arithmetic and copies ran while one was open for 0% of the time, Pallas kernels for 23%

profile of v5, /device:TPU:0, one launch (start us, length us, event | category | flops | bytes accessed | tf_op | source)
XLA Modules:
  0.0 39.8 jit_solution(3812246741703058702)
XLA Ops:
  0.6 0.5 %collective-permute-start = (bf16[16,32,128]{2,1,0:T(8,128)(2,1)}, bf16[16,32,128]{2,1,0:T(8,128)(2,1)S(1)}, u32[]{:S(2)}, u32[]{:S(2)}) collective-permute-start(bf16[16,32,128]{2,1,0:T(8,128)(2,1)} %slab_own.5), channel_id=1, source_target_pairs={{0,1},{1,0},{2,3},{3,2},{4,5},{5,4},{6,7},{7,6},{8,9},{9,8},{10,11... | collective-permute-start | bytes 393224 | tf_op jit(solution)/shard_map/ppermute | solution.py:528
  1.2 0.1 collective-permute-start.2
  1.3 0.0 copy-start.2
  1.3 0.0 copy-start.4
  1.3 0.7 %copy-done.3 = s32[2,256,16,4]{1,3,2,0:T(4,128)S(1)} copy-done((s32[2,256,16,4]{1,3,2,0:T(4,128)S(1)}, s32[2,256,16,4]{1,3,2,0:T(4,128)}, u32[]{:S(2)}) %copy-start.3) | copy-done | bytes 131096
  2.1 0.0 copy-done.6
  2.1 0.0 copy-done.7
  2.1 2.6 %collective-permute-start.1 = (s32[72,128]{1,0:T(8,128)S(1)}, s32[72,128]{1,0:T(8,128)S(1)}, u32[]{:S(2)}, u32[]{:S(2)}) collective-permute-start(s32[72,128]{1,0:T(8,128)S(1)} %get-tuple-element.47), channel_id=1, source_target_pairs={{0,2},{2,0},{1,3},{3,1},{4,6},{6,4},{5,7},{7,5},{8,10},{10,8},{9,1... | collective-permute-start | bytes 110600 | tf_op jit(solution)/shard_map/ppermute | solution.py:528
  4.7 3.6 %collective-permute-start.5 = (bf16[12,32,128]{2,1,0:T(8,128)(2,1)S(1)}, bf16[12,32,128]{2,1,0:T(8,128)(2,1)S(1)}, u32[]{:S(2)}, u32[]{:S(2)}) collective-permute-start(bf16[12,32,128]{2,1,0:T(8,128)(2,1)S(1)} %get-tuple-element.49), channel_id=1, source_target_pairs={{0,12},{4,8},{8,4},{12,0},{1,13},{5,9},{9,5},{13,1},{2,14},{6,10},... | collective-permute-start | bytes 294920 | tf_op jit(solution)/shard_map/ppermute | solution.py:528
  8.3 0.0 collective-permute-start.4
  8.3 0.0 collective-permute-done.1.refs_0_
  8.3 0.8 %collective-permute-start.3 = (bf16[12,32,128]{2,1,0:T(8,128)(2,1)S(1)}, bf16[12,32,128]{2,1,0:T(8,128)(2,1)S(1)}, u32[]{:S(2)}, u32[]{:S(2)}) collective-permute-start(bf16[12,32,128]{2,1,0:T(8,128)(2,1)S(1)} %get-tuple-element.49), channel_id=1, source_target_pairs={{0,4},{4,0},{8,12},{12,8},{1,5},{5,1},{9,13},{13,9},{2,6},{6,2},{1... | collective-permute-start | bytes 294920 | tf_op jit(solution)/shard_map/ppermute | solution.py:528
  9.1 0.0 collective-permute-done.refs_2_.slab_other
  9.1 0.0 collective-permute-done.2.refs_4_.refs_15_
  9.1 5.1 %shard_map.149 = (bf16[6,32,128]{2,1,0:T(8,128)(2,1)S(1)}, bf16[2,32,128]{2,1,0:T(8,128)(2,1)S(1)}, f32[136,128]{1,0:T(8,128)S(1)}) custom-call(s32[2,4]{1,0:T(2,128)S(1)} %copy-done.2, f32[136,128]{1,0:T(8,128)S(1)} %get-tuple-element.57.note_ref.refs_0_.refs_4_, s32[72,128]{1,0:T(8,128)S(1)} %collective-permute-done.1.refs_0_, ...), custom_call_target="tpu_custom_call" | custom-call | flops 1000000000 | bytes 1000000 | tf_op jit(solution)/shard_map/pallas_call | solution.py:613
  14.3 0.1 collective-permute-start.6
  14.4 0.0 collective-permute-done.5.refs_2_.refs_23_
  14.4 2.6 %collective-permute-done.4.refs_1_.refs_22_ = bf16[12,32,128]{2,1,0:T(8,128)(2,1)S(1)} collective-permute-done((bf16[12,32,128]{2,1,0:T(8,128)(2,1)S(1)}, bf16[12,32,128]{2,1,0:T(8,128)(2,1)S(1)}, u32[]{:S(2)}, u32[]{:S(2)}) %collective-permute-start.4) | collective-permute-done | bytes 98336 | tf_op jit(solution)/shard_map/ppermute | solution.py:528
  16.9 0.0 collective-permute-done.3.refs_0_.refs_21_
  16.9 0.2 shard_map.150
  17.2 0.0 collective-permute-done.6.refs_1_
  17.2 0.1 collective-permute-start.10
  17.3 2.5 %collective-permute-start.9 = (bf16[6,32,128]{2,1,0:T(8,128)(2,1)S(1)}, bf16[6,32,128]{2,1,0:T(8,128)(2,1)S(1)}, u32[]{:S(2)}, u32[]{:S(2)}) collective-permute-start(bf16[6,32,128]{2,1,0:T(8,128)(2,1)S(1)} %shard_map.151.refs_6_.refs_17_), channel_id=1, source_target_pairs={{0,12},{4,8},{8,4},{12,0},{1,13},{5,9},{9,5},{13,1},{2,14},{6,10},... | collective-permute-start | bytes 147464 | tf_op jit(solution)/shard_map/ppermute | solution.py:528
  19.8 0.0 collective-permute-start.8
  19.8 1.9 %collective-permute-start.7 = (bf16[6,32,128]{2,1,0:T(8,128)(2,1)S(1)}, bf16[6,32,128]{2,1,0:T(8,128)(2,1)S(1)}, u32[]{:S(2)}, u32[]{:S(2)}) collective-permute-start(bf16[6,32,128]{2,1,0:T(8,128)(2,1)S(1)} %shard_map.151.refs_6_.refs_17_), channel_id=1, source_target_pairs={{0,4},{4,0},{8,12},{12,8},{1,5},{5,1},{9,13},{13,9},{2,6},{6,2},{1... | collective-permute-start | bytes 147464 | tf_op jit(solution)/shard_map/ppermute | solution.py:528
  21.7 2.4 %shard_map.152 = (bf16[512,2048]{1,0:T(8,128)(2,1)S(1)}, bf16[512,2048]{1,0:T(8,128)(2,1)S(1)}, f32[64,2048]{1,0:T(8,128)S(1)}, f32[64,2048]{1,0:T(8,128)S(1)}) custom-call(s32[2,4]{1,0:T(2,128)S(1)} %copy-done.2, bf16[16,32,128]{2,1,0:T(8,128)(2,1)S(1)} %copy-done.4, bf16[16,32,128]{2,1,0:T(8,128)(2,1)S(1)} %collective-permute-done.refs_2_.slab_other, ...), custom_call_target="tpu_custom_call" | custom-call | flops 1000000000 | bytes 1000000 | tf_op jit(solution)/shard_map/pallas_call | solution.py:643
  24.1 0.0 collective-permute-done.9.refs_9_.refs_20_
  24.1 1.3 %collective-permute-done.8.refs_8_.refs_19_ = bf16[6,32,128]{2,1,0:T(8,128)(2,1)S(1)} collective-permute-done((bf16[6,32,128]{2,1,0:T(8,128)(2,1)S(1)}, bf16[6,32,128]{2,1,0:T(8,128)(2,1)S(1)}, u32[]{:S(2)}, u32[]{:S(2)}) %collective-permute-start.8) | collective-permute-done | bytes 49184 | tf_op jit(solution)/shard_map/ppermute | solution.py:528
  25.4 0.0 collective-permute-done.7.refs_7_.refs_18_
  25.4 0.0 collective-permute-done.10.refs_13_
  25.4 3.0 %shard_map.153 = (bf16[4,32,128]{2,1,0:T(8,128)(2,1)S(1)}, bf16[4,32,128]{2,1,0:T(8,128)(2,1)S(1)}, bf16[2,32,128]{2,1,0:T(8,128)(2,1)S(1)}, f32[2,32,128]{2,1,0:T(8,128)S(1)}, f32[2,32,128]{2,1,0:T(8,128)S(1)}) custom-call(s32[2,4]{1,0:T(2,128)S(1)} %copy-done.2, bf16[512,2048]{1,0:T(8,128)(2,1)S(1)} %get-tuple-element.59.refs_0_, ...), custom_call_target="tpu_custom_call" | custom-call | flops 1000000000 | bytes 1000000 | tf_op jit(solution)/shard_map/pallas_call | solution.py:652
  28.4 0.0 copy-start.8
  28.4 0.1 collective-permute-start.11
  28.5 1.2 %collective-permute-done.11.refs_1_ = bf16[4,32,128]{2,1,0:T(8,128)(2,1)S(1)} collective-permute-done((bf16[4,32,128]{2,1,0:T(8,128)(2,1)S(1)}, bf16[4,32,128]{2,1,0:T(8,128)(2,1)S(1)}, u32[]{:S(2)}, u32[]{:S(2)}) %collective-permute-start.11) | collective-permute-done | bytes 32800 | tf_op jit(solution)/shard_map/ppermute | solution.py:528
  29.7 0.0 copy-start.10
  29.7 2.5 %collective-permute-start.14 = (bf16[4,32,128]{2,1,0:T(8,128)(2,1)S(1)}, bf16[4,32,128]{2,1,0:T(8,128)(2,1)S(1)}, u32[]{:S(2)}, u32[]{:S(2)}) collective-permute-start(bf16[4,32,128]{2,1,0:T(8,128)(2,1)S(1)} %shard_map.154.refs_13_), channel_id=1, source_target_pairs={{0,12},{4,8},{8,4},{12,0},{1,13},{5,9},{9,5},{13,1},{2,14},{6,10},... | collective-permute-start | bytes 98312 | tf_op jit(solution)/shard_map/ppermute | solution.py:528
  32.3 0.0 collective-permute-start.13
  32.3 1.9 %collective-permute-start.12 = (bf16[4,32,128]{2,1,0:T(8,128)(2,1)S(1)}, bf16[4,32,128]{2,1,0:T(8,128)(2,1)S(1)}, u32[]{:S(2)}, u32[]{:S(2)}) collective-permute-start(bf16[4,32,128]{2,1,0:T(8,128)(2,1)S(1)} %shard_map.154.refs_13_), channel_id=1, source_target_pairs={{0,4},{4,0},{8,12},{12,8},{1,5},{5,1},{9,13},{13,9},{2,6},{6,2},{1... | collective-permute-start | bytes 98312 | tf_op jit(solution)/shard_map/ppermute | solution.py:528
  34.2 0.3 shard_map.156.refs_8_
  34.5 0.3 shard_map.155
  34.8 0.7 %collective-permute-done.14.refs_16_ = bf16[4,32,128]{2,1,0:T(8,128)(2,1)S(1)} collective-permute-done((bf16[4,32,128]{2,1,0:T(8,128)(2,1)S(1)}, bf16[4,32,128]{2,1,0:T(8,128)(2,1)S(1)}, u32[]{:S(2)}, u32[]{:S(2)}) %collective-permute-start.14) | collective-permute-done | bytes 32800 | tf_op jit(solution)/shard_map/ppermute | solution.py:528
  35.5 1.6 %collective-permute-done.13.refs_15_ = bf16[4,32,128]{2,1,0:T(8,128)(2,1)S(1)} collective-permute-done((bf16[4,32,128]{2,1,0:T(8,128)(2,1)S(1)}, bf16[4,32,128]{2,1,0:T(8,128)(2,1)S(1)}, u32[]{:S(2)}, u32[]{:S(2)}) %collective-permute-start.13) | collective-permute-done | bytes 32800 | tf_op jit(solution)/shard_map/ppermute | solution.py:528
  37.1 0.0 collective-permute-done.12.refs_14_
  37.1 0.7 %shard_map.157 = (f32[4,32,128]{2,1,0:T(8,128)S(1)}, f32[4,32,128]{2,1,0:T(8,128)S(1)}, bf16[4,32,128]{2,1,0:T(8,128)(2,1)S(1)}, f32[8,512]{1,0:T(8,128)S(1)}) custom-call(f32[4,32,128]{2,1,0:T(8,128)S(1)} %get-tuple-element.72.refs_0_, f32[4,32,128]{2,1,0:T(8,128)S(1)} %get-tuple-element.73.refs_1_, f32[4,32,128]{2,1,0:T(8,128)S(1)} %get-tuple-element.74.refs_2_, ...), custom_call_target="tpu_custom_call" | custom-call | flops 1000000000 | bytes 1000000 | tf_op jit(solution)/shard_map/pallas_call | solution.py:689
  37.8 0.1 collective-permute-start.15
  37.9 0.7 %shard_map.158 = (f32[4,32,128]{2,1,0:T(8,128)}, f32[4,32,128]{2,1,0:T(8,128)}, bf16[4,32,128]{2,1,0:T(8,128)(2,1)}) custom-call(f32[4,32,128]{2,1,0:T(8,128)S(1)} %get-tuple-element.81.refs_0_, f32[4,32,128]{2,1,0:T(8,128)S(1)} %get-tuple-element.82.refs_1_, bf16[4,32,128]{2,1,0:T(8,128)(2,1)S(1)} %get-tuple-element.83.refs_2_), custom_call_target="tpu_custom_call" | custom-call | flops 1000000000 | bytes 1000000 | tf_op jit(solution)/shard_map/pallas_call | solution.py:713
  38.6 0.5 %collective-permute-done.15.other_ref = f32[8,512]{1,0:T(8,128)S(1)} collective-permute-done((f32[8,512]{1,0:T(8,128)S(1)}, f32[8,512]{1,0:T(8,128)S(1)}, u32[]{:S(2)}, u32[]{:S(2)}) %collective-permute-start.15) | collective-permute-done | bytes 16416 | tf_op jit(solution)/shard_map/ppermute | solution.py:528
  39.0 0.8 %shard_map.159 = f32[1,8]{1,0:T(1,128)} custom-call(f32[8,512]{1,0:T(8,128)S(1)} %get-tuple-element.87.own_ref, f32[8,512]{1,0:T(8,128)S(1)} %collective-permute-done.15.other_ref, bf16[512,256]{1,0:T(8,128)(2,1)S(1)} %copy-done.1, bf16[1,256]{1,0:T(2,128)(2,1)S(1)} %reshape.15.refs_6_.refs_17_.head_ref), custom_call_target="tpu_custom_call" | custom-call | flops 1000000000 | bytes 1000000 | tf_op jit(solution)/shard_map/pallas_call | solution.py:716
  (22 shorter events, 0.1 us)
Async XLA Ops:
  0.6 8.5 %collective-permute-start = (bf16[16,32,128]{2,1,0:T(8,128)(2,1)}, bf16[16,32,128]{2,1,0:T(8,128)(2,1)S(1)}, u32[]{:S(2)}, u32[]{:S(2)}) collective-permute-start(bf16[16,32,128]{2,1,0:T(8,128)(2,1)} %slab_own.5), channel_id=1, source_target_pairs={{0,1},{1,0},{2,3},{3,2},{4,5},{5,4},{6,7},{7,6},{8,9},{9,8},{10,11... | collective-permute-start | bytes 393224 | tf_op jit(solution)/shard_map/ppermute | solution.py:528
  1.2 0.9 %copy-start.3 = (s32[2,256,16,4]{1,3,2,0:T(4,128)S(1)}, s32[2,256,16,4]{1,3,2,0:T(4,128)}, u32[]{:S(2)}) copy-start(s32[2,256,16,4]{1,3,2,0:T(4,128)} %param.20) | copy-start | bytes 393220
  1.2 0.9 %copy-start.5 = (f32[4,32,128]{2,1,0:T(8,128)S(1)}, f32[4,32,128]{2,1,0:T(8,128)}, u32[]{:S(2)}) copy-start(f32[4,32,128]{2,1,0:T(8,128)} %refs_10_.1) | copy-start | bytes 196612
  1.2 0.9 %copy-start.6 = (f32[4,32,128]{2,1,0:T(8,128)S(1)}, f32[4,32,128]{2,1,0:T(8,128)}, u32[]{:S(2)}) copy-start(f32[4,32,128]{2,1,0:T(8,128)} %refs_11_.1) | copy-start | bytes 196612
  1.2 0.9 %copy-start.7 = (bf16[1,4,32,128]{3,2,1,0:T(8,128)(2,1)S(1)}, bf16[1,4,32,128]{3,2,1,0:T(8,128)(2,1)}, u32[]{:S(2)}) copy-start(bf16[1,4,32,128]{3,2,1,0:T(8,128)(2,1)} %param.15) | copy-start | bytes 98308
  1.2 0.9 %copy-start.9 = (f32[2,256]{1,0:T(2,128)S(1)}, f32[2,256]{1,0:T(2,128)}, u32[]{:S(2)}) copy-start(f32[2,256]{1,0:T(2,128)} %labels_ref.1) | copy-start | bytes 6148
  1.2 7.9 %collective-permute-start.2 = (bf16[512,512]{1,0:T(8,128)(2,1)}, bf16[512,512]{1,0:T(8,128)(2,1)S(1)}, u32[]{:S(2)}, u32[]{:S(2)}) collective-permute-start(bf16[512,512]{1,0:T(8,128)(2,1)} %bitcast.7), channel_id=1, source_target_pairs={{0,1},{1,0},{2,3},{3,2},{4,5},{5,4},{6,7},{7,6},{8,9},{9,8},{10,11... | collective-permute-start | bytes 1572872 | tf_op jit(solution)/shard_map/ppermute | solution.py:528
  1.3 7.8 %copy-start.11 = (bf16[256]{0:T(256)(128)(2,1)S(1)}, bf16[256]{0:T(256)(128)(2,1)}, u32[]{:S(2)}) copy-start(bf16[256]{0:T(256)(128)(2,1)} %param.18) | copy-start | bytes 1540
  1.3 7.8 %copy-start = (bf16[16,32,512]{2,1,0:T(8,128)(2,1)S(1)}, bf16[16,32,512]{2,1,0:T(8,128)(2,1)}, u32[]{:S(2)}) copy-start(bf16[16,32,512]{2,1,0:T(8,128)(2,1)} %param.16) | copy-start | bytes 1572868
  1.3 7.8 %copy-start.1 = (bf16[512,256]{1,0:T(8,128)(2,1)S(1)}, bf16[512,256]{1,0:T(8,128)(2,1)}, u32[]{:S(2)}) copy-start(bf16[512,256]{1,0:T(8,128)(2,1)} %w2_ref.1) | copy-start | bytes 786436
  1.3 7.8 %copy-start.2 = (s32[2,4]{1,0:T(2,128)S(1)}, s32[2,4]{1,0:T(2,128)}, u32[]{:S(2)}) copy-start(s32[2,4]{1,0:T(2,128)} %blocks_ref.9) | copy-start | bytes 100
  1.3 7.8 %copy-start.4 = (bf16[16,32,128]{2,1,0:T(8,128)(2,1)S(1)}, bf16[16,32,128]{2,1,0:T(8,128)(2,1)}, u32[]{:S(2)}) copy-start(bf16[16,32,128]{2,1,0:T(8,128)(2,1)} %slab_own.5) | copy-start | bytes 393220
  2.1 6.2 %collective-permute-start.1 = (s32[72,128]{1,0:T(8,128)S(1)}, s32[72,128]{1,0:T(8,128)S(1)}, u32[]{:S(2)}, u32[]{:S(2)}) collective-permute-start(s32[72,128]{1,0:T(8,128)S(1)} %get-tuple-element.47), channel_id=1, source_target_pairs={{0,2},{2,0},{1,3},{3,1},{4,6},{6,4},{5,7},{7,5},{8,10},{10,8},{9,1... | collective-permute-start | bytes 110600 | tf_op jit(solution)/shard_map/ppermute | solution.py:528
  4.7 9.7 %collective-permute-start.5 = (bf16[12,32,128]{2,1,0:T(8,128)(2,1)S(1)}, bf16[12,32,128]{2,1,0:T(8,128)(2,1)S(1)}, u32[]{:S(2)}, u32[]{:S(2)}) collective-permute-start(bf16[12,32,128]{2,1,0:T(8,128)(2,1)S(1)} %get-tuple-element.49), channel_id=1, source_target_pairs={{0,12},{4,8},{8,4},{12,0},{1,13},{5,9},{9,5},{13,1},{2,14},{6,10},... | collective-permute-start | bytes 294920 | tf_op jit(solution)/shard_map/ppermute | solution.py:528
  8.3 8.6 %collective-permute-start.4 = (bf16[12,32,128]{2,1,0:T(8,128)(2,1)S(1)}, bf16[12,32,128]{2,1,0:T(8,128)(2,1)S(1)}, u32[]{:S(2)}, u32[]{:S(2)}) collective-permute-start(bf16[12,32,128]{2,1,0:T(8,128)(2,1)S(1)} %get-tuple-element.49), channel_id=1, source_target_pairs={{0,8},{4,12},{8,0},{12,4},{1,9},{5,13},{9,1},{13,5},{2,10},{6,14},... | collective-permute-start | bytes 294920 | tf_op jit(solution)/shard_map/ppermute | solution.py:528
  8.3 8.6 %collective-permute-start.3 = (bf16[12,32,128]{2,1,0:T(8,128)(2,1)S(1)}, bf16[12,32,128]{2,1,0:T(8,128)(2,1)S(1)}, u32[]{:S(2)}, u32[]{:S(2)}) collective-permute-start(bf16[12,32,128]{2,1,0:T(8,128)(2,1)S(1)} %get-tuple-element.49), channel_id=1, source_target_pairs={{0,4},{4,0},{8,12},{12,8},{1,5},{5,1},{9,13},{13,9},{2,6},{6,2},{1... | collective-permute-start | bytes 294920 | tf_op jit(solution)/shard_map/ppermute | solution.py:528
  14.3 2.9 %collective-permute-start.6 = (bf16[6,32,128]{2,1,0:T(8,128)(2,1)S(1)}, bf16[6,32,128]{2,1,0:T(8,128)(2,1)S(1)}, u32[]{:S(2)}, u32[]{:S(2)}) collective-permute-start(bf16[6,32,128]{2,1,0:T(8,128)(2,1)S(1)} %get-tuple-element.48.refs_0_), channel_id=1, source_target_pairs={{0,1},{1,0},{2,3},{3,2},{4,5},{5,4},{6,7},{7,6},{8,9},{9,8},{10,11... | collective-permute-start | bytes 147464 | tf_op jit(solution)/shard_map/ppermute | solution.py:528
  17.2 8.2 %collective-permute-start.10 = (f32[6,32,128]{2,1,0:T(8,128)S(1)}, f32[6,32,128]{2,1,0:T(8,128)S(1)}, u32[]{:S(2)}, u32[]{:S(2)}) collective-permute-start(f32[6,32,128]{2,1,0:T(8,128)S(1)} %get-tuple-element.66), channel_id=1, source_target_pairs={{0,1},{1,0},{2,3},{3,2},{4,5},{5,4},{6,7},{7,6},{8,9},{9,8},{10,11... | collective-permute-start | bytes 294920 | tf_op jit(solution)/shard_map/ppermute | solution.py:528
  17.3 6.8 %collective-permute-start.9 = (bf16[6,32,128]{2,1,0:T(8,128)(2,1)S(1)}, bf16[6,32,128]{2,1,0:T(8,128)(2,1)S(1)}, u32[]{:S(2)}, u32[]{:S(2)}) collective-permute-start(bf16[6,32,128]{2,1,0:T(8,128)(2,1)S(1)} %shard_map.151.refs_6_.refs_17_), channel_id=1, source_target_pairs={{0,12},{4,8},{8,4},{12,0},{1,13},{5,9},{9,5},{13,1},{2,14},{6,10},... | collective-permute-start | bytes 147464 | tf_op jit(solution)/shard_map/ppermute | solution.py:528
  19.8 5.6 %collective-permute-start.8 = (bf16[6,32,128]{2,1,0:T(8,128)(2,1)S(1)}, bf16[6,32,128]{2,1,0:T(8,128)(2,1)S(1)}, u32[]{:S(2)}, u32[]{:S(2)}) collective-permute-start(bf16[6,32,128]{2,1,0:T(8,128)(2,1)S(1)} %shard_map.151.refs_6_.refs_17_), channel_id=1, source_target_pairs={{0,8},{4,12},{8,0},{12,4},{1,9},{5,13},{9,1},{13,5},{2,10},{6,14},... | collective-permute-start | bytes 147464 | tf_op jit(solution)/shard_map/ppermute | solution.py:528
  19.8 5.6 %collective-permute-start.7 = (bf16[6,32,128]{2,1,0:T(8,128)(2,1)S(1)}, bf16[6,32,128]{2,1,0:T(8,128)(2,1)S(1)}, u32[]{:S(2)}, u32[]{:S(2)}) collective-permute-start(bf16[6,32,128]{2,1,0:T(8,128)(2,1)S(1)} %shard_map.151.refs_6_.refs_17_), channel_id=1, source_target_pairs={{0,4},{4,0},{8,12},{12,8},{1,5},{5,1},{9,13},{13,9},{2,6},{6,2},{1... | collective-permute-start | bytes 147464 | tf_op jit(solution)/shard_map/ppermute | solution.py:528
  28.4 5.8 %copy-start.8 = (s32[1,8,16,4]{2,3,1,0:T(4,128)S(1)}, s32[1,8,16,4]{2,3,1,0:T(4,128)}, u32[]{:S(2)}) copy-start(s32[1,8,16,4]{2,3,1,0:T(4,128)} %param.23) | copy-start | bytes 6148
  28.4 1.3 %collective-permute-start.11 = (bf16[4,32,128]{2,1,0:T(8,128)(2,1)S(1)}, bf16[4,32,128]{2,1,0:T(8,128)(2,1)S(1)}, u32[]{:S(2)}, u32[]{:S(2)}) collective-permute-start(bf16[4,32,128]{2,1,0:T(8,128)(2,1)S(1)} %get-tuple-element.68), channel_id=1, source_target_pairs={{0,1},{1,0},{2,3},{3,2},{4,5},{5,4},{6,7},{7,6},{8,9},{9,8},{10,11... | collective-permute-start | bytes 98312 | tf_op jit(solution)/shard_map/ppermute | solution.py:528
  29.7 4.7 %copy-start.10 = (s32[1,4]{1,0:T(1,128)S(1)}, s32[1,4]{1,0:T(1,128)}, u32[]{:S(2)}) copy-start(s32[1,4]{1,0:T(1,128)} %layout_ref.1) | copy-start | bytes 52
  29.7 5.8 %collective-permute-start.14 = (bf16[4,32,128]{2,1,0:T(8,128)(2,1)S(1)}, bf16[4,32,128]{2,1,0:T(8,128)(2,1)S(1)}, u32[]{:S(2)}, u32[]{:S(2)}) collective-permute-start(bf16[4,32,128]{2,1,0:T(8,128)(2,1)S(1)} %shard_map.154.refs_13_), channel_id=1, source_target_pairs={{0,12},{4,8},{8,4},{12,0},{1,13},{5,9},{9,5},{13,1},{2,14},{6,10},... | collective-permute-start | bytes 98312 | tf_op jit(solution)/shard_map/ppermute | solution.py:528
  32.3 4.8 %collective-permute-start.13 = (bf16[4,32,128]{2,1,0:T(8,128)(2,1)S(1)}, bf16[4,32,128]{2,1,0:T(8,128)(2,1)S(1)}, u32[]{:S(2)}, u32[]{:S(2)}) collective-permute-start(bf16[4,32,128]{2,1,0:T(8,128)(2,1)S(1)} %shard_map.154.refs_13_), channel_id=1, source_target_pairs={{0,8},{4,12},{8,0},{12,4},{1,9},{5,13},{9,1},{13,5},{2,10},{6,14},... | collective-permute-start | bytes 98312 | tf_op jit(solution)/shard_map/ppermute | solution.py:528
  32.3 4.8 %collective-permute-start.12 = (bf16[4,32,128]{2,1,0:T(8,128)(2,1)S(1)}, bf16[4,32,128]{2,1,0:T(8,128)(2,1)S(1)}, u32[]{:S(2)}, u32[]{:S(2)}) collective-permute-start(bf16[4,32,128]{2,1,0:T(8,128)(2,1)S(1)} %shard_map.154.refs_13_), channel_id=1, source_target_pairs={{0,4},{4,0},{8,12},{12,8},{1,5},{5,1},{9,13},{13,9},{2,6},{6,2},{1... | collective-permute-start | bytes 98312 | tf_op jit(solution)/shard_map/ppermute | solution.py:528
  37.8 1.2 %collective-permute-start.15 = (f32[8,512]{1,0:T(8,128)S(1)}, f32[8,512]{1,0:T(8,128)S(1)}, u32[]{:S(2)}, u32[]{:S(2)}) collective-permute-start(f32[8,512]{1,0:T(8,128)S(1)} %get-tuple-element.87.own_ref), channel_id=1, source_target_pairs={{0,1},{1,0},{2,3},{3,2},{4,5},{5,4},{6,7},{7,6},{8,9},{9,8},{10,11... | collective-permute-start | bytes 49160 | tf_op jit(solution)/shard_map/ppermute | solution.py:528
